TPU v7x, 32 devices: a whole 2x2x4 slice. The times are simulated.
32 devices in a mesh: seq: 4 (over z), exp: 8 (over y, x, core).
Axes of the slice: x: 2, y: 2, z: 4, core: 2. Of those that a mesh axis runs over, the one named last changes fastest.
Arguments:
- tokens: bfloat16 [16, 512, 2048], P('exp', 'seq'), may hold values from -6 to 6
- cotangent: bfloat16 [16, 512, 2048], P('exp', 'seq'), may hold values from -6 to 6
- lengths: int32 [16], P('exp'), may hold values from 128 to 512, as said below
- adapter_choice: int32 [16, 8], P('exp'), may hold values from 0 to 1, as said below
- expert_ids: int32 [8, 4, 2, 128, 8], P('exp', 'seq'), may hold values from 0 to 31, all different within a row; in each aligned block of 256 rows (0 to 255, 256 to 511, ..., all dimensions but the last counted through in order) at most 96 rows name the same one
- gate_weights: float32 [8, 4, 2, 128, 8], P('exp', 'seq'), may hold values from 0.0625 to 0.1875
- attn_gain: float32 [2048], replicated, may hold values from 0.5 to 1.5
- moe_gain: float32 [2048], replicated, may hold values from 0.5 to 1.5
- query_gain: float32 [128], replicated, may hold values from 1 to 2
- key_gain: float32 [128], replicated, may hold values from 1 to 2
- w_qkv: bfloat16 [3, 2048, 2048], replicated, may hold values from -0.125 to 0.125
- w_out: bfloat16 [2048, 2048], replicated, may hold values from -0.5 to 0.5
- expert_gate: bfloat16 [32, 2048, 1024], P('exp'), may hold values from -0.125 to 0.125
- expert_up: bfloat16 [32, 2048, 1024], P('exp'), may hold values from -0.125 to 0.125
- expert_down: bfloat16 [32, 1024, 2048], P('exp'), may hold values from -1 to 1
- adapt_down: float32 [8, 4, 2048, 16], P(None, None, 'exp'), may hold values from -0.125 to 0.125
- first_down: float32 [8, 4, 2048, 16], P(None, None, 'exp'), may hold values from -1024 to 1024
- second_down: float32 [8, 4, 2048, 16], P(None, None, 'exp'), may hold values from 36864 to 147456
- adapt_up: float32 [8, 4, 16, 2048], P(None, None, None, 'exp'), may hold values from -1.5 to 1.5
- first_up: float32 [8, 4, 16, 2048], P(None, None, None, 'exp'), may hold values from -192 to 192
- second_up: float32 [8, 4, 16, 2048], P(None, None, None, 'exp'), may hold values from 1024 to 4096
Outputs:
- output: bfloat16 [16, 512, 2048], P('exp', 'seq')
- grad_input: float32 [16, 512, 2048], P('exp', 'seq')
- new_first_down: float32 [8, 4, 2048, 16], P(None, None, 'exp')
- new_second_down: float32 [8, 4, 2048, 16], P(None, None, 'exp')
- new_down: float32 [8, 4, 2048, 16], P(None, None, 'exp')
- new_first_up: float32 [8, 4, 16, 2048], P(None, None, None, 'exp')
- new_second_up: float32 [8, 4, 16, 2048], P(None, None, None, 'exp')
- new_up: float32 [8, 4, 16, 2048], P(None, None, None, 'exp')
Inputs may be any that keep to these rules, and one draw needn't show every extreme that they name: `lengths`: in each group of 2 sequences that share an index of exp, one, drawn from the seed, has length 512; the others are at least 128. `adapter_choice`: each row holds a single 1. `expert_ids`: each token names 8 different experts. Among the 256 tokens of one device (one index of exp and of seq) no expert is named more than 96 times, a bound that some block reaches.
All inputs are finite; a program needn't handle non-finite values.
Results may differ from a plain program's by a relative error of at most 0.025.
Values may be sent and summed in bfloat16 or wider, within the bound.
No kernel may reach another device: no remote copies, remote signals or barrier semaphores. Data moves between devices by JAX's collectives and lax.ppermute only.
A program may use at most 384 MiB of HBM per device.

v0:
```python
import functools

import jax
import jax.numpy as jnp
from jax import lax
from jax.experimental import pallas as pl
from jax.experimental.pallas import tpu as pltpu
from jax.sharding import PartitionSpec as P

HEAD = 128
STEP = 5

NORM_EPS = 1e-05
ROPE_BASE = 50000.0
ADAPTER_SCALE = 0.5
BETA_FIRST = 0.5
BETA_SECOND = 0.5
RATE_DOWN = 0.02
RATE_UP = 0.2
WEIGHT_DECAY = 0.01
ADAM_EPS = 1e-08
MASKED = -1e30
SCORE_SCALE = HEAD ** (-0.5)

F32 = jnp.float32
BF16 = jnp.bfloat16
VMEM_LIMIT = 62 * 1024 * 1024
COST_SHARE = 0.01


def dot_nn(a, b):
    return lax.dot_general(a, b, (((1,), (0,)), ((), ())), preferred_element_type=F32)


def dot_nt(a, b):
    return lax.dot_general(a, b, (((1,), (1,)), ((), ())), preferred_element_type=F32)


def dot_tn(a, b):
    return lax.dot_general(a, b, (((0,), (0,)), ((), ())), preferred_element_type=F32)


def inverse_rms(values):
    return lax.rsqrt(jnp.mean(values * values, axis=-1, keepdims=True) + NORM_EPS)


def norm_back(values, gain, upstream):
    inverse = inverse_rms(values)
    scaled = upstream * gain
    return inverse * scaled - values * (inverse * inverse * inverse) * jnp.mean(
        values * scaled, axis=-1, keepdims=True
    )


def sigmoid(values):
    return 0.5 + 0.5 * jnp.tanh(0.5 * values)


def adam_update(weight, gradient, first, second, step_rate):
    new_first = BETA_FIRST * first + (1.0 - BETA_FIRST) * gradient
    new_second = BETA_SECOND * second + (1.0 - BETA_SECOND) * gradient * gradient
    first_hat = new_first / (1.0 - BETA_FIRST**STEP)
    second_hat = new_second / (1.0 - BETA_SECOND**STEP)
    new_weight = weight - step_rate * (
        first_hat / (jnp.sqrt(second_hat) + ADAM_EPS) + WEIGHT_DECAY * weight
    )
    return (new_first, new_second, new_weight)


def shape_of(shape, dtype):
    return jax.ShapeDtypeStruct(shape, dtype)


def whole_block(shape):
    rank = len(shape)
    return pl.BlockSpec(tuple(shape), lambda *_: (0,) * rank)


def kernel_call(
    body, name, grid, in_specs, out_specs, out_shape, scratch=(), prefetch=0, flops=0, moved=0,
    aliases=None,
):
    return pl.pallas_call(
        body,
        grid_spec=pltpu.PrefetchScalarGridSpec(
            num_scalar_prefetch=prefetch,
            grid=grid,
            in_specs=in_specs,
            out_specs=out_specs,
            scratch_shapes=list(scratch),
        ),
        out_shape=out_shape,
        input_output_aliases=aliases or {},
        name=name,
        cost_estimate=pl.CostEstimate(
            flops=int(flops * COST_SHARE), bytes_accessed=int(moved * COST_SHARE), transcendentals=0
        ),
        compiler_params=pltpu.CompilerParams(vmem_limit_bytes=VMEM_LIMIT),
    )


def swap(values, mask):
    count = lax.axis_size("exp")
    return lax.ppermute(values, "exp", [(i, i ^ mask) for i in range(count)])


def shift(values, distance):
    count = lax.axis_size("seq")
    return lax.ppermute(values, "seq", [(i, (i + distance) % count) for i in range(count)])


def shift_order():
    count = lax.axis_size("seq")
    return sorted(range(1, count), key=lambda r: -min(r, count - r))


def forward_seq(pieces):
    if not isinstance(pieces, (list, tuple)):
        return lax.all_to_all(pieces, "seq", 0, 0)
    came = {r: shift(pieces[r], r) for r in shift_order()}
    return [pieces[0]] + [came[r] for r in range(1, len(pieces))]


def backward_seq(pieces):
    if not isinstance(pieces, (list, tuple)):
        return lax.all_to_all(pieces, "seq", 0, 0)
    came = {r: shift(pieces[r], -r) for r in shift_order()}
    return [pieces[0]] + [came[r] for r in range(1, len(pieces))]


def tell_all(values, axis):
    count = lax.axis_size(axis)
    return lax.all_to_all(jnp.broadcast_to(values[None], (count,) + values.shape), axis, 0, 0)


def by_distance(stacked):
    count = lax.axis_size("seq")
    order = (lax.axis_index("seq") - jnp.arange(count)) % count
    return jnp.take(stacked, order, axis=0)


def by_relative(stacked):
    count = lax.axis_size("exp")
    return jnp.take(stacked, lax.axis_index("exp") ^ jnp.arange(count), axis=0)


WAYS = ((2, 4), (4, 2))


def gather_rows(rows):
    count = lax.axis_size("exp")
    if count != 8 or len(rows) != 2:
        everything = by_relative(lax.all_gather(jnp.concatenate(rows), "exp"))
        return [[everything[m]] for m in range(count)]
    near = {2: [None, None], 4: [None, None], 6: [None, None]}
    for g, (first, _) in enumerate(WAYS):
        near[first][g] = swap(rows[g], first)
    for g, (_, second) in enumerate(WAYS):
        near[second][g] = swap(rows[g], second)
    for g, (first, second) in enumerate(WAYS):
        near[6][g] = swap(near[first][g], second)
    found = [list(rows), [swap(block, 1) for block in rows]]
    for m in (2, 4, 6):
        found += [near[m], [swap(block, 1) for block in near[m]]]
    return found


def add_low(*values):
    return functools.reduce(jnp.add, [value.astype(F32) for value in values]).astype(BF16)


def after(values, *first):
    return lax.optimization_barrier((values, first))[0]


ANYWHERE = pl.BlockSpec(memory_space=pl.ANY)


def group_block(shape, group):
    rank = len(shape) - 1
    return pl.BlockSpec((None,) + tuple(shape[1:]), lambda *_: (group,) + (0,) * rank)


def is_list(pieces):
    return isinstance(pieces, (list, tuple))


def piece_shape(pieces):
    if is_list(pieces):
        return len(pieces), pieces[0].shape
    return pieces.shape[0], pieces.shape[1:]


def piece_arrays(pieces, splits):
    return list(pieces) if is_list(pieces) else [pieces] * splits


def piece_specs(pieces, block, index):
    if is_list(pieces):
        return [pl.BlockSpec(block, index)] * len(pieces)
    return [
        pl.BlockSpec((None,) + tuple(block), lambda *at, r=r: (r,) + tuple(index(*at)))
        for r in range(pieces.shape[0])
    ]


def out_specs_of(listed, splits, block, index):
    if listed:
        return [pl.BlockSpec(block, index)] * splits
    return [pl.BlockSpec((splits,) + tuple(block), lambda *at: (0,) + tuple(index(*at)))]


def out_shapes_of(listed, splits, shape, dtype):
    if listed:
        return [shape_of(shape, dtype)] * splits
    return [shape_of((splits,) + tuple(shape), dtype)]


def out_refs_of(listed, refs):
    return list(refs) if listed else [refs[0].at[r] for r in range(refs[0].shape[0])]


def out_pieces_of(listed, results):
    return list(results) if listed else results[0]


def project_first(place, tokens, gain, w_qkv, groups, splits, listed):
    rows, width = tokens.shape
    part = width // splits
    shard = rows // groups
    counts = [splits if listed[g] else 1 for g in range(groups)]
    total = sum(counts)

    def body(place_ref, tok_ref, gain_ref, w_ref, *rest):
        outs = rest[:total]
        parts_ref, normed_ref, held, sem = rest[total:]
        which = pl.program_id(0)

        def owner(r):
            return lax.rem(place_ref[0] + r, splits)

        def copy(p, r):
            columns = pl.ds(pl.multiple_of(owner(r) * part, part), part)
            return pltpu.make_async_copy(
                w_ref.at[p, :, columns],
                held.at[p, :, pl.ds(r * part, part)],
                sem.at[p, r],
            )

        @pl.when(which == 0)
        def _():
            for p in range(3):
                for r in range(splits):
                    copy(p, r).start()
            values = tok_ref[...].astype(F32)
            low = (values * inverse_rms(values) * gain_ref[...]).astype(BF16)
            normed_ref[...] = low
            for z in range(splits):
                for g in range(groups):
                    parts_ref[z, g] = low[
                        g * shard : (g + 1) * shard, z * part : (z + 1) * part
                    ]

        for r in range(splits):
            copy(which, r).wait()
            result = dot_nn(normed_ref[...], held[which, :, r * part : (r + 1) * part])
            first = 0
            for g in range(groups):
                low = result[g * shard : (g + 1) * shard].astype(BF16)
                if listed[g]:
                    outs[first + r][0] = low
                else:
                    outs[first][owner(r), 0] = low
                first += counts[g]

    specs, shapes = [], []
    for g in range(groups):
        specs += out_specs_of(listed[g], splits, (1, shard, part), lambda p, s: (p, 0, 0))
        shapes += out_shapes_of(listed[g], splits, (3, shard, part), BF16)
    result = kernel_call(
        body,
        "project_first",
        (3,),
        [whole_block((rows, width)), whole_block((1, width)), ANYWHERE],
        specs + [whole_block((splits, groups, shard, part)), whole_block((rows, width))],
        shapes
        + [shape_of((splits, groups, shard, part), BF16), shape_of((rows, width), BF16)],
        scratch=[
            pltpu.VMEM((3, width, width), BF16),
            pltpu.SemaphoreType.DMA((3, splits)),
        ],
        prefetch=1,
        flops=6 * rows * width * width,
        moved=6 * width * width,
    )(place, tokens, gain, w_qkv)
    outs, first = [], 0
    for g in range(groups):
        outs.append(out_pieces_of(listed[g], result[first : first + counts[g]]))
        first += counts[g]
    return outs, result[total], result[total + 1]


def pick_sets(gathered, picks, groups, sets, sections, normed=None):
    count, _, part = gathered.shape
    width = count * part
    shard = normed.shape[0] // groups if normed is not None else 0
    number = len(sections)

    def body(pick_ref, in_ref, *rest):
        normed_ref = rest[0] if shard else None
        outs = rest[1:] if shard else rest
        outs, sem = outs[:-1], outs[-1]
        copies = []
        for g in range(groups):
            for i, (first, own) in enumerate(sections):
                for e in range(count):
                    copies.append(
                        pltpu.make_async_copy(
                            in_ref.at[e, pl.ds(pl.multiple_of(first + pick_ref[g] * own, own), own)],
                            outs[i].at[g, :, pl.ds(e * part, part)],
                            sem.at[(g * number + i) * count + e],
                        )
                    )
        for copy in copies:
            copy.start()
        for copy in copies:
            copy.wait()
        if shard:
            for g in range(groups):
                outs[number][g] = dot_nt(
                    outs[0][g], normed_ref[g * shard : (g + 1) * shard]
                ).astype(BF16)

    shapes = [(groups, own, width) for _, own in sections]
    if shard:
        shapes.append((groups, sections[0][1], shard))
    return kernel_call(
        body,
        "pick_sets",
        (1,),
        [ANYWHERE] + ([whole_block(normed.shape)] if shard else []),
        [whole_block(shape) for shape in shapes],
        [shape_of(shape, BF16) for shape in shapes],
        scratch=[pltpu.SemaphoreType.DMA((groups * number * count,))],
        prefetch=1,
        moved=4 * groups * width * sum(own for _, own in sections),
    )(picks, gathered, *([normed] if shard else []))


def route(ids, gates, choice, experts):
    top, tokens = ids.shape

    def body(ids_ref, gates_ref, choice_ref, out_ref):
        expert = lax.broadcasted_iota(jnp.int32, (experts, tokens), 0)
        weights = jnp.zeros((experts, tokens), F32)
        named = jnp.zeros((experts, tokens), F32)
        for k in range(top):
            hit = expert == ids_ref[k : k + 1]
            weights = jnp.where(hit, gates_ref[k : k + 1], weights)
            named = jnp.where(hit, 1.0, named)
        earlier = lax.broadcasted_iota(jnp.int32, (tokens, tokens), 0) < lax.broadcasted_iota(
            jnp.int32, (tokens, tokens), 1
        )
        ranks = dot_nn(named.astype(BF16), jnp.where(earlier, 1.0, 0.0).astype(BF16))
        slots = jnp.where(named > 0.0, ranks, -1.0)
        front = weights.astype(BF16)
        out_ref[:experts] = slots.astype(BF16)
        out_ref[experts : 2 * experts] = front
        out_ref[2 * experts : 3 * experts] = (weights - front.astype(F32)).astype(BF16)
        out_ref[3 * experts :] = jnp.broadcast_to(choice_ref[...], (16, tokens)).astype(BF16)

    shape = (3 * experts + 16, tokens)
    return kernel_call(
        body,
        "route",
        (1,),
        [whole_block(ids.shape), whole_block(gates.shape), whole_block(choice.shape)],
        whole_block(shape),
        shape_of(shape, BF16),
        moved=12 * experts * tokens,
    )(ids, gates, choice)


def rotate(values, cosine, sine):
    return values * cosine + pltpu.roll(values, HEAD // 2, 1) * sine


def rotate_back(values, cosine, sine):
    return values * cosine - pltpu.roll(values, HEAD // 2, 1) * sine


def softmax_rows(queries, keys, live):
    scores = jnp.where(live, dot_nt(queries, keys) * SCORE_SCALE, MASKED)
    exponent = jnp.exp(scores - jnp.max(scores, axis=-1, keepdims=True))
    return exponent * (1.0 / jnp.sum(exponent, axis=-1, keepdims=True))


def attend(length, raw, mids, ups, query_gain, key_gain, positions, cosine, sine):
    listed = is_list(raw)
    splits, (_, shard, part) = piece_shape(raw)
    rank = ups.shape[1]
    total = splits * shard
    heads = part // HEAD

    def body(len_ref, up_ref, qg_ref, kg_ref, pos_ref, cos_ref, sin_ref, *rest):
        raw_refs, mid_ref = rest[:splits], rest[splits]
        att_refs = out_refs_of(listed, rest[splits + 1 : -5])
        q_ref, k_ref, v_ref, rq_ref, rk_ref = rest[-5:]

        def full(which):
            base = jnp.concatenate([ref[which] for ref in raw_refs], axis=0).astype(F32)
            mid = jnp.concatenate(
                [mid_ref[r, which * rank : (which + 1) * rank] for r in range(splits)], axis=1
            )
            return base + ADAPTER_SCALE * dot_tn(mid, up_ref[which])

        raw_q, raw_k, raw_v = full(0), full(1), full(2)
        rq_ref[0] = raw_q
        rk_ref[0] = raw_k
        cosine, sine = cos_ref[...], sin_ref[...]
        queries = rotate(raw_q * inverse_rms(raw_q) * qg_ref[...], cosine, sine).astype(BF16)
        keys = rotate(raw_k * inverse_rms(raw_k) * kg_ref[...], cosine, sine).astype(BF16)
        values = raw_v.astype(BF16)
        q_ref[0] = queries
        k_ref[0] = keys
        v_ref[0] = values
        weights = softmax_rows(queries, keys, pos_ref[...] < len_ref[0]).astype(BF16)
        result = dot_nn(weights, values).astype(BF16)
        for r in range(splits):
            att_refs[r][...] = result[r * shard : (r + 1) * shard]

    head_block = pl.BlockSpec((1, total, HEAD), lambda h, s: (h, 0, 0))
    result = kernel_call(
        body,
        "attend",
        (heads,),
        [
            pl.BlockSpec((3, rank, HEAD), lambda h, s: (0, 0, h)),
            whole_block((1, HEAD)),
            whole_block((1, HEAD)),
            whole_block((1, total)),
            whole_block((total, HEAD)),
            whole_block((total, HEAD)),
        ]
        + piece_specs(raw, (3, shard, HEAD), lambda h, s: (0, 0, h))
        + [whole_block(mids.shape)],
        out_specs_of(listed, splits, (shard, HEAD), lambda h, s: (0, h)) + [head_block] * 5,
        out_shapes_of(listed, splits, (shard, part), BF16)
        + [shape_of((heads, total, HEAD), BF16)] * 3
        + [shape_of((heads, total, HEAD), F32)] * 2,
        prefetch=1,
        flops=4 * heads * total * total * HEAD,
        moved=heads * total * HEAD * 24 + 4 * heads * total * total,
    )(length, ups, query_gain, key_gain, positions, cosine, sine, *piece_arrays(raw, splits), mids)
    return out_pieces_of(listed, result[:-5]), result[-5:]


def attend_back(length, grads, group, saved, mids, rank, query_gain, key_gain, positions, cosine, sine):
    listed = False
    splits, _, shard, part = grads.shape
    total = splits * shard
    heads = part // HEAD

    def body(len_ref, qg_ref, kg_ref, pos_ref, cos_ref, sin_ref, *rest):
        grad_refs, mid_ref = rest[:splits], rest[splits]
        q_ref, k_ref, v_ref, rq_ref, rk_ref = rest[splits + 1 : splits + 6]
        out_refs = out_refs_of(listed, rest[splits + 6 : -1])
        gup_ref = rest[-1]
        queries, keys, values = q_ref[0], k_ref[0], v_ref[0]
        grad = jnp.concatenate([ref[...] for ref in grad_refs], axis=0)
        weights = softmax_rows(queries, keys, pos_ref[...] < len_ref[0])
        grad_probs = dot_nt(grad, values)
        inner = jnp.sum(weights * grad_probs, axis=-1, keepdims=True)
        grad_scores = (weights * (grad_probs - inner)).astype(BF16)
        grad_q = dot_nn(grad_scores, keys) * SCORE_SCALE
        grad_k = dot_tn(grad_scores, queries) * SCORE_SCALE
        grad_v = dot_tn(weights.astype(BF16), grad)
        cosine, sine = cos_ref[...], sin_ref[...]
        grad_q = norm_back(rq_ref[0], qg_ref[...], rotate_back(grad_q, cosine, sine))
        grad_k = norm_back(rk_ref[0], kg_ref[...], rotate_back(grad_k, cosine, sine))

        for which, value in enumerate((grad_q, grad_k, grad_v)):
            low = value.astype(BF16)
            for r in range(splits):
                out_refs[r][which] = low[r * shard : (r + 1) * shard]
            mid = jnp.concatenate(
                [mid_ref[r, which * rank : (which + 1) * rank] for r in range(splits)], axis=1
            )
            gup_ref[which * rank : (which + 1) * rank] = (
                ADAPTER_SCALE * dot_nn(mid, low)
            ).astype(BF16)

    head_block = pl.BlockSpec((1, total, HEAD), lambda h, s: (h, 0, 0))
    result = kernel_call(
        body,
        "attend_back",
        (heads,),
        [
            whole_block((1, HEAD)),
            whole_block((1, HEAD)),
            whole_block((1, total)),
            whole_block((total, HEAD)),
            whole_block((total, HEAD)),
        ]
        + [
            pl.BlockSpec((None, None, shard, HEAD), lambda h, s, r=r: (r, group, 0, h))
            for r in range(splits)
        ]
        + [whole_block(mids.shape)]
        + [head_block] * 5,
        out_specs_of(listed, splits, (3, shard, HEAD), lambda h, s: (0, 0, h))
        + [pl.BlockSpec((3 * rank, HEAD), lambda h, s: (0, h))],
        out_shapes_of(listed, splits, (3, shard, part), BF16)
        + [shape_of((3 * rank, part), BF16)],
        prefetch=1,
        flops=10 * heads * total * total * HEAD,
        moved=heads * total * HEAD * 24 + 8 * heads * total * total,
    )(length, query_gain, key_gain, positions, cosine, sine, *[grads] * splits, mids, *saved)
    return out_pieces_of(listed, result[:-1]), result[-1]


def project_out(attended, w_out, down, up, tokens, gain):
    splits, groups, shard, part = attended.shape
    width = splits * part
    rank = down.shape[1]
    rows = groups * shard

    def body(att_ref, w_ref, down_ref, up_ref, tok_ref, gain_ref, *rest):
        mixed_ref, mid_ref = rest[:2]
        moe_refs = rest[2 : 2 + groups]
        att, held, sem = rest[2 + groups :]
        copies = [
            pltpu.make_async_copy(
                w_ref.at[pl.ds(i * part, part)], held.at[pl.ds(i * part, part)], sem.at[i]
            )
            for i in range(splits)
        ]
        for copy in copies:
            copy.start()
        adapter = []
        for g in range(groups):
            at = slice(g * shard, (g + 1) * shard)
            for z in range(splits):
                att[at, z * part : (z + 1) * part] = att_ref[z, g]
            mid = dot_nt(down_ref[g], att[at]).astype(BF16)
            mid_ref[g] = mid
            adapter.append(
                tok_ref[g].astype(F32) + ADAPTER_SCALE * dot_tn(mid, up_ref[g])
            )
        total = jnp.concatenate(adapter, axis=0)
        for i, copy in enumerate(copies):
            copy.wait()
            total += dot_nn(att[:, i * part : (i + 1) * part], held[i * part : (i + 1) * part])
        low = (total * inverse_rms(total) * gain_ref[...]).astype(BF16)
        for g in range(groups):
            mixed_ref[g] = total[g * shard : (g + 1) * shard]
            moe_refs[g][...] = low[g * shard : (g + 1) * shard]

    result = kernel_call(
        body,
        "project_out",
        (1,),
        [
            whole_block(attended.shape),
            ANYWHERE,
            whole_block(down.shape),
            whole_block(up.shape),
            whole_block(tokens.shape),
            whole_block((1, width)),
        ],
        [
            whole_block((groups, shard, width)),
            whole_block((groups, rank, shard)),
        ]
        + [whole_block((shard, width))] * groups,
        [shape_of((groups, shard, width), F32), shape_of((groups, rank, shard), BF16)]
        + [shape_of((shard, width), BF16)] * groups,
        scratch=[
            pltpu.VMEM((rows, width), BF16),
            pltpu.VMEM((width, width), BF16),
            pltpu.SemaphoreType.DMA((splits,)),
        ],
        flops=2 * rows * width * width,
        moved=2 * width * width,
    )(attended, w_out, down, up, tokens, gain)
    return result[0], result[1], result[2:]


def one_hot(slot_row, capacity):
    tokens = slot_row.shape[1]
    index = lax.broadcasted_iota(jnp.int32, (capacity, tokens), 0).astype(F32)
    return index == slot_row


def pick_rows(sources, meta_ref, ring, sem, picked, capacity, weigh, begin=0):
    count = meta_ref.shape[0]
    experts = picked.shape[0]
    slots = ring.shape[0]

    def copies(m):
        found = sources(m)
        size = ring.shape[1] // len(found)
        return [
            pltpu.make_async_copy(
                ref, ring.at[m % slots, pl.ds(i * size, size)], sem.at[m, i]
            )
            for i, ref in enumerate(found)
        ]

    for m in range(slots):
        for copy in copies(m):
            copy.start()
    for m in range(count):
        named = jnp.concatenate(
            [one_hot(meta_ref[m, 0, e : e + 1], capacity) for e in range(begin, begin + experts)], axis=0
        )
        for copy in copies(m):
            copy.wait()
        result = dot_nn(named.astype(BF16), ring[m % slots])
        if weigh:
            weights = jnp.concatenate(
                [
                    jnp.broadcast_to(meta_ref[m, 1, e : e + 1], (capacity, named.shape[1]))
                    for e in range(begin, begin + experts)
                ],
                axis=0,
            )
            result = result * jnp.sum(jnp.where(named, weights, 0.0), axis=1, keepdims=True)
        low = result.astype(BF16)
        for e in range(experts):
            picked[e, m * capacity : (m + 1) * capacity] = low[e * capacity : (e + 1) * capacity]
        if m + slots < count:
            for copy in copies(m + slots):
                copy.start()


def expert_grad_hidden(place, gathered, meta, expert_down, capacity, begin, end):
    _, hidden, width = expert_down.shape
    experts = end - begin
    count = meta.shape[0]
    tokens = meta.shape[-1]
    rows = count * capacity

    def body(place_ref, meta_ref, w_ref, rows_ref, *rest):
        out_ref, ring, picked, sem = rest[-4:]
        expert = pl.program_id(0)

        @pl.when(expert == 0)
        def _():
            pick_rows(
                lambda m: [rows_ref.at[place_ref[1] ^ m]],
                meta_ref, ring, sem, picked, capacity, True, begin,
            )

        out_ref[0] = dot_nt(picked[expert], w_ref[0]).astype(BF16)

    return kernel_call(
        body,
        "expert_grad_hidden",
        (experts,),
        [
            whole_block(meta.shape),
            pl.BlockSpec((1, hidden, width), lambda e, s: (e + begin, 0, 0)),
            ANYWHERE,
        ],
        pl.BlockSpec((1, rows, hidden), lambda e, s: (e, 0, 0)),
        shape_of((experts, rows, hidden), BF16),
        scratch=[
            pltpu.VMEM((4, tokens, width), BF16),
            pltpu.VMEM((experts, rows, width), BF16),
            pltpu.SemaphoreType.DMA((count, 1)),
        ],
        prefetch=1,
        flops=2 * experts * rows * (hidden + tokens) * width,
        moved=2 * experts * hidden * width + 2 * count * tokens * width,
    )(place, meta, expert_down, gathered)


def combine_rows(meta_ref, picked, m, capacity):
    experts, _, width = picked.shape
    named = jnp.concatenate(
        [one_hot(meta_ref[m, 0, e : e + 1], capacity) for e in range(experts)], axis=0
    )
    named = jnp.where(named, 1.0, 0.0).T.astype(BF16)
    held = jnp.concatenate(
        [picked[e, m * capacity : (m + 1) * capacity] for e in range(experts)], axis=0
    )
    return dot_nn(named, held)


def send_combined(meta_ref, picked, ring, sem, capacity, targets):
    count = meta_ref.shape[0]
    tokens = ring.shape[1]
    slots = ring.shape[0]
    waiting = {}
    for i, m in enumerate(reversed(range(count))):
        for copy in waiting.pop(i - slots, []):
            copy.wait()
        ring[i % slots] = combine_rows(meta_ref, picked, m, capacity).astype(BF16)
        found = targets(m)
        size = tokens // len(found)
        waiting[i] = [
            pltpu.make_async_copy(
                ring.at[i % slots, pl.ds(b * size, size)], ref, sem.at[i % slots, b]
            )
            for b, ref in enumerate(found)
        ]
        for copy in waiting[i]:
            copy.start()
    for copies in waiting.values():
        for copy in copies:
            copy.wait()


def expert_middle(
    place, gathered, meta, expert_gate, expert_up, grad_hidden, capacity, groups, paired
):
    experts, width, hidden = expert_gate.shape
    count = meta.shape[0]
    tokens = meta.shape[-1]
    rows = count * capacity
    chunk = 256 if rows % 256 == 0 else rows
    numbers = [len(found) for found in gathered]
    arrays = [array for found in gathered for array in found]
    even = [m for m in range(count) if m % 2 == 0]

    def body(place_ref, meta_ref, gate_ref, up_ref, gh_ref, *rest):
        refs, (h_ref, *outs) = rest[: len(arrays)], rest[len(arrays) : -5]
        ring, picked, made, sem, out_sem = rest[-5:]
        expert = pl.program_id(0)

        @pl.when(expert == 0)
        def _():
            pick_rows(
                lambda m: refs[sum(numbers[:m]) : sum(numbers[: m + 1])],
                meta_ref, ring, sem, picked, capacity, False,
            )

        for c in range(rows // chunk):
            at = slice(c * chunk, (c + 1) * chunk)
            x = picked[expert, at]
            gate = dot_nn(x, gate_ref[0])
            up = dot_nn(x, up_ref[0])
            sigma = sigmoid(gate)
            value = gate * sigma
            grad = gh_ref[0, at].astype(F32)
            h_ref[0, at] = (value * up).astype(BF16)
            grad_gate = (grad * up * (sigma + value * (1.0 - sigma))).astype(BF16)
            grad_up = (grad * value).astype(BF16)
            made[expert, at] = (
                dot_nt(grad_gate, gate_ref[0]) + dot_nt(grad_up, up_ref[0])
            ).astype(BF16)

        @pl.when(expert == experts - 1)
        def _():
            def targets(m):
                if not paired:
                    return [outs[0].at[place_ref[1] ^ m]]
                if m % 2:
                    return [outs[-1].at[m // 2]]
                return outs[m // 2 * groups : (m // 2 + 1) * groups]

            send_combined(meta_ref, made, ring, out_sem, capacity, targets)

    if paired:
        shapes = [shape_of((tokens // groups, width), BF16)] * (len(even) * groups)
        shapes.append(shape_of((count // 2, tokens, width), BF16))
    else:
        shapes = [shape_of((count, tokens, width), BF16)]
    result = kernel_call(
        body,
        "expert_middle",
        (experts,),
        [
            whole_block(meta.shape),
            pl.BlockSpec((1, width, hidden), lambda e, s: (e, 0, 0)),
            pl.BlockSpec((1, width, hidden), lambda e, s: (e, 0, 0)),
            pl.BlockSpec((1, rows, hidden), lambda e, s: (e, 0, 0)),
        ]
        + [ANYWHERE] * len(arrays),
        [pl.BlockSpec((1, rows, hidden), lambda e, s: (e, 0, 0))] + [ANYWHERE] * len(shapes),
        [shape_of((experts, rows, hidden), BF16)] + shapes,
        scratch=[
            pltpu.VMEM((2, tokens, width), BF16),
            pltpu.VMEM((experts, rows, width), BF16),
            pltpu.VMEM((experts, rows, width), BF16),
            pltpu.SemaphoreType.DMA((count, max(numbers))),
            pltpu.SemaphoreType.DMA((2, groups)),
        ],
        prefetch=1,
        flops=2 * experts * rows * (4 * hidden + tokens) * width,
        moved=4 * experts * hidden * width + 4 * experts * rows * width,
    )(place, meta, expert_gate, expert_up, grad_hidden, *arrays)
    if not paired:
        return result[0], result[1], None
    near = {m: result[1 + i * groups : 1 + (i + 1) * groups] for i, m in enumerate(even)}
    return result[0], near, result[-1]


def expert_produce(place, hidden_rows, meta, expert_down, capacity, first, last, before=None):
    experts, hidden, width = expert_down.shape
    count = meta.shape[0]
    tokens = meta.shape[-1]
    rows = count * capacity
    held = before.shape[0] if before is not None else 0

    def body(place_ref, meta_ref, h_ref, w_ref, *rest):
        expert = pl.program_id(0) + first
        result = dot_nn(h_ref[0], w_ref[0])
        if held:
            before_ref, out_ref, ring, made, sem, before_sem = rest
            copy = pltpu.make_async_copy(before_ref, made.at[pl.ds(0, held)], before_sem)

            @pl.when(expert == first)
            def _():
                copy.start()

        else:
            (out_ref,) = rest
        for m in range(count):
            named = one_hot(meta_ref[m, 0, pl.ds(expert, 1)], capacity)
            weight = jnp.sum(
                jnp.where(named, meta_ref[m, 1, pl.ds(expert, 1)], 0.0), axis=1, keepdims=True
            )
            at = slice(m * capacity, (m + 1) * capacity)
            value = (weight * result[at]).astype(BF16)
            if held:
                made[expert, at] = value
            else:
                out_ref[0, at] = value

        if held:

            @pl.when(expert == last - 1)
            def _():
                copy.wait()
                send_combined(
                    meta_ref, made, ring, sem, capacity, lambda m: [out_ref.at[place_ref[1] ^ m]]
                )

    out_spec, shape = ANYWHERE, shape_of((count, tokens, width), BF16)
    if not held:
        out_spec = pl.BlockSpec((1, rows, width), lambda e, s: (e, 0, 0))
        shape = shape_of((last - first, rows, width), BF16)
    return kernel_call(
        body,
        "expert_produce",
        (last - first,),
        [
            whole_block(meta.shape),
            pl.BlockSpec((1, rows, hidden), lambda e, s: (e + first, 0, 0)),
            pl.BlockSpec((1, hidden, width), lambda e, s: (e + first, 0, 0)),
        ]
        + ([ANYWHERE] if held else []),
        out_spec,
        shape,
        scratch=[
            pltpu.VMEM((2, tokens, width), BF16),
            pltpu.VMEM((experts, rows, width), BF16),
            pltpu.SemaphoreType.DMA((2, 1)),
            pltpu.SemaphoreType.DMA,
        ]
        if held
        else [],
        prefetch=1,
        flops=2 * (last - first) * rows * hidden * width,
        moved=2 * experts * hidden * width + 2 * experts * rows * width,
    )(place, meta, hidden_rows, expert_down, *([before] if held else []))


def project_out_back(pieces, mixed, upstream, gain, w_out, down, up, attended, mids):
    splits, groups, shard, part = attended.shape
    width = splits * part
    rank = down.shape[1]
    rows = groups * shard
    number = len(pieces[0])

    def body(up_stream_ref, gain_ref, w_ref, down_ref, up_ref, mixed_ref, att_ref, mid_ref, *rest):
        refs, rest = rest[: groups * number], rest[groups * number :]
        gm_ref, gdown_ref, gup_ref, out_ref, low, held, sem = rest
        copies = [
            pltpu.make_async_copy(w_ref.at[pl.ds(z * part, part)], held.at[z], sem.at[z])
            for z in range(splits)
        ]
        for copy in copies:
            copy.start()
        smalls = []
        for g in range(groups):
            total = refs[g * number][...].astype(F32)
            for ref in refs[g * number + 1 : (g + 1) * number]:
                total += ref[...].astype(F32)
            grad = up_stream_ref[g].astype(F32) + norm_back(mixed_ref[g], gain_ref[...], total)
            gm_ref[g] = grad
            grad = grad.astype(BF16)
            low[g * shard : (g + 1) * shard] = grad
            small = (ADAPTER_SCALE * dot_nt(up_ref[g], grad)).astype(BF16)
            smalls.append(small)
            gup_ref[g] = (ADAPTER_SCALE * dot_nn(mid_ref[g], grad)).astype(BF16)
        for z in range(splits):
            columns = slice(z * part, (z + 1) * part)
            copies[z].wait()
            result = dot_nt(low[...], held[z])
            for g in range(groups):
                out_ref[z, g] = (
                    result[g * shard : (g + 1) * shard] + dot_tn(smalls[g], down_ref[g, :, columns])
                ).astype(BF16)
                gdown_ref[g, :, columns] = dot_nn(smalls[g], att_ref[z, g]).astype(BF16)

    return kernel_call(
        body,
        "project_out_back",
        (1,),
        [
            whole_block(upstream.shape),
            whole_block((1, width)),
            ANYWHERE,
            whole_block(down.shape),
            whole_block(up.shape),
            whole_block(mixed.shape),
            whole_block(attended.shape),
            whole_block(mids.shape),
        ]
        + [whole_block((shard, width))] * (groups * number),
        [
            whole_block((groups, shard, width)),
            whole_block((groups, rank, width)),
            whole_block((groups, rank, width)),
            whole_block(attended.shape),
        ],
        [
            shape_of((groups, shard, width), F32),
            shape_of((groups, rank, width), BF16),
            shape_of((groups, rank, width), BF16),
            shape_of(attended.shape, BF16),
        ],
        scratch=[
            pltpu.VMEM((rows, width), BF16),
            pltpu.VMEM((splits, part, width), BF16),
            pltpu.SemaphoreType.DMA((splits,)),
        ],
        flops=2 * rows * width * width,
        moved=2 * width * width,
    )(
        upstream, gain, w_out, down, up, mixed, attended, mids,
        *[array for found in pieces for array in found],
    )


def adapter_grads(place, group, grads, normed, ups, devices):
    listed = is_list(grads)
    splits, (_, shard, part) = piece_shape(grads)
    width = splits * part
    own = ups.shape[1]
    rank = own // 3
    slice_width = width // devices

    def body(place_ref, normed_ref, up_ref, *rest):
        refs, (small_ref, down_ref, low) = rest[:splits], rest[splits:]
        for which in range(3):
            for r in range(splits):
                owner = lax.rem(place_ref[0] + r, splits) if listed else r
                low[:, pl.ds(pl.multiple_of(owner * part, part), part)] = refs[r][which]
            at = slice(which * rank, (which + 1) * rank)
            small = (ADAPTER_SCALE * dot_nt(up_ref[at], low[...])).astype(BF16)
            small_ref[at] = small
            result = dot_nn(small, normed_ref[...]).astype(BF16)
            for e in range(devices):
                down_ref[e, at] = result[:, e * slice_width : (e + 1) * slice_width]

    return kernel_call(
        body,
        "adapter_grads",
        (1,),
        [
            pl.BlockSpec((shard, width), lambda i, s: (group, 0)),
            group_block(ups.shape, group),
        ]
        + piece_specs(grads, (3, shard, part), lambda i, s: (0, 0, 0)),
        [whole_block((own, shard)), whole_block((devices, own, slice_width))],
        [shape_of((own, shard), BF16), shape_of((devices, own, slice_width), BF16)],
        scratch=[pltpu.VMEM((shard, width), BF16)],
        prefetch=1,
        flops=12 * shard * rank * width,
        moved=6 * shard * width,
    )(place, normed, ups, *piece_arrays(grads, splits))


def project_first_back(place, grads, smalls, downs, w_qkv, tokens, gain, grad_mixed):
    groups = len(grads)
    listed = [is_list(pieces) for pieces in grads]
    splits, (_, shard, part) = piece_shape(grads[0])
    width = splits * part
    rows = groups * shard

    rank = downs.shape[1] // 3

    def body(place_ref, down_ref, w_ref, tok_ref, gain_ref, mixed_ref, *rest):
        small_refs, refs = rest[:groups], rest[groups : groups + groups * splits]
        out_ref, low, total, held, sem = rest[groups + groups * splits :]
        which = pl.program_id(0)

        def copy(p):
            return pltpu.make_async_copy(w_ref.at[p], held.at[p], sem.at[p])

        @pl.when(which == 0)
        def _():
            for p in range(3):
                copy(p).start()

        for g in range(groups):
            for r in range(splits):
                owner = lax.rem(place_ref[0] + r, splits) if listed[g] else r
                low[
                    g * shard : (g + 1) * shard, pl.ds(pl.multiple_of(owner * part, part), part)
                ] = refs[g * splits + r][0]
        at = pl.ds(pl.multiple_of(which * rank, rank), rank)
        small = jnp.concatenate(
            [dot_tn(small_refs[g][at], down_ref[g, at]) for g in range(groups)], axis=0
        )
        copy(which).wait()
        result = dot_nt(low[...], held[which]) + small

        @pl.when(which == 0)
        def _():
            total[...] = result

        @pl.when(which == 1)
        def _():
            total[...] += result

        @pl.when(which == 2)
        def _():
            back = norm_back(tok_ref[...].astype(F32), gain_ref[...], total[...] + result)
            for g in range(groups):
                out_ref[g] = mixed_ref[g] + back[g * shard : (g + 1) * shard]

    return kernel_call(
        body,
        "project_first_back",
        (3,),
        [
            whole_block(downs.shape),
            ANYWHERE,
            whole_block((rows, width)),
            whole_block((1, width)),
            whole_block(grad_mixed.shape),
        ]
        + [whole_block((3 * rank, shard))] * groups
        + [
            spec
            for pieces in grads
            for spec in piece_specs(pieces, (1, shard, part), lambda p, s: (p, 0, 0))
        ],
        whole_block((groups, shard, width)),
        shape_of((groups, shard, width), F32),
        scratch=[
            pltpu.VMEM((rows, width), BF16),
            pltpu.VMEM((rows, width), F32),
            pltpu.VMEM((3, width, width), BF16),
            pltpu.SemaphoreType.DMA((3,)),
        ],
        prefetch=1,
        flops=6 * rows * width * width,
        moved=6 * width * width,
    )(
        place, downs, w_qkv, tokens, gain, grad_mixed, *smalls,
        *[piece for pieces in grads for piece in piece_arrays(pieces, splits)],
    )


def local(
    tokens,
    cotangent,
    lengths,
    adapter_choice,
    expert_ids,
    gate_weights,
    attn_gain,
    moe_gain,
    query_gain,
    key_gain,
    w_qkv,
    w_out,
    expert_gate,
    expert_up,
    expert_down,
    adapt_down,
    first_down,
    second_down,
    adapt_up,
    first_up,
    second_up,
):
    groups, shard, width = tokens.shape
    splits = lax.axis_size("seq")
    devices = lax.axis_size("exp")
    here = lax.axis_index("seq")
    total = shard * splits
    part = width // splits
    rows = groups * shard
    sets, projections, slice_width, rank = adapt_down.shape
    local_experts = expert_gate.shape[0]
    experts = local_experts * devices
    top = expert_ids.shape[-1]
    capacity = 3 * rows * top // (2 * experts)
    listed = [False] * groups

    position = lax.axis_index("exp")
    place = jnp.stack([here, position]).astype(jnp.int32)
    flat_tokens = tokens.reshape(rows, width)
    gain_row = attn_gain.reshape(1, width)
    moe_row = moe_gain.reshape(1, width)
    query_row = query_gain.reshape(1, HEAD)
    key_row = key_gain.reshape(1, HEAD)

    own_positions = here * shard + jnp.arange(shard, dtype=jnp.int32)
    own_live = own_positions[None, :] < lengths[:, None]
    upstream = jnp.where(own_live[:, :, None], cotangent, jnp.zeros((), BF16))
    ids = expert_ids.reshape(rows, top).T
    gates = gate_weights.reshape(rows, top).T
    choice = adapter_choice.astype(F32).reshape(1, groups * sets)
    choice = jnp.pad(choice, ((0, 0), (0, rows - groups * sets)))
    routed = route(ids, gates, choice, experts)
    down_rows = jnp.swapaxes(adapt_down.astype(BF16), 2, 3)
    adapter_rows = jnp.concatenate(
        [
            down_rows[:, :3].reshape(-1, slice_width),
            down_rows[:, 3].reshape(-1, slice_width),
            adapt_up[:, :3].astype(BF16).reshape(-1, slice_width),
            adapt_up[:, 3].astype(BF16).reshape(-1, slice_width),
            routed.reshape(-1, slice_width),
        ]
    )
    all_adapters = lax.all_gather(adapter_rows, "exp")

    base, _, normed = project_first(
        place, after(flat_tokens, adapter_rows), gain_row, w_qkv, groups, splits, listed
    )
    raw = [forward_seq(base[0])]
    cot_rows = lax.all_gather(after(upstream, normed).reshape(rows, width), "exp")

    own = 3 * rank
    chosen = jnp.sum(adapter_choice * jnp.arange(sets, dtype=jnp.int32)[None, :], axis=1)
    sections = [
        (0, own), (sets * own, rank), (sets * (own + rank), own), (sets * (2 * own + rank), rank),
    ]
    downs, out_downs, ups, out_ups, mids = pick_sets(
        all_adapters, chosen, groups, sets, sections, normed
    )
    all_mids = by_distance(jnp.stack(forward_seq([mids] * splits)))
    raw[0], all_mids = lax.optimization_barrier((raw[0], all_mids))
    for g in range(1, groups):
        raw.append(forward_seq(after(base[g], raw[g - 1])))
    gathered = after(all_adapters, raw[0])[:, 2 * sets * projections * rank :]
    gathered = gathered.reshape(devices, 3 * experts + 16, rows)
    choices = gathered[:, 3 * experts, : groups * sets].reshape(devices, groups, sets)
    meta = gathered[:, : 3 * experts].reshape(devices, 3, experts, rows)
    meta = lax.dynamic_slice_in_dim(meta, position * local_experts, local_experts, axis=2)
    meta = meta.astype(F32)
    meta = by_relative(jnp.stack([meta[:, 0], meta[:, 1] + meta[:, 2]], axis=1))
    own_ups = lax.dynamic_slice_in_dim(ups, here * part, part, axis=2)
    own_ups = own_ups.reshape(groups, 3, rank, part)

    blocks = jnp.arange(splits, dtype=jnp.int32)
    frequency = ROPE_BASE ** (-(2.0 / HEAD) * jnp.arange(HEAD // 2, dtype=F32))
    tables = []
    for g in range(groups):
        positions = blocks[:, None] * shard + jnp.arange(shard, dtype=jnp.int32)[None, :]
        angles = after(positions, raw[0]).reshape(total, 1).astype(F32) * frequency[None, :]
        cosine, sine = jnp.cos(angles), jnp.sin(angles)
        tables.append(
            (
                positions.reshape(1, total),
                jnp.concatenate([cosine, cosine], axis=1),
                jnp.concatenate([-sine, sine], axis=1),
            )
        )

    saved, heads_rows = [], []
    for g in range(groups):
        if g:
            raw[g] = after(raw[g], heads_rows)
        att, kept = attend(
            lengths[g : g + 1],
            raw[g],
            all_mids[:, g],
            own_ups[g],
            query_row,
            key_row,
            *tables[g],
        )
        saved.append(kept)
        heads_rows.append(att)
    heads_rows = jnp.stack(heads_rows, axis=1)
    attended = lax.all_to_all(heads_rows, "seq", 0, 0)
    grad_hidden = expert_grad_hidden(
        place, cot_rows, after(meta, heads_rows), expert_down, capacity, 0, local_experts
    )
    attended, grad_hidden = lax.optimization_barrier((attended, grad_hidden))
    mixed, mid_out, moe_rows = project_out(
        attended, w_out, out_downs, out_ups, tokens, moe_row
    )
    gathered = gather_rows(moe_rows)
    half = local_experts // 2

    paired = devices == 8 and groups == 2
    hidden, parts, others = expert_middle(
        place,
        gathered,
        meta,
        expert_gate,
        expert_up,
        grad_hidden,
        capacity,
        groups,
        paired,
    )
    if paired:
        beside = swap(others, 1).reshape(devices // 2, groups, shard, width)
        far_sums = [add_low(parts[6][g], beside[3][g]) for g in range(groups)]
        near_sums = [add_low(parts[WAYS[g][0]][g], beside[WAYS[g][0] // 2][g]) for g in range(groups)]
        far_sums, near_sums = lax.optimization_barrier((far_sums, near_sums))
        far = [swap(far_sums[g], WAYS[g][0]) for g in range(groups)]
        near = [swap(near_sums[g], WAYS[g][0]) for g in range(groups)]
        produced = expert_produce(
            place, after(hidden, far_sums), meta, expert_down, capacity, 0, half
        )
        far, produced = lax.optimization_barrier((far, produced))
        joined_sums = [
            add_low(parts[WAYS[g][1]][g], beside[WAYS[g][1] // 2][g], far[g]) for g in range(groups)
        ]
        joined = [swap(joined_sums[g], WAYS[g][1]) for g in range(groups)]
        grad_pieces = [
            [parts[0][g], beside[0][g], near[g], joined[g]] for g in range(groups)
        ]
    else:
        summed = lax.psum_scatter(parts, "exp").reshape(groups, shard, width)
        grad_pieces = [[summed[g]] for g in range(groups)]
        produced = expert_produce(place, hidden, meta, expert_down, capacity, 0, half)
    grad_mixed, grad_out_downs, grad_out_ups, grad_att = project_out_back(
        grad_pieces, mixed, upstream, moe_row, w_out, out_downs, out_ups, attended, mid_out
    )
    out_parts = expert_produce(
        place, hidden, after(meta, grad_mixed), expert_down, capacity, half, local_experts, produced
    )
    grad_att = lax.all_to_all(grad_att, "seq", 0, 0)
    grad_raw, gups = [], []
    for g in range(groups):
        if g:
            grad_att = after(grad_att, gups)
        back, gup = attend_back(
            lengths[g : g + 1],
            grad_att,
            g,
            saved[g],
            all_mids[:, g],
            rank,
            query_row,
            key_row,
            *tables[g],
        )
        gups.append(gup)
        if not g:
            out_sum = lax.psum_scatter(after(out_parts, gup), "exp")
        grad_raw.append(forward_seq(after(back, grad_raw) if g else back))
    out_sum = out_sum.reshape(groups, shard, width)

    gups = jnp.stack(after(gups, grad_raw[0]))
    wide_ups = lax.dynamic_update_slice_in_dim(
        jnp.zeros((groups, own, width), BF16), gups, here * part, axis=2
    )
    early = jnp.concatenate([grad_out_downs, wide_ups, grad_out_ups], axis=1)
    early = jnp.moveaxis(early.reshape(groups, -1, devices, slice_width), 2, 0)
    output = (mixed + after(out_sum, gups).astype(F32)).astype(BF16)

    smalls, late = [], []
    for g in range(groups):
        small, down = adapter_grads(place, g, grad_raw[g], normed, ups, devices)
        smalls.append(small)
        late.append(down)
    late = jnp.concatenate([jnp.stack(late, axis=1), early], axis=2)
    late = lax.all_to_all(late, "exp", 0, 0)
    grad_input = project_first_back(
        place, grad_raw, smalls, downs, w_qkv, after(flat_tokens, output), gain_row, grad_mixed
    )
    late = after(late, grad_input)
    pieces = jnp.einsum("dgk,dgrw->krw", choices, late, preferred_element_type=F32)
    pieces = pieces.astype(BF16)
    pieces = pieces.reshape(splits, -1, slice_width)
    order = (here + jnp.arange(splits)) % splits
    pieces = list(jnp.take(pieces, order, axis=0))
    summed = add_low(*forward_seq(pieces))
    in_sets = by_distance(jnp.stack(forward_seq([summed] * splits)))
    in_sets = in_sets.reshape(sets, 2, projections, rank, slice_width).astype(F32)
    shard_down = jnp.swapaxes(in_sets[:, 0], 2, 3)
    shard_up = in_sets[:, 1]
    new_first_down, new_second_down, new_down = adam_update(
        adapt_down, shard_down, first_down, second_down, RATE_DOWN
    )
    new_first_up, new_second_up, new_up = adam_update(
        adapt_up, shard_up, first_up, second_up, RATE_UP
    )
    return (
        output,
        grad_input,
        new_first_down,
        new_second_down,
        new_down,
        new_first_up,
        new_second_up,
        new_up,
    )


def solution(mesh):
    in_specs = (
        P("exp", "seq", None),
        P("exp", "seq", None),
        P("exp"),
        P("exp", None),
        P("exp", "seq", None, None, None),
        P("exp", "seq", None, None, None),
        P(),
        P(),
        P(),
        P(),
        P(),
        P(),
        P("exp", None, None),
        P("exp", None, None),
        P("exp", None, None),
        P(None, None, "exp", None),
        P(None, None, "exp", None),
        P(None, None, "exp", None),
        P(None, None, None, "exp"),
        P(None, None, None, "exp"),
        P(None, None, None, "exp"),
    )
    out_specs = (
        P("exp", "seq", None),
        P("exp", "seq", None),
        P(None, None, "exp", None),
        P(None, None, "exp", None),
        P(None, None, "exp", None),
        P(None, None, None, "exp"),
        P(None, None, None, "exp"),
        P(None, None, None, "exp"),
    )
    return jax.shard_map(local, mesh=mesh, in_specs=in_specs, out_specs=out_specs, check_vma=False)
```

profile of v0, /device:TPU:0, one launch (start us, length us, event | category | flops | bytes accessed | tf_op | source)
XLA Modules:
  0.0 556.8 jit_solution(7610557651542772153)
XLA Ops:
  14.6 14.4 %project_first.1 = (bf16[4,3,128,512]{3,2,1,0:T(8,128)(2,1)}, bf16[4,3,128,512]{3,2,1,0:T(8,128)(2,1)}, bf16[4,2,128,512]{3,2,1,0:T(8,128)(2,1)}, bf16[256,2048]{1,0:T(8,128)(2,1)}) custom-call(s32[2]{0:T(128)} %pad_add_fusion.place_ref, bf16[256,2048]{1,0:T(8,128)(2,1)} %bitcast.135, f32[1,2048]{1,0:T(1,128)} %bitcast.168, bf16[3,2048,2048]{2,1,0:T(8,128)(2,1)} %w_ref.13), custom_call_target="tpu_custom_call" | custom-call | flops 64424508 | bytes 251658 | tf_op jit(solution)/shard_map/project_first/pallas_call | solution.py:280
  36.7 18.8 %all-gather.6.cloned.1.call-done = bf16[9088,256]{1,0:T(8,128)(2,1)} async-done(((bf16[1136,256]{1,0:T(8,128)(2,1)}), bf16[9088,256]{1,0:T(8,128)(2,1)}) %all-gather.6.cloned.1.call-update) | async-done | bytes 4653072 | tf_op jit(solution)/shard_map/all_gather | solution.py:1134
  65.3 10.3 %collective-permute-done.1 = bf16[2,48,128]{2,1,0:T(8,128)(2,1)S(1)} collective-permute-done((bf16[2,48,128]{2,1,0:T(8,128)(2,1)}, bf16[2,48,128]{2,1,0:T(8,128)(2,1)S(1)}, u32[]{:S(2)}, u32[]{:S(2)}) %collective-permute-start.1) | collective-permute-done | bytes 24608 | tf_op jit(solution)/shard_map/ppermute | solution.py:109
  86.3 9.9 %attend.2 = (bf16[4,128,512]{2,1,0:T(8,128)(2,1)}, bf16[4,512,128]{2,1,0:T(8,128)(2,1)}, bf16[4,512,128]{2,1,0:T(8,128)(2,1)}, bf16[4,512,128]{2,1,0:T(8,128)(2,...) custom-call(s32[1]{0:T(128)} %get-tuple-element.185.len_ref, bf16[3,16,512]{2,1,0:T(8,128)(2,1)} %bitcast.154, ...), custom_call_target="tpu_custom_call" | custom-call | flops 5368709 | bytes 104857 | tf_op jit(solution)/shard_map/attend/pallas_call | solution.py:433
  96.2 21.8 %all-to-all-done.1.rest_0_.rest_1_.rest_2_.rest_3_ = bf16[4,3,128,512]{3,2,1,0:T(8,128)(2,1)} async-done(((bf16[4,3,128,512]{3,2,1,0:T(8,128)(2,1)}), bf16[4,3,128,512]{3,2,1,0:T(8,128)(2,1)}, u32[]{:S(2)}, u32[]{:S(2)}) %all-to-all-start.1) | async-done | bytes 1572896 | tf_op jit(solution)/shard_map/all_to_all | solution.py:119
  118.0 10.0 %attend.3 = (bf16[4,128,512]{2,1,0:T(8,128)(2,1)}, bf16[4,512,128]{2,1,0:T(8,128)(2,1)}, bf16[4,512,128]{2,1,0:T(8,128)(2,1)}, bf16[4,512,128]{2,1,0:T(8,128)(2,...) custom-call(s32[1]{0:T(128)} %get-tuple-element.186.len_ref, bf16[3,16,512]{2,1,0:T(8,128)(2,1)} %bitcast.153, ...), custom_call_target="tpu_custom_call" | custom-call | flops 5368709 | bytes 104857 | tf_op jit(solution)/shard_map/attend/pallas_call | solution.py:433
  136.4 24.4 %expert_grad_hidden.1.gh_ref = bf16[4,768,1024]{2,1,0:T(8,128)(2,1)} custom-call(s32[2]{0:T(128)} %pad_add_fusion.place_ref, f32[8,2,4,256]{3,2,1,0:T(4,128)} %broadcast_select_fusion.3.meta_ref, bf16[4,1024,2048]{2,1,0:T(8,128)(2,1)} %w_ref.12, bf16[8,256,2048]{2,1,0:T(8,128)(2,1)} %all-gather.4.cloned.1.call-done.rows_ref), custom_call_target="tpu_custom_call" | custom-call | flops 161061280 | bytes 251658 | tf_op jit(solution)/shard_map/expert_grad_hidden/pallas_call | solution.py:657
  161.7 7.5 %project_out.1 = (f32[2,128,2048]{2,1,0:T(8,128)}, bf16[2,16,128]{2,1,0:T(8,128)(2,1)}, bf16[128,2048]{1,0:T(8,128)(2,1)}, bf16[128,2048]{1,0:T(8,128)(2,1)}) custom-call(bf16[4,2,128,512]{3,2,1,0:T(8,128)(2,1)} %copy-done.3, bf16[2048,2048]{1,0:T(8,128)(2,1)} %w_ref.11, bf16[2,16,2048]{2,1,0:T(8,128)(2,1)} %get-tuple-element.100.down_ref, ...), custom_call_target="tpu_custom_call" | custom-call | flops 21474836 | bytes 83886 | tf_op jit(solution)/shard_map/project_out/pallas_call | solution.py:559
  173.4 11.0 %collective-permute-done.9.rest_8_ = bf16[128,2048]{1,0:T(8,128)(2,1)S(1)} collective-permute-done((bf16[128,2048]{1,0:T(8,128)(2,1)}, bf16[128,2048]{1,0:T(8,128)(2,1)S(1)}, u32[]{:S(2)}, u32[]{:S(2)}) %collective-permute-start.9) | collective-permute-done | bytes 524320 | tf_op jit(solution)/shard_map/ppermute | solution.py:104
  186.5 9.1 %collective-permute-done.10.rest_9_ = bf16[128,2048]{1,0:T(8,128)(2,1)S(1)} collective-permute-done((bf16[128,2048]{1,0:T(8,128)(2,1)}, bf16[128,2048]{1,0:T(8,128)(2,1)S(1)}, u32[]{:S(2)}, u32[]{:S(2)}) %collective-permute-start.10) | collective-permute-done | bytes 524320 | tf_op jit(solution)/shard_map/ppermute | solution.py:104
  197.7 7.1 %collective-permute-done.13.rest_12_ = bf16[128,2048]{1,0:T(8,128)(2,1)S(1)} collective-permute-done((bf16[128,2048]{1,0:T(8,128)(2,1)S(1)}, bf16[128,2048]{1,0:T(8,128)(2,1)S(1)}, u32[]{:S(2)}, u32[]{:S(2)}) %collective-permute-start.13) | collective-permute-done | bytes 524320 | tf_op jit(solution)/shard_map/ppermute | solution.py:104
  208.3 91.5 %expert_middle.1 = (bf16[4,768,1024]{2,1,0:T(8,128)(2,1)}, bf16[128,2048]{1,0:T(8,128)(2,1)}, bf16[128,2048]{1,0:T(8,128)(2,1)}, bf16[128,2048]{1,0:T(8,128)(2,1...) custom-call(s32[2]{0:T(128)} %pad_add_fusion.place_ref, ...), custom_call_target="tpu_custom_call" | custom-call | flops 547608320 | bytes 587202 | tf_op jit(solution)/shard_map/expert_middle/pallas_call | solution.py:770
  300.2 7.0 %collective-permute-done.17 = bf16[4,256,2048]{2,1,0:T(8,128)(2,1)S(1)} collective-permute-done((bf16[4,256,2048]{2,1,0:T(8,128)(2,1)}, bf16[4,256,2048]{2,1,0:T(8,128)(2,1)S(1)}, u32[]{:S(2)}, u32[]{:S(2)}) %collective-permute-start.17) | collective-permute-done | bytes 4194336 | tf_op jit(solution)/shard_map/ppermute | solution.py:104
  316.0 12.2 %expert_produce.2.rest_0_ = bf16[2,768,2048]{2,1,0:T(8,128)(2,1)} custom-call(s32[2]{0:T(128)} %pad_add_fusion.place_ref, f32[8,2,4,256]{3,2,1,0:T(4,128)} %broadcast_select_fusion.3.meta_ref, bf16[4,768,1024]{2,1,0:T(8,128)(2,1)} %get-tuple-element.118.h_ref, bf16[4,1024,2048]{2,1,0:T(8,128)(2,1)} %w_ref.12), custom_call_target="tpu_custom_call" | custom-call | flops 64424508 | bytes 293601 | tf_op jit(solution)/shard_map/expert_produce/pallas_call | solution.py:845
  339.6 9.2 %collective-permute-done.23.rest_7_ = bf16[128,2048]{1,0:T(8,128)(2,1)} collective-permute-done((bf16[128,2048]{1,0:T(8,128)(2,1)S(1)}, bf16[128,2048]{1,0:T(8,128)(2,1)}, u32[]{:S(2)}, u32[]{:S(2)}) %collective-permute-start.23) | collective-permute-done | bytes 524320 | tf_op jit(solution)/shard_map/ppermute | solution.py:104
  350.1 9.5 %project_out_back.1 = (f32[2,128,2048]{2,1,0:T(8,128)}, bf16[2,16,2048]{2,1,0:T(8,128)(2,1)}, bf16[2,16,2048]{2,1,0:T(8,128)(2,1)}, bf16[4,2,128,512]{3,2,1,0:T(8,128)(2,1)}) custom-call(bf16[2,128,2048]{2,1,0:T(8,128)(2,1)} %broadcast_select_fusion.up_stream_ref, f32[1,2048]{1,0:T(1,128)} %bitcast.167, bf16[2048,2048]{1,0:T(8,128)(2,1)} %w_ref.11, ...), custom_call_target="tpu_custom_call" | custom-call | flops 21474836 | bytes 83886 | tf_op jit(solution)/shard_map/project_out_back/pallas_call | solution.py:909
  364.4 18.1 %expert_produce.3 = bf16[8,256,2048]{2,1,0:T(8,128)(2,1)} custom-call(s32[2]{0:T(128)} %pad_add_fusion.place_ref, f32[8,2,4,256]{3,2,1,0:T(4,128)} %broadcast_select_fusion.3.meta_ref, bf16[4,768,1024]{2,1,0:T(8,128)(2,1)} %get-tuple-element.118.h_ref, bf16[4,1024,2048]{2,1,0:T(8,128)(2,1)} %w_ref.12, bf16[2,768,2048]{2,1,0:T(8,128)(2,1)} %expert_produce.2.rest_0_), custom_call_target="tpu_custom_call" | custom-call | flops 64424508 | bytes 293601 | tf_op jit(solution)/shard_map/expert_produce/pallas_call | solution.py:845
  382.5 7.0 %all-to-all-done.3.rest_0_.rest_1_.rest_2_.rest_3_ = bf16[4,2,128,512]{3,2,1,0:T(8,128)(2,1)S(1)} async-done(((bf16[4,2,128,512]{3,2,1,0:T(8,128)(2,1)}), bf16[4,2,128,512]{3,2,1,0:T(8,128)(2,1)S(1)}, u32[]{:S(2)}, u32[]{:S(2)}) %all-to-all-start.3) | async-done | bytes 1048608 | tf_op jit(solution)/shard_map/all_to_all | solution.py:1246
  390.5 12.7 %attend_back.2 = (bf16[4,3,128,512]{3,2,1,0:T(8,128)(2,1)}, bf16[48,512]{1,0:T(8,128)(2,1)}) custom-call(s32[1]{0:T(128)} %get-tuple-element.185.len_ref, f32[1,128]{1,0:T(1,128)} %bitcast.176, f32[1,128]{1,0:T(1,128)} %bitcast.180, s32[1,512]{1,0:T(1,128)} %bitcast.162, f32[512,128]{1,0:T(8,128)} %get-tuple-element.187.cos_ref, ...), custom_call_target="tpu_custom_call" | custom-call | flops 13421772 | bytes 146800 | tf_op jit(solution)/shard_map/attend_back/pallas_call | solution.py:494
  406.9 13.3 %attend_back.3 = (bf16[4,3,128,512]{3,2,1,0:T(8,128)(2,1)}, bf16[48,512]{1,0:T(8,128)(2,1)}) custom-call(s32[1]{0:T(128)} %get-tuple-element.186.len_ref, f32[1,128]{1,0:T(1,128)} %bitcast.177, f32[1,128]{1,0:T(1,128)} %bitcast.181, s32[1,512]{1,0:T(1,128)} %bitcast.163, f32[512,128]{1,0:T(8,128)} %get-tuple-element.187.cos_ref, ...), custom_call_target="tpu_custom_call" | custom-call | flops 13421772 | bytes 146800 | tf_op jit(solution)/shard_map/attend_back/pallas_call | solution.py:494
  420.2 23.0 %all-to-all-done.4.rest_0_.rest_1_.rest_2_.rest_3_.rest_4_.rest_5_ = bf16[4,3,128,512]{3,2,1,0:T(8,128)(2,1)S(1)} async-done(((bf16[4,3,128,512]{3,2,1,0:T(8,128)(2,1)}), bf16[4,3,128,512]{3,2,1,0:T(8,128)(2,1)S(1)}, u32[]{:S(2)}, u32[]{:S(2)}) %all-to-all-start.4) | async-done | bytes 1572896 | tf_op jit(solution)/shard_map/all_to_all | solution.py:119
  452.9 31.4 %all-to-all-done.5.rest_0_.rest_1_.rest_2_.rest_3_.rest_6_.rest_7_.rest_8_.rest_9_ = bf16[4,3,128,512]{3,2,1,0:T(8,128)(2,1)} async-done(((bf16[4,3,128,512]{3,2,1,0:T(8,128)(2,1)}), bf16[4,3,128,512]{3,2,1,0:T(8,128)(2,1)}, u32[]{:S(2)}, u32[]{:S(2)}) %all-to-all-start.5) | async-done | bytes 1572896 | tf_op jit(solution)/shard_map/all_to_all | solution.py:119
  499.0 17.6 %project_first_back.1 = f32[2,128,2048]{2,1,0:T(8,128)} custom-call(s32[2]{0:T(128)} %pad_add_fusion.place_ref, bf16[2,48,2048]{2,1,0:T(8,128)(2,1)} %get-tuple-element.146.down_ref, bf16[3,2048,2048]{2,1,0:T(8,128)(2,1)} %w_ref.13, bf16[256,2048]{1,0:T(8,128)(2,1)} %bitcast.136, f32[1,2048]{1,0:T(1,128)} %bitcast.169, ...), custom_call_target="tpu_custom_call" | custom-call | flops 64424508 | bytes 251658 | tf_op jit(solution)/shard_map/project_first_back/pallas_call | solution.py:1037
  538.2 7.0 %collective-permute-done.28 = bf16[256,256]{1,0:T(8,128)(2,1)S(1)} collective-permute-done((bf16[256,256]{1,0:T(8,128)(2,1)S(1)}, bf16[256,256]{1,0:T(8,128)(2,1)S(1)}, u32[]{:S(2)}, u32[]{:S(2)}) %collective-permute-start.28) | collective-permute-done | bytes 131104 | tf_op jit(solution)/shard_map/ppermute | solution.py:109
  (226 shorter events, 138.2 us)
Async XLA Ops:
  7.2 48.3 %all-gather.6.cloned.1.call-start = ((), (), s32[]{:S(2)}) async-start(), calls=%async_computation.10 | async-start | bytes 5234688 | tf_op jit(solution)/shard_map/all_gather | solution.py:1134
  14.0 122.4 %all-gather.4.cloned.1.call-start = ((), (), s32[]{:S(2)}) async-start(), calls=%async_computation.8 | async-start | bytes 9437184 | tf_op jit(solution)/shard_map/all_gather | solution.py:1140
  30.3 46.8 %all-to-all-start = ((bf16[4,3,128,512]{3,2,1,0:T(8,128)(2,1)}), bf16[4,3,128,512]{3,2,1,0:T(8,128)(2,1)S(1)}, u32[]{:S(2)}, u32[]{:S(2)}) async-start(bf16[4,3,128,512]{3,2,1,0:T(8,128)(2,1)} %get-tuple-element.86), calls=%async_computation | async-start | bytes 3145728 | tf_op jit(solution)/shard_map/all_to_all | solution.py:119
  63.6 12.1 %collective-permute-start.1 = (bf16[2,48,128]{2,1,0:T(8,128)(2,1)}, bf16[2,48,128]{2,1,0:T(8,128)(2,1)S(1)}, u32[]{:S(2)}, u32[]{:S(2)}) collective-permute-start(bf16[2,48,128]{2,1,0:T(8,128)(2,1)} %get-tuple-element.87), channel_id=1, source_target_pairs={{0,16},{8,24},{16,0},{24,8},{1,17},{9,25},{17,1},{25,9},{2,18},{10... | collective-permute-start | bytes 73736 | tf_op jit(solution)/shard_map/ppermute | solution.py:109
  77.1 40.9 %all-to-all-start.1 = ((bf16[4,3,128,512]{3,2,1,0:T(8,128)(2,1)}), bf16[4,3,128,512]{3,2,1,0:T(8,128)(2,1)}, u32[]{:S(2)}, u32[]{:S(2)}) async-start(bf16[4,3,128,512]{3,2,1,0:T(8,128)(2,1)} %get-tuple-element.93), calls=%async_computation.1 | async-start | bytes 3145728 | tf_op jit(solution)/shard_map/all_to_all | solution.py:119
  130.1 30.6 %all-to-all-start.2 = ((bf16[4,2,128,512]{3,2,1,0:T(8,128)(2,1)}), bf16[4,2,128,512]{3,2,1,0:T(8,128)(2,1)S(1)}, u32[]{:S(2)}, u32[]{:S(2)}) async-start(bf16[4,2,128,512]{3,2,1,0:T(8,128)(2,1)} %pad_maximum_fusion), calls=%async_computation.2 | async-start | bytes 2097152 | tf_op jit(solution)/shard_map/all_to_all | solution.py:1195
  169.3 15.1 %collective-permute-start.9 = (bf16[128,2048]{1,0:T(8,128)(2,1)}, bf16[128,2048]{1,0:T(8,128)(2,1)S(1)}, u32[]{:S(2)}, u32[]{:S(2)}) collective-permute-start(bf16[128,2048]{1,0:T(8,128)(2,1)} %get-tuple-element.105.rest_0_), channel_id=1, source_target_pairs={{0,4},{1,5},{2,6},{3,7},{4,0},{5,1},{6,2},{7,3},{8,12},{9,13},{10,... | collective-permute-start | bytes 1572872 | tf_op jit(solution)/shard_map/ppermute | solution.py:104
  170.8 15.1 %collective-permute-start.5 = (bf16[128,2048]{1,0:T(8,128)(2,1)}, bf16[128,2048]{1,0:T(8,128)(2,1)S(1)}, u32[]{:S(2)}, u32[]{:S(2)}) collective-permute-start(bf16[128,2048]{1,0:T(8,128)(2,1)} %get-tuple-element.105.rest_0_), channel_id=1, source_target_pairs={{0,2},{1,3},{2,0},{3,1},{4,6},{5,7},{6,4},{7,5},{8,10},{9,11},{10,... | collective-permute-start | bytes 1572872 | tf_op jit(solution)/shard_map/ppermute | solution.py:104
  172.3 13.6 %collective-permute-start.3 = (bf16[128,2048]{1,0:T(8,128)(2,1)}, bf16[128,2048]{1,0:T(8,128)(2,1)S(1)}, u32[]{:S(2)}, u32[]{:S(2)}) collective-permute-start(bf16[128,2048]{1,0:T(8,128)(2,1)} %get-tuple-element.105.rest_0_), channel_id=1, source_target_pairs={{0,1},{1,0},{2,3},{3,2},{4,5},{5,4},{6,7},{7,6},{8,9},{9,8},{10,11... | collective-permute-start | bytes 1572872 | tf_op jit(solution)/shard_map/ppermute | solution.py:104
  172.3 23.3 %collective-permute-start.10 = (bf16[128,2048]{1,0:T(8,128)(2,1)}, bf16[128,2048]{1,0:T(8,128)(2,1)S(1)}, u32[]{:S(2)}, u32[]{:S(2)}) collective-permute-start(bf16[128,2048]{1,0:T(8,128)(2,1)} %get-tuple-element.106.rest_1_), channel_id=1, source_target_pairs={{0,4},{1,5},{2,6},{3,7},{4,0},{5,1},{6,2},{7,3},{8,12},{9,13},{10,... | collective-permute-start | bytes 1572872 | tf_op jit(solution)/shard_map/ppermute | solution.py:104
  172.8 24.3 %collective-permute-start.6 = (bf16[128,2048]{1,0:T(8,128)(2,1)}, bf16[128,2048]{1,0:T(8,128)(2,1)S(1)}, u32[]{:S(2)}, u32[]{:S(2)}) collective-permute-start(bf16[128,2048]{1,0:T(8,128)(2,1)} %get-tuple-element.106.rest_1_), channel_id=1, source_target_pairs={{0,2},{1,3},{2,0},{3,1},{4,6},{5,7},{6,4},{7,5},{8,10},{9,11},{10,... | collective-permute-start | bytes 1572872 | tf_op jit(solution)/shard_map/ppermute | solution.py:104
  184.4 12.7 %collective-permute-start.4 = (bf16[128,2048]{1,0:T(8,128)(2,1)}, bf16[128,2048]{1,0:T(8,128)(2,1)S(1)}, u32[]{:S(2)}, u32[]{:S(2)}) collective-permute-start(bf16[128,2048]{1,0:T(8,128)(2,1)} %get-tuple-element.106.rest_1_), channel_id=1, source_target_pairs={{0,1},{1,0},{2,3},{3,2},{4,5},{5,4},{6,7},{7,6},{8,9},{9,8},{10,11... | collective-permute-start | bytes 1572872 | tf_op jit(solution)/shard_map/ppermute | solution.py:104
  185.9 18.9 %collective-permute-start.13 = (bf16[128,2048]{1,0:T(8,128)(2,1)S(1)}, bf16[128,2048]{1,0:T(8,128)(2,1)S(1)}, u32[]{:S(2)}, u32[]{:S(2)}) collective-permute-start(bf16[128,2048]{1,0:T(8,128)(2,1)S(1)} %collective-permute-done.5.rest_4_), channel_id=1, source_target_pairs={{0,4},{1,5},{2,6},{3,7},{4,0},{5,1},{6,2},{7,3},{8,12},{9,13},{10,... | collective-permute-start | bytes 1572872 | tf_op jit(solution)/shard_map/ppermute | solution.py:104
  311.9 16.3 %collective-permute-start.19 = (bf16[128,2048]{1,0:T(8,128)(2,1)}, bf16[128,2048]{1,0:T(8,128)(2,1)}, u32[]{:S(2)}, u32[]{:S(2)}) collective-permute-start(bf16[128,2048]{1,0:T(8,128)(2,1)} %get-tuple-element.115), channel_id=1, source_target_pairs={{0,2},{1,3},{2,0},{3,1},{4,6},{5,7},{6,4},{7,5},{8,10},{9,11},{10,... | collective-permute-start | bytes 1572872 | tf_op jit(solution)/shard_map/ppermute | solution.py:104
  313.4 15.1 %collective-permute-start.20 = (bf16[128,2048]{1,0:T(8,128)(2,1)}, bf16[128,2048]{1,0:T(8,128)(2,1)}, u32[]{:S(2)}, u32[]{:S(2)}) collective-permute-start(bf16[128,2048]{1,0:T(8,128)(2,1)} %get-tuple-element.116), channel_id=1, source_target_pairs={{0,4},{1,5},{2,6},{3,7},{4,0},{5,1},{6,2},{7,3},{8,12},{9,13},{10,... | collective-permute-start | bytes 1572872 | tf_op jit(solution)/shard_map/ppermute | solution.py:104
  314.4 23.7 %collective-permute-start.18 = (bf16[128,2048]{1,0:T(8,128)(2,1)}, bf16[128,2048]{1,0:T(8,128)(2,1)S(1)}, u32[]{:S(2)}, u32[]{:S(2)}) collective-permute-start(bf16[128,2048]{1,0:T(8,128)(2,1)} %get-tuple-element.113), channel_id=1, source_target_pairs={{0,2},{1,3},{2,0},{3,1},{4,6},{5,7},{6,4},{7,5},{8,10},{9,11},{10,... | collective-permute-start | bytes 1572872 | tf_op jit(solution)/shard_map/ppermute | solution.py:104
  314.9 24.7 %collective-permute-start.22 = (bf16[128,2048]{1,0:T(8,128)(2,1)S(1)}, bf16[128,2048]{1,0:T(8,128)(2,1)S(1)}, u32[]{:S(2)}, u32[]{:S(2)}) collective-permute-start(bf16[128,2048]{1,0:T(8,128)(2,1)S(1)} %get-tuple-element.121), channel_id=1, source_target_pairs={{0,4},{1,5},{2,6},{3,7},{4,0},{5,1},{6,2},{7,3},{8,12},{9,13},{10,... | collective-permute-start | bytes 1572872 | tf_op jit(solution)/shard_map/ppermute | solution.py:104
  330.9 18.0 %collective-permute-start.23 = (bf16[128,2048]{1,0:T(8,128)(2,1)S(1)}, bf16[128,2048]{1,0:T(8,128)(2,1)}, u32[]{:S(2)}, u32[]{:S(2)}) collective-permute-start(bf16[128,2048]{1,0:T(8,128)(2,1)S(1)} %get-tuple-element.163), channel_id=1, source_target_pairs={{0,2},{1,3},{2,0},{3,1},{4,6},{5,7},{6,4},{7,5},{8,10},{9,11},{10,... | collective-permute-start | bytes 1572872 | tf_op jit(solution)/shard_map/ppermute | solution.py:104
  332.1 18.0 %collective-permute-start.21 = (bf16[128,2048]{1,0:T(8,128)(2,1)S(1)}, bf16[128,2048]{1,0:T(8,128)(2,1)}, u32[]{:S(2)}, u32[]{:S(2)}) collective-permute-start(bf16[128,2048]{1,0:T(8,128)(2,1)S(1)} %get-tuple-element.164), channel_id=1, source_target_pairs={{0,4},{1,5},{2,6},{3,7},{4,0},{5,1},{6,2},{7,3},{8,12},{9,13},{10,... | collective-permute-start | bytes 1572872 | tf_op jit(solution)/shard_map/ppermute | solution.py:104
  359.6 29.9 %all-to-all-start.3 = ((bf16[4,2,128,512]{3,2,1,0:T(8,128)(2,1)}), bf16[4,2,128,512]{3,2,1,0:T(8,128)(2,1)S(1)}, u32[]{:S(2)}, u32[]{:S(2)}) async-start(bf16[4,2,128,512]{3,2,1,0:T(8,128)(2,1)} %get-tuple-element.127), calls=%async_computation.3 | async-start | bytes 2097152 | tf_op jit(solution)/shard_map/all_to_all | solution.py:1246
  364.4 132.1 %reduce-scatter.2.cloned.1.call-start = ((), (), s32[]{:S(2)}) async-start(), calls=%async_computation.9 | async-start | bytes 9437184 | tf_op jit(solution)/shard_map/reduce_scatter | solution.py:1264
  403.2 40.0 %all-to-all-start.4 = ((bf16[4,3,128,512]{3,2,1,0:T(8,128)(2,1)}), bf16[4,3,128,512]{3,2,1,0:T(8,128)(2,1)S(1)}, u32[]{:S(2)}, u32[]{:S(2)}) async-start(bf16[4,3,128,512]{3,2,1,0:T(8,128)(2,1)} %get-tuple-element.142), calls=%async_computation.5 | async-start | bytes 3145728 | tf_op jit(solution)/shard_map/all_to_all | solution.py:119
  443.2 41.1 %all-to-all-start.5 = ((bf16[4,3,128,512]{3,2,1,0:T(8,128)(2,1)}), bf16[4,3,128,512]{3,2,1,0:T(8,128)(2,1)}, u32[]{:S(2)}, u32[]{:S(2)}) async-start(bf16[4,3,128,512]{3,2,1,0:T(8,128)(2,1)} %get-tuple-element.150), calls=%async_computation.6 | async-start | bytes 3145728 | tf_op jit(solution)/shard_map/all_to_all | solution.py:119
  492.1 24.5 %all-to-all-start.6 = ((bf16[8,2,128,256]{3,1,2,0:T(2,128)(2,1)}), bf16[8,2,128,256]{3,1,2,0:T(2,128)(2,1)S(1)}, u32[]{:S(2)}, u32[]{:S(2)}) async-start(bf16[8,2,128,256]{3,1,2,0:T(2,128)(2,1)} %copy.48), calls=%async_computation.7 | async-start | bytes 2097152 | tf_op jit(solution)/shard_map/all_to_all | solution.py:1282
  (54 other events, 405.1 us)
Sparse Core Ops, SparseCore 0:
  14.1 41.3 all-gather.5
  57.4 54.3 all-gather.3
  403.3 68.5 reduce-scatter.1
where the time goes:
time: 558 us; the launch traced here: 557 us
  Pallas kernels  256 us (46%)
  waiting for transfers between devices  186 us (33%)
  starting transfers between devices  55.4 us (10%)
  other arithmetic  24.5 us (4%)
  local copies, waits for them, and re-layouts  18.6 us (3%)
  between operations  14.7 us (3%)
    pallas_call x1, Pallas kernels, expert_middle(): kernel_call(body, 'expert_middle', (experts,), [whole_block(meta.shape),...  91.5 us
    all_to_all x4, waiting for transfers between devices, forward_seq(): return lax.all_to_all(pieces, 'seq', 0, 0)  76.2 us
    ppermute x21, waiting for transfers between devices, swap(): return lax.ppermute(values, 'exp', [(i, i ^ mask) for i in range(count)])  52.7 us
    ppermute x9, waiting for transfers between devices, shift(): lax.ppermute(values, 'seq', [(i, (i + distance) % count) for i in range(c...  31.7 us
    pallas_call x2, Pallas kernels, expert_produce(): kernel_call(body, 'expert_produce', (last - first,), [whole_block(meta.sh...  30.3 us
    pallas_call x2, Pallas kernels, attend_back(): kernel_call(body, 'attend_back', (heads,), [whole_block((1, HEAD)), whole...  26 us
    pallas_call x1, Pallas kernels, expert_grad_hidden(): kernel_call(body, 'expert_grad_hidden', (experts,), [whole_block(meta.sha...  24.4 us
    pallas_call x2, Pallas kernels, attend(): kernel_call(body, 'attend', (heads,), [pl.BlockSpec((3, rank, HEAD), lamb...  19.9 us
  transfers between devices with their start and end apart: 40, of which 24 were waited for; matrix products, arithmetic and copies ran while one was open for 4% of the time, Pallas kernels for 24%

commit v1 on v0

--- a/solution.py
+++ b/solution.py
@@ -144,25 +144,58 @@
     return jnp.take(stacked, lax.axis_index("exp") ^ jnp.arange(count), axis=0)
 
 
+STEP_HEADS = 1
+
 WAYS = ((2, 4), (4, 2))
 
 
-def gather_rows(rows):
-    count = lax.axis_size("exp")
-    if count != 8 or len(rows) != 2:
-        everything = by_relative(lax.all_gather(jnp.concatenate(rows), "exp"))
-        return [[everything[m]] for m in range(count)]
-    near = {2: [None, None], 4: [None, None], 6: [None, None]}
+def gather_near(rows):
+    near = {2: [None] * len(rows), 4: [None] * len(rows)}
     for g, (first, _) in enumerate(WAYS):
         near[first][g] = swap(rows[g], first)
     for g, (_, second) in enumerate(WAYS):
         near[second][g] = swap(rows[g], second)
-    for g, (first, second) in enumerate(WAYS):
-        near[6][g] = swap(near[first][g], second)
-    found = [list(rows), [swap(block, 1) for block in rows]]
-    for m in (2, 4, 6):
-        found += [near[m], [swap(block, 1) for block in near[m]]]
+    return near
+
+
+def far_of(near):
+    return [swap(near[first][g], second) for g, (first, second) in enumerate(WAYS)]
+
+
+def gather_far(rows, near, far=None):
+    far = far or far_of(near)
+    found = []
+    for blocks in (rows, near[2], near[4], far):
+        found += [list(blocks), [swap(block, 1) for block in blocks]]
     return found
+
+
+def gather_whole(rows):
+    everything = by_relative(lax.all_gather(jnp.concatenate(rows), "exp"))
+    return [[block] for block in everything]
+
+
+def near_sums_of(parts, others):
+    groups = len(parts[0])
+    beside = swap(others, 1).reshape((4, groups) + parts[0][0].shape)
+    far = [add_low(parts[6][g], beside[3][g]) for g in range(groups)]
+    near = [add_low(parts[WAYS[g][0]][g], beside[WAYS[g][0] // 2][g]) for g in range(groups)]
+    return lax.optimization_barrier((far, near)) + (beside,)
+
+
+def send_near(far, near):
+    far = [swap(far[g], WAYS[g][0]) for g in range(len(far))]
+    return far, [swap(near[g], WAYS[g][0]) for g in range(len(near))]
+
+
+def joined_sums_of(parts, beside, far):
+    return [
+        add_low(parts[WAYS[g][1]][g], beside[WAYS[g][1] // 2][g], far[g]) for g in range(len(far))
+    ]
+
+
+def send_joined(joined):
+    return [swap(joined[g], WAYS[g][1]) for g in range(len(joined))]
 
 
 def add_low(*values):
@@ -300,51 +333,49 @@
     return outs, result[total], result[total + 1]
 
 
-def pick_sets(gathered, picks, groups, sets, sections, normed=None):
-    count, _, part = gathered.shape
+def pick_sets(gathered, picks, groups, sections, normed):
+    count = len(gathered)
+    part = gathered[0].shape[1]
     width = count * part
-    shard = normed.shape[0] // groups if normed is not None else 0
+    shard = normed.shape[0] // groups
     number = len(sections)
 
-    def body(pick_ref, in_ref, *rest):
-        normed_ref = rest[0] if shard else None
-        outs = rest[1:] if shard else rest
-        outs, sem = outs[:-1], outs[-1]
+    def body(pick_ref, normed_ref, *rest):
+        refs, outs, sem = rest[:count], rest[count:-1], rest[-1]
         copies = []
         for g in range(groups):
             for i, (first, own) in enumerate(sections):
-                for e in range(count):
+                for m in range(count):
+                    columns = pl.ds(pl.multiple_of((pick_ref[groups] ^ m) * part, part), part)
                     copies.append(
                         pltpu.make_async_copy(
-                            in_ref.at[e, pl.ds(pl.multiple_of(first + pick_ref[g] * own, own), own)],
-                            outs[i].at[g, :, pl.ds(e * part, part)],
-                            sem.at[(g * number + i) * count + e],
+                            refs[m].at[pl.ds(pl.multiple_of(first + pick_ref[g] * own, own), own)],
+                            outs[i].at[g, :, columns],
+                            sem.at[(g * number + i) * count + m],
                         )
                     )
         for copy in copies:
             copy.start()
         for copy in copies:
             copy.wait()
-        if shard:
-            for g in range(groups):
-                outs[number][g] = dot_nt(
-                    outs[0][g], normed_ref[g * shard : (g + 1) * shard]
-                ).astype(BF16)
+        for g in range(groups):
+            outs[number][g] = dot_nt(
+                outs[0][g], normed_ref[g * shard : (g + 1) * shard]
+            ).astype(BF16)
 
     shapes = [(groups, own, width) for _, own in sections]
-    if shard:
-        shapes.append((groups, sections[0][1], shard))
+    shapes.append((groups, sections[0][1], shard))
     return kernel_call(
         body,
         "pick_sets",
         (1,),
-        [ANYWHERE] + ([whole_block(normed.shape)] if shard else []),
+        [whole_block(normed.shape)] + [ANYWHERE] * count,
         [whole_block(shape) for shape in shapes],
         [shape_of(shape, BF16) for shape in shapes],
         scratch=[pltpu.SemaphoreType.DMA((groups * number * count,))],
         prefetch=1,
         moved=4 * groups * width * sum(own for _, own in sections),
-    )(picks, gathered, *([normed] if shard else []))
+    )(picks, normed, *gathered)
 
 
 def route(ids, gates, choice, experts):
@@ -401,50 +432,59 @@
     rank = ups.shape[1]
     total = splits * shard
     heads = part // HEAD
+    step_heads = min(heads, STEP_HEADS)
 
     def body(len_ref, up_ref, qg_ref, kg_ref, pos_ref, cos_ref, sin_ref, *rest):
         raw_refs, mid_ref = rest[:splits], rest[splits]
         att_refs = out_refs_of(listed, rest[splits + 1 : -5])
         q_ref, k_ref, v_ref, rq_ref, rk_ref = rest[-5:]
 
-        def full(which):
-            base = jnp.concatenate([ref[which] for ref in raw_refs], axis=0).astype(F32)
-            mid = jnp.concatenate(
+        mids = [
+            jnp.concatenate(
                 [mid_ref[r, which * rank : (which + 1) * rank] for r in range(splits)], axis=1
             )
-            return base + ADAPTER_SCALE * dot_tn(mid, up_ref[which])
-
-        raw_q, raw_k, raw_v = full(0), full(1), full(2)
-        rq_ref[0] = raw_q
-        rk_ref[0] = raw_k
+            for which in range(3)
+        ]
         cosine, sine = cos_ref[...], sin_ref[...]
-        queries = rotate(raw_q * inverse_rms(raw_q) * qg_ref[...], cosine, sine).astype(BF16)
-        keys = rotate(raw_k * inverse_rms(raw_k) * kg_ref[...], cosine, sine).astype(BF16)
-        values = raw_v.astype(BF16)
-        q_ref[0] = queries
-        k_ref[0] = keys
-        v_ref[0] = values
-        weights = softmax_rows(queries, keys, pos_ref[...] < len_ref[0]).astype(BF16)
-        result = dot_nn(weights, values).astype(BF16)
-        for r in range(splits):
-            att_refs[r][...] = result[r * shard : (r + 1) * shard]
-
-    head_block = pl.BlockSpec((1, total, HEAD), lambda h, s: (h, 0, 0))
+        for h in range(step_heads):
+            at = slice(h * HEAD, (h + 1) * HEAD)
+
+            def full(which):
+                base = jnp.concatenate([ref[which, :, at] for ref in raw_refs], axis=0)
+                added = dot_tn(mids[which], up_ref[which, :, at])
+                return base.astype(F32) + ADAPTER_SCALE * added
+
+            raw_q, raw_k, raw_v = full(0), full(1), full(2)
+            rq_ref[h] = raw_q
+            rk_ref[h] = raw_k
+            queries = rotate(raw_q * inverse_rms(raw_q) * qg_ref[...], cosine, sine).astype(BF16)
+            keys = rotate(raw_k * inverse_rms(raw_k) * kg_ref[...], cosine, sine).astype(BF16)
+            values = raw_v.astype(BF16)
+            q_ref[h] = queries
+            k_ref[h] = keys
+            v_ref[h] = values
+            weights = softmax_rows(queries, keys, pos_ref[...] < len_ref[0]).astype(BF16)
+            result = dot_nn(weights, values).astype(BF16)
+            for r in range(splits):
+                att_refs[r][:, at] = result[r * shard : (r + 1) * shard]
+
+    wide = step_heads * HEAD
+    head_block = pl.BlockSpec((step_heads, total, HEAD), lambda h, s: (h, 0, 0))
     result = kernel_call(
         body,
         "attend",
-        (heads,),
+        (heads // step_heads,),
         [
-            pl.BlockSpec((3, rank, HEAD), lambda h, s: (0, 0, h)),
+            pl.BlockSpec((3, rank, wide), lambda h, s: (0, 0, h)),
             whole_block((1, HEAD)),
             whole_block((1, HEAD)),
             whole_block((1, total)),
             whole_block((total, HEAD)),
             whole_block((total, HEAD)),
         ]
-        + piece_specs(raw, (3, shard, HEAD), lambda h, s: (0, 0, h))
+        + piece_specs(raw, (3, shard, wide), lambda h, s: (0, 0, h))
         + [whole_block(mids.shape)],
-        out_specs_of(listed, splits, (shard, HEAD), lambda h, s: (0, h)) + [head_block] * 5,
+        out_specs_of(listed, splits, (shard, wide), lambda h, s: (0, h)) + [head_block] * 5,
         out_shapes_of(listed, splits, (shard, part), BF16)
         + [shape_of((heads, total, HEAD), BF16)] * 3
         + [shape_of((heads, total, HEAD), F32)] * 2,
@@ -460,41 +500,47 @@
     splits, _, shard, part = grads.shape
     total = splits * shard
     heads = part // HEAD
+    step_heads = min(heads, STEP_HEADS)
 
     def body(len_ref, qg_ref, kg_ref, pos_ref, cos_ref, sin_ref, *rest):
         grad_refs, mid_ref = rest[:splits], rest[splits]
         q_ref, k_ref, v_ref, rq_ref, rk_ref = rest[splits + 1 : splits + 6]
         out_refs = out_refs_of(listed, rest[splits + 6 : -1])
         gup_ref = rest[-1]
-        queries, keys, values = q_ref[0], k_ref[0], v_ref[0]
-        grad = jnp.concatenate([ref[...] for ref in grad_refs], axis=0)
-        weights = softmax_rows(queries, keys, pos_ref[...] < len_ref[0])
-        grad_probs = dot_nt(grad, values)
-        inner = jnp.sum(weights * grad_probs, axis=-1, keepdims=True)
-        grad_scores = (weights * (grad_probs - inner)).astype(BF16)
-        grad_q = dot_nn(grad_scores, keys) * SCORE_SCALE
-        grad_k = dot_tn(grad_scores, queries) * SCORE_SCALE
-        grad_v = dot_tn(weights.astype(BF16), grad)
         cosine, sine = cos_ref[...], sin_ref[...]
-        grad_q = norm_back(rq_ref[0], qg_ref[...], rotate_back(grad_q, cosine, sine))
-        grad_k = norm_back(rk_ref[0], kg_ref[...], rotate_back(grad_k, cosine, sine))
-
-        for which, value in enumerate((grad_q, grad_k, grad_v)):
-            low = value.astype(BF16)
-            for r in range(splits):
-                out_refs[r][which] = low[r * shard : (r + 1) * shard]
-            mid = jnp.concatenate(
+        mids = [
+            jnp.concatenate(
                 [mid_ref[r, which * rank : (which + 1) * rank] for r in range(splits)], axis=1
             )
-            gup_ref[which * rank : (which + 1) * rank] = (
-                ADAPTER_SCALE * dot_nn(mid, low)
-            ).astype(BF16)
-
-    head_block = pl.BlockSpec((1, total, HEAD), lambda h, s: (h, 0, 0))
+            for which in range(3)
+        ]
+        for h in range(step_heads):
+            at = slice(h * HEAD, (h + 1) * HEAD)
+            queries, keys, values = q_ref[h], k_ref[h], v_ref[h]
+            grad = jnp.concatenate([ref[:, at] for ref in grad_refs], axis=0)
+            weights = softmax_rows(queries, keys, pos_ref[...] < len_ref[0])
+            grad_probs = dot_nt(grad, values)
+            inner = jnp.sum(weights * grad_probs, axis=-1, keepdims=True)
+            grad_scores = (weights * (grad_probs - inner)).astype(BF16)
+            grad_q = dot_nn(grad_scores, keys) * SCORE_SCALE
+            grad_k = dot_tn(grad_scores, queries) * SCORE_SCALE
+            grad_v = dot_tn(weights.astype(BF16), grad)
+            grad_q = norm_back(rq_ref[h], qg_ref[...], rotate_back(grad_q, cosine, sine))
+            grad_k = norm_back(rk_ref[h], kg_ref[...], rotate_back(grad_k, cosine, sine))
+            for which, value in enumerate((grad_q, grad_k, grad_v)):
+                low = value.astype(BF16)
+                for r in range(splits):
+                    out_refs[r][which, :, at] = low[r * shard : (r + 1) * shard]
+                gup_ref[which * rank : (which + 1) * rank, at] = (
+                    ADAPTER_SCALE * dot_nn(mids[which], low)
+                ).astype(BF16)
+
+    wide = step_heads * HEAD
+    head_block = pl.BlockSpec((step_heads, total, HEAD), lambda h, s: (h, 0, 0))
     result = kernel_call(
         body,
         "attend_back",
-        (heads,),
+        (heads // step_heads,),
         [
             whole_block((1, HEAD)),
             whole_block((1, HEAD)),
@@ -503,13 +549,13 @@
             whole_block((total, HEAD)),
         ]
         + [
-            pl.BlockSpec((None, None, shard, HEAD), lambda h, s, r=r: (r, group, 0, h))
+            pl.BlockSpec((None, None, shard, wide), lambda h, s, r=r: (r, group, 0, h))
             for r in range(splits)
         ]
         + [whole_block(mids.shape)]
         + [head_block] * 5,
-        out_specs_of(listed, splits, (3, shard, HEAD), lambda h, s: (0, 0, h))
-        + [pl.BlockSpec((3 * rank, HEAD), lambda h, s: (0, h))],
+        out_specs_of(listed, splits, (3, shard, wide), lambda h, s: (0, 0, h))
+        + [pl.BlockSpec((3 * rank, wide), lambda h, s: (0, h))],
         out_shapes_of(listed, splits, (3, shard, part), BF16)
         + [shape_of((3 * rank, part), BF16)],
         prefetch=1,
@@ -634,22 +680,23 @@
                 copy.start()
 
 
-def expert_grad_hidden(place, gathered, meta, expert_down, capacity, begin, end):
-    _, hidden, width = expert_down.shape
-    experts = end - begin
+def expert_grad_hidden(gathered, meta, expert_down, capacity):
+    experts, hidden, width = expert_down.shape
+    numbers = [len(found) for found in gathered]
+    arrays = [array for found in gathered for array in found]
     count = meta.shape[0]
     tokens = meta.shape[-1]
     rows = count * capacity
 
-    def body(place_ref, meta_ref, w_ref, rows_ref, *rest):
-        out_ref, ring, picked, sem = rest[-4:]
+    def body(meta_ref, w_ref, *rest):
+        refs, (out_ref, ring, picked, sem) = rest[: len(arrays)], rest[len(arrays) :]
         expert = pl.program_id(0)
 
         @pl.when(expert == 0)
         def _():
             pick_rows(
-                lambda m: [rows_ref.at[place_ref[1] ^ m]],
-                meta_ref, ring, sem, picked, capacity, True, begin,
+                lambda m: refs[sum(numbers[:m]) : sum(numbers[: m + 1])],
+                meta_ref, ring, sem, picked, capacity, True,
             )
 
         out_ref[0] = dot_nt(picked[expert], w_ref[0]).astype(BF16)
@@ -660,20 +707,19 @@
         (experts,),
         [
             whole_block(meta.shape),
-            pl.BlockSpec((1, hidden, width), lambda e, s: (e + begin, 0, 0)),
-            ANYWHERE,
-        ],
-        pl.BlockSpec((1, rows, hidden), lambda e, s: (e, 0, 0)),
+            pl.BlockSpec((1, hidden, width), lambda e: (e, 0, 0)),
+        ]
+        + [ANYWHERE] * len(arrays),
+        pl.BlockSpec((1, rows, hidden), lambda e: (e, 0, 0)),
         shape_of((experts, rows, hidden), BF16),
         scratch=[
             pltpu.VMEM((4, tokens, width), BF16),
             pltpu.VMEM((experts, rows, width), BF16),
-            pltpu.SemaphoreType.DMA((count, 1)),
+            pltpu.SemaphoreType.DMA((count, max(numbers))),
         ],
-        prefetch=1,
         flops=2 * experts * rows * (hidden + tokens) * width,
         moved=2 * experts * hidden * width + 2 * count * tokens * width,
-    )(place, meta, expert_down, gathered)
+    )(meta, expert_down, *arrays)
 
 
 def combine_rows(meta_ref, picked, m, capacity):
@@ -712,6 +758,27 @@
             copy.wait()
 
 
+def sum_shapes(count, tokens, width, groups, paired):
+    if not paired:
+        return [shape_of((count, tokens, width), BF16)]
+    one = shape_of((tokens // groups, width), BF16)
+    return [one] * (count // 2 * groups) + [shape_of((count // 2, tokens, width), BF16)]
+
+
+def sum_targets(outs, place_ref, m, groups, paired):
+    if not paired:
+        return [outs[0].at[place_ref[1] ^ m]]
+    if m % 2:
+        return [outs[-1].at[m // 2]]
+    return outs[m // 2 * groups : (m // 2 + 1) * groups]
+
+
+def sums_of(result, count, groups, paired):
+    if not paired:
+        return result[0], None
+    return {m: result[m // 2 * groups : (m // 2 + 1) * groups] for m in range(0, count, 2)}, result[-1]
+
+
 def expert_middle(
     place, gathered, meta, expert_gate, expert_up, grad_hidden, capacity, groups, paired
 ):
@@ -722,7 +789,6 @@
     chunk = 256 if rows % 256 == 0 else rows
     numbers = [len(found) for found in gathered]
     arrays = [array for found in gathered for array in found]
-    even = [m for m in range(count) if m % 2 == 0]
 
     def body(place_ref, meta_ref, gate_ref, up_ref, gh_ref, *rest):
         refs, (h_ref, *outs) = rest[: len(arrays)], rest[len(arrays) : -5]
@@ -753,20 +819,12 @@
 
         @pl.when(expert == experts - 1)
         def _():
-            def targets(m):
-                if not paired:
-                    return [outs[0].at[place_ref[1] ^ m]]
-                if m % 2:
-                    return [outs[-1].at[m // 2]]
-                return outs[m // 2 * groups : (m // 2 + 1) * groups]
-
-            send_combined(meta_ref, made, ring, out_sem, capacity, targets)
-
-    if paired:
-        shapes = [shape_of((tokens // groups, width), BF16)] * (len(even) * groups)
-        shapes.append(shape_of((count // 2, tokens, width), BF16))
-    else:
-        shapes = [shape_of((count, tokens, width), BF16)]
+            send_combined(
+                meta_ref, made, ring, out_sem, capacity,
+                lambda m: sum_targets(outs, place_ref, m, groups, paired),
+            )
+
+    shapes = sum_shapes(count, tokens, width, groups, paired)
     result = kernel_call(
         body,
         "expert_middle",
@@ -791,13 +849,12 @@
         flops=2 * experts * rows * (4 * hidden + tokens) * width,
         moved=4 * experts * hidden * width + 4 * experts * rows * width,
     )(place, meta, expert_gate, expert_up, grad_hidden, *arrays)
-    if not paired:
-        return result[0], result[1], None
-    near = {m: result[1 + i * groups : 1 + (i + 1) * groups] for i, m in enumerate(even)}
-    return result[0], near, result[-1]
-
-
-def expert_produce(place, hidden_rows, meta, expert_down, capacity, first, last, before=None):
+    return (result[0],) + sums_of(result[1:], count, groups, paired)
+
+
+def expert_produce(
+    place, hidden_rows, meta, expert_down, capacity, first, last, groups, paired, before=None
+):
     experts, hidden, width = expert_down.shape
     count = meta.shape[0]
     tokens = meta.shape[-1]
@@ -808,7 +865,7 @@
         expert = pl.program_id(0) + first
         result = dot_nn(h_ref[0], w_ref[0])
         if held:
-            before_ref, out_ref, ring, made, sem, before_sem = rest
+            before_ref, outs, (ring, made, sem, before_sem) = rest[0], rest[1:-4], rest[-4:]
             copy = pltpu.make_async_copy(before_ref, made.at[pl.ds(0, held)], before_sem)
 
             @pl.when(expert == first)
@@ -835,14 +892,17 @@
             def _():
                 copy.wait()
                 send_combined(
-                    meta_ref, made, ring, sem, capacity, lambda m: [out_ref.at[place_ref[1] ^ m]]
+                    meta_ref, made, ring, sem, capacity,
+                    lambda m: sum_targets(outs, place_ref, m, groups, paired),
                 )
 
-    out_spec, shape = ANYWHERE, shape_of((count, tokens, width), BF16)
-    if not held:
-        out_spec = pl.BlockSpec((1, rows, width), lambda e, s: (e, 0, 0))
-        shape = shape_of((last - first, rows, width), BF16)
-    return kernel_call(
+    if held:
+        shapes = sum_shapes(count, tokens, width, groups, paired)
+        out_specs = [ANYWHERE] * len(shapes)
+    else:
+        shapes = [shape_of((last - first, rows, width), BF16)]
+        out_specs = [pl.BlockSpec((1, rows, width), lambda e, s: (e, 0, 0))]
+    result = kernel_call(
         body,
         "expert_produce",
         (last - first,),
@@ -852,12 +912,12 @@
             pl.BlockSpec((1, hidden, width), lambda e, s: (e + first, 0, 0)),
         ]
         + ([ANYWHERE] if held else []),
-        out_spec,
-        shape,
+        out_specs,
+        shapes,
         scratch=[
             pltpu.VMEM((2, tokens, width), BF16),
             pltpu.VMEM((experts, rows, width), BF16),
-            pltpu.SemaphoreType.DMA((2, 1)),
+            pltpu.SemaphoreType.DMA((2, groups)),
             pltpu.SemaphoreType.DMA,
         ]
         if held
@@ -866,6 +926,7 @@
         flops=2 * (last - first) * rows * hidden * width,
         moved=2 * experts * hidden * width + 2 * experts * rows * width,
     )(place, meta, hidden_rows, expert_down, *([before] if held else []))
+    return sums_of(result, count, groups, paired) if held else result[0]
 
 
 def project_out_back(pieces, mixed, upstream, gain, w_out, down, up, attended, mids):
@@ -946,16 +1007,17 @@
     )
 
 
-def adapter_grads(place, group, grads, normed, ups, devices):
+def adapter_grads(place, group, grads, normed, ups, into):
     listed = is_list(grads)
     splits, (_, shard, part) = piece_shape(grads)
     width = splits * part
     own = ups.shape[1]
+    devices = into.shape[0]
     rank = own // 3
     slice_width = width // devices
 
     def body(place_ref, normed_ref, up_ref, *rest):
-        refs, (small_ref, down_ref, low) = rest[:splits], rest[splits:]
+        refs, (_, small_ref, down_ref, low) = rest[:splits], rest[splits:]
         for which in range(3):
             for r in range(splits):
                 owner = lax.rem(place_ref[0] + r, splits) if listed else r
@@ -975,96 +1037,78 @@
             pl.BlockSpec((shard, width), lambda i, s: (group, 0)),
             group_block(ups.shape, group),
         ]
-        + piece_specs(grads, (3, shard, part), lambda i, s: (0, 0, 0)),
-        [whole_block((own, shard)), whole_block((devices, own, slice_width))],
-        [shape_of((own, shard), BF16), shape_of((devices, own, slice_width), BF16)],
+        + piece_specs(grads, (3, shard, part), lambda i, s: (0, 0, 0))
+        + [ANYWHERE],
+        [
+            whole_block((own, shard)),
+            pl.BlockSpec((devices, None, own, slice_width), lambda i, s: (0, group, 0, 0)),
+        ],
+        [shape_of((own, shard), BF16), shape_of(into.shape, BF16)],
         scratch=[pltpu.VMEM((shard, width), BF16)],
         prefetch=1,
+        aliases={3 + splits: 1},
         flops=12 * shard * rank * width,
         moved=6 * shard * width,
-    )(place, normed, ups, *piece_arrays(grads, splits))
-
-
-def project_first_back(place, grads, smalls, downs, w_qkv, tokens, gain, grad_mixed):
-    groups = len(grads)
-    listed = [is_list(pieces) for pieces in grads]
-    splits, (_, shard, part) = piece_shape(grads[0])
+    )(place, normed, ups, *piece_arrays(grads, splits), into)
+
+
+def project_first_back(group, grads, smalls, downs, w_qkv, tokens, gain, grad_mixed, into=None):
+    splits, _, shard, part = grads.shape
     width = splits * part
-    rows = groups * shard
-
     rank = downs.shape[1] // 3
-
-    def body(place_ref, down_ref, w_ref, tok_ref, gain_ref, mixed_ref, *rest):
-        small_refs, refs = rest[:groups], rest[groups : groups + groups * splits]
-        out_ref, low, total, held, sem = rest[groups + groups * splits :]
-        which = pl.program_id(0)
-
-        def copy(p):
-            return pltpu.make_async_copy(w_ref.at[p], held.at[p], sem.at[p])
-
-        @pl.when(which == 0)
-        def _():
-            for p in range(3):
-                copy(p).start()
-
-        for g in range(groups):
-            for r in range(splits):
-                owner = lax.rem(place_ref[0] + r, splits) if listed[g] else r
-                low[
-                    g * shard : (g + 1) * shard, pl.ds(pl.multiple_of(owner * part, part), part)
-                ] = refs[g * splits + r][0]
-        at = pl.ds(pl.multiple_of(which * rank, rank), rank)
-        small = jnp.concatenate(
-            [dot_tn(small_refs[g][at], down_ref[g, at]) for g in range(groups)], axis=0
-        )
-        copy(which).wait()
-        result = dot_nt(low[...], held[which]) + small
-
-        @pl.when(which == 0)
-        def _():
-            total[...] = result
-
-        @pl.when(which == 1)
-        def _():
-            total[...] += result
-
-        @pl.when(which == 2)
-        def _():
-            back = norm_back(tok_ref[...].astype(F32), gain_ref[...], total[...] + result)
-            for g in range(groups):
-                out_ref[g] = mixed_ref[g] + back[g * shard : (g + 1) * shard]
+    groups = tokens.shape[0]
+
+    def body(down_ref, w_ref, tok_ref, gain_ref, mixed_ref, small_ref, grad_ref, *rest):
+        out_ref, low, held, sem = rest[-4:]
+
+        def copy(p, i):
+            at = pl.ds(i * part, part)
+            return pltpu.make_async_copy(w_ref.at[p, at], held.at[p, at], sem.at[p, i])
+
+        for p in range(3):
+            for i in range(splits):
+                copy(p, i).start()
+        totals = [None] * splits
+        for p in range(3):
+            for z in range(splits):
+                low[:, z * part : (z + 1) * part] = grad_ref[z, p]
+            at = slice(p * rank, (p + 1) * rank)
+            small = dot_tn(small_ref[at], down_ref[at])
+            for i in range(splits):
+                copy(p, i).wait()
+                columns = slice(i * part, (i + 1) * part)
+                result = dot_nt(low[...], held[p, columns]) + small[:, columns]
+                totals[i] = result if p == 0 else totals[i] + result
+        total = jnp.concatenate(totals, axis=1)
+        out_ref[...] = mixed_ref[...] + norm_back(tok_ref[...].astype(F32), gain_ref[...], total)
 
     return kernel_call(
         body,
         "project_first_back",
-        (3,),
+        (1,),
         [
-            whole_block(downs.shape),
+            group_block(downs.shape, group),
             ANYWHERE,
-            whole_block((rows, width)),
+            group_block(tokens.shape, group),
             whole_block((1, width)),
-            whole_block(grad_mixed.shape),
-        ]
-        + [whole_block((3 * rank, shard))] * groups
-        + [
-            spec
-            for pieces in grads
-            for spec in piece_specs(pieces, (1, shard, part), lambda p, s: (p, 0, 0))
-        ],
-        whole_block((groups, shard, width)),
+            group_block(grad_mixed.shape, group),
+            whole_block((3 * rank, shard)),
+            whole_block(grads.shape),
+        ]
+        + ([ANYWHERE] if into is not None else []),
+        pl.BlockSpec((None, shard, width), lambda i: (group, 0, 0)),
         shape_of((groups, shard, width), F32),
         scratch=[
-            pltpu.VMEM((rows, width), BF16),
-            pltpu.VMEM((rows, width), F32),
+            pltpu.VMEM((shard, width), BF16),
             pltpu.VMEM((3, width, width), BF16),
-            pltpu.SemaphoreType.DMA((3,)),
+            pltpu.SemaphoreType.DMA((3, splits)),
         ],
-        prefetch=1,
-        flops=6 * rows * width * width,
+        aliases={7: 0} if into is not None else None,
+        flops=6 * shard * width * width,
         moved=6 * width * width,
     )(
-        place, downs, w_qkv, tokens, gain, grad_mixed, *smalls,
-        *[piece for pieces in grads for piece in piece_arrays(pieces, splits)],
+        downs, w_qkv, tokens, gain, grad_mixed, smalls, grads,
+        *([into] if into is not None else []),
     )
 
 
@@ -1113,60 +1157,64 @@
     query_row = query_gain.reshape(1, HEAD)
     key_row = key_gain.reshape(1, HEAD)
 
+    paired = devices == 8 and groups == 2
     own_positions = here * shard + jnp.arange(shard, dtype=jnp.int32)
     own_live = own_positions[None, :] < lengths[:, None]
-    upstream = jnp.where(own_live[:, :, None], cotangent, jnp.zeros((), BF16))
-    ids = expert_ids.reshape(rows, top).T
-    gates = gate_weights.reshape(rows, top).T
+
+    base, _, normed = project_first(
+        place, flat_tokens, gain_row, w_qkv, groups, splits, listed
+    )
+    raw = [forward_seq(base[0])]
+
+    adapt_down_low, adapt_up_low, ids, gates = after(
+        (adapt_down, adapt_up, expert_ids, gate_weights), normed
+    )
+    ids = ids.reshape(rows, top).T
+    gates = gates.reshape(rows, top).T
     choice = adapter_choice.astype(F32).reshape(1, groups * sets)
     choice = jnp.pad(choice, ((0, 0), (0, rows - groups * sets)))
     routed = route(ids, gates, choice, experts)
-    down_rows = jnp.swapaxes(adapt_down.astype(BF16), 2, 3)
-    adapter_rows = jnp.concatenate(
-        [
-            down_rows[:, :3].reshape(-1, slice_width),
-            down_rows[:, 3].reshape(-1, slice_width),
-            adapt_up[:, :3].astype(BF16).reshape(-1, slice_width),
-            adapt_up[:, 3].astype(BF16).reshape(-1, slice_width),
-            routed.reshape(-1, slice_width),
-        ]
-    )
-    all_adapters = lax.all_gather(adapter_rows, "exp")
-
-    base, _, normed = project_first(
-        place, after(flat_tokens, adapter_rows), gain_row, w_qkv, groups, splits, listed
-    )
-    raw = [forward_seq(base[0])]
-    cot_rows = lax.all_gather(after(upstream, normed).reshape(rows, width), "exp")
-
+    down_rows = jnp.swapaxes(adapt_down_low.astype(BF16), 2, 3)
+    up_rows = adapt_up_low.astype(BF16)
     own = 3 * rank
+    blocks = [
+        jnp.concatenate([found.reshape(-1, slice_width) for found in sources])
+        for sources in (
+            (down_rows[:, :3], down_rows[:, 3], routed),
+            (up_rows[:, :3], up_rows[:, 3]),
+        )
+    ]
+    if paired:
+        all_blocks = gather_far(blocks, gather_near(blocks))
+        all_downs, all_ups = ([found[g] for found in all_blocks] for g in range(2))
+    else:
+        cut = blocks[0].shape[0]
+        all_downs = [found[0][:cut] for found in gather_whole(blocks)]
+        all_ups = [found[0][cut:] for found in gather_whole(blocks)]
     chosen = jnp.sum(adapter_choice * jnp.arange(sets, dtype=jnp.int32)[None, :], axis=1)
-    sections = [
-        (0, own), (sets * own, rank), (sets * (own + rank), own), (sets * (2 * own + rank), rank),
-    ]
-    downs, out_downs, ups, out_ups, mids = pick_sets(
-        all_adapters, chosen, groups, sets, sections, normed
-    )
+    picks = jnp.concatenate([chosen, position.reshape(1)]).astype(jnp.int32)
+    sections = [(0, own), (sets * own, rank)]
+    downs, out_downs, mids = pick_sets(all_downs, picks, groups, sections, normed)
+    ups, out_ups, _ = pick_sets(after(all_ups, mids), picks, groups, sections, normed)
     all_mids = by_distance(jnp.stack(forward_seq([mids] * splits)))
-    raw[0], all_mids = lax.optimization_barrier((raw[0], all_mids))
-    for g in range(1, groups):
-        raw.append(forward_seq(after(base[g], raw[g - 1])))
-    gathered = after(all_adapters, raw[0])[:, 2 * sets * projections * rank :]
-    gathered = gathered.reshape(devices, 3 * experts + 16, rows)
-    choices = gathered[:, 3 * experts, : groups * sets].reshape(devices, groups, sets)
-    meta = gathered[:, : 3 * experts].reshape(devices, 3, experts, rows)
+
+    live_rows = after(own_live, mids)
+    upstream = jnp.where(live_rows[:, :, None], cotangent, jnp.zeros((), BF16))
+    upstream = [upstream[g] for g in range(groups)]
+    routes = jnp.stack([found[sets * (own + rank) :] for found in after(all_downs, mids)])
+    routes = routes.reshape(devices, 3 * experts + 16, rows)
+    choices = by_relative(routes[:, 3 * experts, : groups * sets])
+    choices = choices.reshape(devices, groups, sets)
+    meta = routes[:, : 3 * experts].reshape(devices, 3, experts, rows)
     meta = lax.dynamic_slice_in_dim(meta, position * local_experts, local_experts, axis=2)
     meta = meta.astype(F32)
-    meta = by_relative(jnp.stack([meta[:, 0], meta[:, 1] + meta[:, 2]], axis=1))
-    own_ups = lax.dynamic_slice_in_dim(ups, here * part, part, axis=2)
-    own_ups = own_ups.reshape(groups, 3, rank, part)
-
+    meta = jnp.stack([meta[:, 0], meta[:, 1] + meta[:, 2]], axis=1)
     blocks = jnp.arange(splits, dtype=jnp.int32)
     frequency = ROPE_BASE ** (-(2.0 / HEAD) * jnp.arange(HEAD // 2, dtype=F32))
     tables = []
     for g in range(groups):
         positions = blocks[:, None] * shard + jnp.arange(shard, dtype=jnp.int32)[None, :]
-        angles = after(positions, raw[0]).reshape(total, 1).astype(F32) * frequency[None, :]
+        angles = after(positions, normed).reshape(total, 1).astype(F32) * frequency[None, :]
         cosine, sine = jnp.cos(angles), jnp.sin(angles)
         tables.append(
             (
@@ -1175,6 +1223,14 @@
                 jnp.concatenate([-sine, sine], axis=1),
             )
         )
+
+    raw[0], all_mids, meta, choices, tables = lax.optimization_barrier(
+        (raw[0], all_mids, meta, choices, tables)
+    )
+    for g in range(1, groups):
+        raw.append(forward_seq(after(base[g], raw[g - 1])))
+    own_ups = lax.dynamic_slice_in_dim(ups, here * part, part, axis=2)
+    own_ups = own_ups.reshape(groups, 3, rank, part)
 
     saved, heads_rows = [], []
     for g in range(groups):
@@ -1191,19 +1247,26 @@
         )
         saved.append(kept)
         heads_rows.append(att)
+        if paired and g == 0:
+            near = gather_near(upstream)
+            far = far_of(after(near, att))
+            cot_rows = gather_far(upstream, near, far)
+    if not paired:
+        cot_rows = gather_whole(upstream)
     heads_rows = jnp.stack(heads_rows, axis=1)
+    if paired:
+        heads_rows, cot_rows = lax.optimization_barrier((heads_rows, cot_rows))
     attended = lax.all_to_all(heads_rows, "seq", 0, 0)
     grad_hidden = expert_grad_hidden(
-        place, cot_rows, after(meta, heads_rows), expert_down, capacity, 0, local_experts
+        cot_rows, after(meta, heads_rows), expert_down, capacity
     )
     attended, grad_hidden = lax.optimization_barrier((attended, grad_hidden))
     mixed, mid_out, moe_rows = project_out(
         attended, w_out, out_downs, out_ups, tokens, moe_row
     )
-    gathered = gather_rows(moe_rows)
+    gathered = gather_far(moe_rows, gather_near(moe_rows)) if paired else gather_whole(moe_rows)
     half = local_experts // 2
 
-    paired = devices == 8 and groups == 2
     hidden, parts, others = expert_middle(
         place,
         gathered,
@@ -1216,32 +1279,28 @@
         paired,
     )
     if paired:
-        beside = swap(others, 1).reshape(devices // 2, groups, shard, width)
-        far_sums = [add_low(parts[6][g], beside[3][g]) for g in range(groups)]
-        near_sums = [add_low(parts[WAYS[g][0]][g], beside[WAYS[g][0] // 2][g]) for g in range(groups)]
-        far_sums, near_sums = lax.optimization_barrier((far_sums, near_sums))
-        far = [swap(far_sums[g], WAYS[g][0]) for g in range(groups)]
-        near = [swap(near_sums[g], WAYS[g][0]) for g in range(groups)]
+        far, near, beside = near_sums_of(parts, others)
         produced = expert_produce(
-            place, after(hidden, far_sums), meta, expert_down, capacity, 0, half
+            place, after(hidden, far), meta, expert_down, capacity, 0, half, groups, paired
         )
+        far, near = send_near(far, near)
         far, produced = lax.optimization_barrier((far, produced))
-        joined_sums = [
-            add_low(parts[WAYS[g][1]][g], beside[WAYS[g][1] // 2][g], far[g]) for g in range(groups)
-        ]
-        joined = [swap(joined_sums[g], WAYS[g][1]) for g in range(groups)]
+        joined = send_joined(joined_sums_of(parts, beside, far))
         grad_pieces = [
             [parts[0][g], beside[0][g], near[g], joined[g]] for g in range(groups)
         ]
     else:
         summed = lax.psum_scatter(parts, "exp").reshape(groups, shard, width)
         grad_pieces = [[summed[g]] for g in range(groups)]
-        produced = expert_produce(place, hidden, meta, expert_down, capacity, 0, half)
+        produced = expert_produce(
+            place, hidden, meta, expert_down, capacity, 0, half, groups, paired
+        )
     grad_mixed, grad_out_downs, grad_out_ups, grad_att = project_out_back(
-        grad_pieces, mixed, upstream, moe_row, w_out, out_downs, out_ups, attended, mid_out
-    )
-    out_parts = expert_produce(
-        place, hidden, after(meta, grad_mixed), expert_down, capacity, half, local_experts, produced
+        grad_pieces, mixed, jnp.stack(upstream), moe_row, w_out, out_downs, out_ups, attended, mid_out
+    )
+    out_parts, out_others = expert_produce(
+        place, hidden, after(meta, grad_mixed), expert_down, capacity, half, local_experts,
+        groups, paired, produced,
     )
     grad_att = lax.all_to_all(grad_att, "seq", 0, 0)
     grad_raw, gups = [], []
@@ -1260,30 +1319,52 @@
             *tables[g],
         )
         gups.append(gup)
-        if not g:
-            out_sum = lax.psum_scatter(after(out_parts, gup), "exp")
+        if paired and not g:
+            out_far, out_near, out_beside = near_sums_of(out_parts, after(out_others, gup))
+        if paired and g:
+            out_far, out_near = send_near(out_far, out_near)
+            back, out_far, out_near = lax.optimization_barrier((back, out_far, out_near))
         grad_raw.append(forward_seq(after(back, grad_raw) if g else back))
-    out_sum = out_sum.reshape(groups, shard, width)
-
+    if paired:
+        joined_sums = joined_sums_of(out_parts, out_beside, out_far)
+        out_joined = send_joined(joined_sums)
+        normed = after(normed, joined_sums)
     gups = jnp.stack(after(gups, grad_raw[0]))
     wide_ups = lax.dynamic_update_slice_in_dim(
         jnp.zeros((groups, own, width), BF16), gups, here * part, axis=2
     )
     early = jnp.concatenate([grad_out_downs, wide_ups, grad_out_ups], axis=1)
     early = jnp.moveaxis(early.reshape(groups, -1, devices, slice_width), 2, 0)
-    output = (mixed + after(out_sum, gups).astype(F32)).astype(BF16)
-
-    smalls, late = [], []
+
+    late = jnp.pad(early, ((0, 0), (0, 0), (own, 0), (0, 0)))
+    grad_input = None
     for g in range(groups):
-        small, down = adapter_grads(place, g, grad_raw[g], normed, ups, devices)
-        smalls.append(small)
-        late.append(down)
-    late = jnp.concatenate([jnp.stack(late, axis=1), early], axis=2)
-    late = lax.all_to_all(late, "exp", 0, 0)
-    grad_input = project_first_back(
-        place, grad_raw, smalls, downs, w_qkv, after(flat_tokens, output), gain_row, grad_mixed
-    )
-    late = after(late, grad_input)
+        small, late = adapter_grads(place, g, grad_raw[g], normed, ups, late)
+        if g == groups - 1:
+            late = lax.all_to_all(late, "exp", 0, 0)
+        grad_input = project_first_back(
+            g, grad_raw[g], small, downs, w_qkv, tokens, gain_row, grad_mixed, grad_input
+        )
+        if g < groups - 1:
+            late, grad_input = lax.optimization_barrier((late, grad_input))
+            if paired:
+                outputs = [
+                    mixed[g]
+                    + functools.reduce(
+                        jnp.add,
+                        [
+                            value.astype(F32)
+                            for value in (out_parts[0][g], out_beside[0][g], out_near[g], out_joined[g])
+                        ],
+                    )
+                    for g in range(groups)
+                ]
+                output = jnp.stack(outputs).astype(BF16)
+            else:
+                out_sum = lax.psum_scatter(out_parts, "exp").reshape(groups, shard, width)
+                output = (mixed + out_sum.astype(F32)).astype(BF16)
+            late, output = lax.optimization_barrier((late, output))
+    late, grad_input = lax.optimization_barrier((late, grad_input))
     pieces = jnp.einsum("dgk,dgrw->krw", choices, late, preferred_element_type=F32)
     pieces = pieces.astype(BF16)
     pieces = pieces.reshape(splits, -1, slice_width)

time: 558 us -> 553 us (level); the launches traced: 557 us -> 543 us
  waiting for transfers between devices: 186 us -> 137 us
  starting transfers between devices: 55.4 us -> 77.5 us
  Pallas kernels: 256 us -> 269 us
  between operations: 14.7 us -> 2.07 us
  local copies, waits for them, and re-layouts: 18.6 us -> 25.6 us
  other arithmetic: 24.5 us -> 31.4 us
    all_to_all x4, waiting for transfers between devices: 76.2 us -> 10.8 us  [forward_seq(): return lax.all_to_all(pieces, 'seq', 0, 0)]
    ppermute x21 -> x56, waiting for transfers between devices: 52.7 us -> 93.2 us  [swap(): return lax.ppermute(values, 'exp', [(i, i ^ mask) for i in range(count)])]
    ppermute x21 -> x56, starting transfers between devices: 13.5 us -> 37.2 us  [swap(): return lax.ppermute(values, 'exp', [(i, i ^ mask) for i in range(count)])]
    all_gather x2 -> x0, waiting for transfers between devices: 18.8 us -> none  [the longest x1 18.8 us: local(): all_adapters = lax.all_gather(adapter_rows, 'exp')]
    pallas_call x6 -> x8, Pallas kernels: 68.2 us -> 82.2 us  [the longest x2 28.4 us: project_first_back(): kernel_call(body, 'project_first_back', (1,), [group_block(downs.shape, g...]
    ppermute x9, waiting for transfers between devices: 31.7 us -> 22.1 us  [shift(): lax.ppermute(values, 'seq', [(i, (i + distance) % count) for i in range(c...]
    unnamed x81 -> x100, local copies, waits for them, and re-layouts: 5.58 us -> 14.2 us
    convert_element_type x3 -> x5, other arithmetic: 7.13 us -> 13.1 us  [add_low(): functools.reduce(jnp.add, [value.astype(F32) for value in values])]
  transfers between devices with their start and end apart: 40 -> 72, of which waited for: 24 -> 28; matrix products, arithmetic and copies ran while one was open for 4% -> 7% of each run, Pallas kernels for 24% -> 24%
where the time goes in v1:
time: 553 us; the launch traced here: 543 us
  Pallas kernels  269 us (49%)
  waiting for transfers between devices  137 us (25%)
  starting transfers between devices  77.5 us (14%)
  other arithmetic  31.4 us (6%)
  local copies, waits for them, and re-layouts  25.6 us (5%)
    ppermute x56, waiting for transfers between devices, swap(): return lax.ppermute(values, 'exp', [(i, i ^ mask) for i in range(count)])  93.2 us
    pallas_call x1, Pallas kernels, expert_middle(): kernel_call(body, 'expert_middle', (experts,), [whole_block(meta.shape),...  91.5 us
    ppermute x56, starting transfers between devices, swap(): return lax.ppermute(values, 'exp', [(i, i ^ mask) for i in range(count)])  37.2 us
    pallas_call x2, Pallas kernels, expert_produce(): kernel_call(body, 'expert_produce', (last - first,), [whole_block(meta.sh...  30.2 us
    pallas_call x2, Pallas kernels, project_first_back(): kernel_call(body, 'project_first_back', (1,), [group_block(downs.shape, g...  28.4 us
    pallas_call x2, Pallas kernels, attend_back(): kernel_call(body, 'attend_back', (heads // step_heads,), [whole_block((1,...  25.5 us
    pallas_call x1, Pallas kernels, expert_grad_hidden(): kernel_call(body, 'expert_grad_hidden', (experts,), [whole_block(meta.sha...  23.8 us
    ppermute x9, waiting for transfers between devices, shift(): lax.ppermute(values, 'seq', [(i, (i + distance) % count) for i in range(c...  22.1 us
  transfers between devices with their start and end apart: 72, of which 28 were waited for; matrix products, arithmetic and copies ran while one was open for 7% of the time, Pallas kernels for 24%

profile of v1, /device:TPU:0, one launch (start us, length us, event | category | flops | bytes accessed | tf_op | source)
XLA Modules:
  0.0 543.2 jit_solution(6059716810345830065)
XLA Ops:
  1.2 14.0 %project_first.1 = (bf16[4,3,128,512]{3,2,1,0:T(8,128)(2,1)}, bf16[4,3,128,512]{3,2,1,0:T(8,128)(2,1)}, bf16[4,2,128,512]{3,2,1,0:T(8,128)(2,1)}, bf16[256,2048]{1,0:T(8,128)(2,1)}) custom-call(s32[2]{0:T(128)} %pad_add_fusion.place_ref, bf16[256,2048]{1,0:T(8,128)(2,1)} %bitcast.201, f32[1,2048]{1,0:T(1,128)} %bitcast.224, bf16[3,2048,2048]{2,1,0:T(8,128)(2,1)} %w_ref.15), custom_call_target="tpu_custom_call" | custom-call | flops 64424508 | bytes 251658 | tf_op jit(solution)/shard_map/project_first/pallas_call | solution.py:313
  35.2 9.5 %collective-permute-done.5.rest_6_ = bf16[624,256]{1,0:T(8,128)(2,1)S(1)} collective-permute-done((bf16[624,256]{1,0:T(8,128)(2,1)S(1)}, bf16[624,256]{1,0:T(8,128)(2,1)S(1)}, u32[]{:S(2)}, u32[]{:S(2)}) %collective-permute-start.5) | collective-permute-done | bytes 319520 | tf_op jit(solution)/shard_map/ppermute | solution.py:104
  86.3 10.0 %attend.2 = (bf16[4,128,512]{2,1,0:T(8,128)(2,1)}, bf16[4,512,128]{2,1,0:T(8,128)(2,1)}, bf16[4,512,128]{2,1,0:T(8,128)(2,1)}, bf16[4,512,128]{2,1,0:T(8,128)(2,...) custom-call(s32[1]{0:T(128)} %get-tuple-element.329.len_ref, bf16[3,16,512]{2,1,0:T(8,128)(2,1)} %bitcast.215, ...), custom_call_target="tpu_custom_call" | custom-call | flops 5368709 | bytes 104857 | tf_op jit(solution)/shard_map/attend/pallas_call | solution.py:473
  104.2 11.5 %collective-permute-done.27.rest_12_ = bf16[128,2048]{1,0:T(8,128)(2,1)S(1)} collective-permute-done((bf16[128,2048]{1,0:T(8,128)(2,1)}, bf16[128,2048]{1,0:T(8,128)(2,1)S(1)}, u32[]{:S(2)}, u32[]{:S(2)}) %collective-permute-start.27) | collective-permute-done | bytes 524320 | tf_op jit(solution)/shard_map/ppermute | solution.py:104
  116.2 9.9 %attend.3 = (bf16[4,128,512]{2,1,0:T(8,128)(2,1)}, bf16[4,512,128]{2,1,0:T(8,128)(2,1)}, bf16[4,512,128]{2,1,0:T(8,128)(2,1)}, bf16[4,512,128]{2,1,0:T(8,128)(2,...) custom-call(s32[1]{0:T(128)} %get-tuple-element.330.len_ref, bf16[3,16,512]{2,1,0:T(8,128)(2,1)} %bitcast.214, ...), custom_call_target="tpu_custom_call" | custom-call | flops 5368709 | bytes 104857 | tf_op jit(solution)/shard_map/attend/pallas_call | solution.py:473
  133.5 23.8 %expert_grad_hidden.1.gh_ref = bf16[4,768,1024]{2,1,0:T(8,128)(2,1)} custom-call(f32[8,2,4,256]{3,2,1,0:T(4,128)} %pad_maximum_fusion.9.meta_ref, bf16[4,1024,2048]{2,1,0:T(8,128)(2,1)} %w_ref.13, bf16[128,2048]{1,0:T(8,128)(2,1)} %get-tuple-element.196.rest_0_, bf16[128,2048]{1,0:T(8,128)(2,1)} %get-tuple-element.197.rest_1_, ...), custom_call_target="tpu_custom_call" | custom-call | flops 161061280 | bytes 251658 | tf_op jit(solution)/shard_map/expert_grad_hidden/pallas_call | solution.py:704
  160.5 7.5 %project_out.1 = (f32[2,128,2048]{2,1,0:T(8,128)}, bf16[2,16,128]{2,1,0:T(8,128)(2,1)}, bf16[128,2048]{1,0:T(8,128)(2,1)}, bf16[128,2048]{1,0:T(8,128)(2,1)}) custom-call(bf16[4,2,128,512]{3,2,1,0:T(8,128)(2,1)} %copy-done.4, bf16[2048,2048]{1,0:T(8,128)(2,1)} %w_ref.12, bf16[2,16,2048]{2,1,0:T(8,128)(2,1)} %get-tuple-element.167.down_ref, ...), custom_call_target="tpu_custom_call" | custom-call | flops 21474836 | bytes 83886 | tf_op jit(solution)/shard_map/project_out/pallas_call | solution.py:605
  172.4 10.7 %collective-permute-done.33.rest_4_ = bf16[128,2048]{1,0:T(8,128)(2,1)S(1)} collective-permute-done((bf16[128,2048]{1,0:T(8,128)(2,1)}, bf16[128,2048]{1,0:T(8,128)(2,1)S(1)}, u32[]{:S(2)}, u32[]{:S(2)}) %collective-permute-start.33) | collective-permute-done | bytes 524320 | tf_op jit(solution)/shard_map/ppermute | solution.py:104
  185.4 9.0 %collective-permute-done.34.rest_5_ = bf16[128,2048]{1,0:T(8,128)(2,1)S(1)} collective-permute-done((bf16[128,2048]{1,0:T(8,128)(2,1)}, bf16[128,2048]{1,0:T(8,128)(2,1)S(1)}, u32[]{:S(2)}, u32[]{:S(2)}) %collective-permute-start.34) | collective-permute-done | bytes 524320 | tf_op jit(solution)/shard_map/ppermute | solution.py:104
  195.6 10.1 %collective-permute-done.41.rest_12_ = bf16[128,2048]{1,0:T(8,128)(2,1)S(1)} collective-permute-done((bf16[128,2048]{1,0:T(8,128)(2,1)S(1)}, bf16[128,2048]{1,0:T(8,128)(2,1)S(1)}, u32[]{:S(2)}, u32[]{:S(2)}) %collective-permute-start.41) | collective-permute-done | bytes 524320 | tf_op jit(solution)/shard_map/ppermute | solution.py:104
  208.6 91.5 %expert_middle.1 = (bf16[4,768,1024]{2,1,0:T(8,128)(2,1)}, bf16[128,2048]{1,0:T(8,128)(2,1)}, bf16[128,2048]{1,0:T(8,128)(2,1)}, bf16[128,2048]{1,0:T(8,128)(2,1...) custom-call(s32[2]{0:T(128)} %pad_add_fusion.place_ref, ...), custom_call_target="tpu_custom_call" | custom-call | flops 547608320 | bytes 587202 | tf_op jit(solution)/shard_map/expert_middle/pallas_call | solution.py:828
  300.3 7.3 %collective-permute-done.45 = bf16[4,256,2048]{2,1,0:T(8,128)(2,1)S(1)} collective-permute-done((bf16[4,256,2048]{2,1,0:T(8,128)(2,1)}, bf16[4,256,2048]{2,1,0:T(8,128)(2,1)S(1)}, u32[]{:S(2)}, u32[]{:S(2)}) %collective-permute-start.45) | collective-permute-done | bytes 4194336 | tf_op jit(solution)/shard_map/ppermute | solution.py:104
  316.7 12.3 %expert_produce.2.rest_0_ = bf16[2,768,2048]{2,1,0:T(8,128)(2,1)} custom-call(s32[2]{0:T(128)} %pad_add_fusion.place_ref, f32[8,2,4,256]{3,2,1,0:T(4,128)} %pad_maximum_fusion.9.meta_ref, bf16[4,768,1024]{2,1,0:T(8,128)(2,1)} %get-tuple-element.229.h_ref, bf16[4,1024,2048]{2,1,0:T(8,128)(2,1)} %w_ref.13), custom_call_target="tpu_custom_call" | custom-call | flops 64424508 | bytes 293601 | tf_op jit(solution)/shard_map/expert_produce/pallas_call | solution.py:905
  340.4 10.2 %collective-permute-done.49.rest_3_ = bf16[128,2048]{1,0:T(8,128)(2,1)} collective-permute-done((bf16[128,2048]{1,0:T(8,128)(2,1)S(1)}, bf16[128,2048]{1,0:T(8,128)(2,1)}, u32[]{:S(2)}, u32[]{:S(2)}) %collective-permute-start.49) | collective-permute-done | bytes 524320 | tf_op jit(solution)/shard_map/ppermute | solution.py:104
  350.6 9.5 %project_out_back.1 = (f32[2,128,2048]{2,1,0:T(8,128)}, bf16[2,16,2048]{2,1,0:T(8,128)(2,1)}, bf16[2,16,2048]{2,1,0:T(8,128)(2,1)}, bf16[4,2,128,512]{3,2,1,0:T(8,128)(2,1)}) custom-call(bf16[2,128,2048]{2,1,0:T(8,128)(2,1)} %copy-done.5, f32[1,2048]{1,0:T(1,128)} %bitcast.230, bf16[2048,2048]{1,0:T(8,128)(2,1)} %w_ref.12, ...), custom_call_target="tpu_custom_call" | custom-call | flops 21474836 | bytes 83886 | tf_op jit(solution)/shard_map/project_out_back/pallas_call | solution.py:970
  363.8 17.9 %expert_produce.3 = (bf16[128,2048]{1,0:T(8,128)(2,1)}, bf16[128,2048]{1,0:T(8,128)(2,1)}, bf16[128,2048]{1,0:T(8,128)(2,1)}, bf16[128,2048]{1,0:T(8,128)(2,1)},...) custom-call(s32[2]{0:T(128)} %pad_add_fusion.place_ref, ...), custom_call_target="tpu_custom_call" | custom-call | flops 64424508 | bytes 293601 | tf_op jit(solution)/shard_map/expert_produce/pallas_call | solution.py:905
  381.8 7.2 %all-to-all-done.3.rest_0_.rest_1_.rest_2_.rest_3_ = bf16[4,2,128,512]{3,2,1,0:T(8,128)(2,1)S(1)} async-done(((bf16[4,2,128,512]{3,2,1,0:T(8,128)(2,1)}), bf16[4,2,128,512]{3,2,1,0:T(8,128)(2,1)S(1)}, u32[]{:S(2)}, u32[]{:S(2)}) %all-to-all-start.3) | async-done | bytes 1048608 | tf_op jit(solution)/shard_map/all_to_all | solution.py:1305
  390.0 12.7 %attend_back.2 = (bf16[4,3,128,512]{3,2,1,0:T(8,128)(2,1)}, bf16[48,512]{1,0:T(8,128)(2,1)}) custom-call(s32[1]{0:T(128)} %get-tuple-element.329.len_ref, f32[1,128]{1,0:T(1,128)} %bitcast.237, f32[1,128]{1,0:T(1,128)} %bitcast.241, s32[1,512]{1,0:T(1,128)} %bitcast.222, f32[512,128]{1,0:T(8,128)} %get-tuple-element.180.cos_ref, ...), custom_call_target="tpu_custom_call" | custom-call | flops 13421772 | bytes 146800 | tf_op jit(solution)/shard_map/attend_back/pallas_call | solution.py:540
  418.4 12.8 %attend_back.3 = (bf16[4,3,128,512]{3,2,1,0:T(8,128)(2,1)}, bf16[48,512]{1,0:T(8,128)(2,1)}) custom-call(s32[1]{0:T(128)} %get-tuple-element.330.len_ref, f32[1,128]{1,0:T(1,128)} %bitcast.238, f32[1,128]{1,0:T(1,128)} %bitcast.242, s32[1,512]{1,0:T(1,128)} %bitcast.223, f32[512,128]{1,0:T(8,128)} %get-tuple-element.180.cos_ref, ...), custom_call_target="tpu_custom_call" | custom-call | flops 13421772 | bytes 146800 | tf_op jit(solution)/shard_map/attend_back/pallas_call | solution.py:540
  431.2 8.6 %collective-permute-done.55 = bf16[128,2048]{1,0:T(8,128)(2,1)} collective-permute-done((bf16[128,2048]{1,0:T(8,128)(2,1)}, bf16[128,2048]{1,0:T(8,128)(2,1)}, u32[]{:S(2)}, u32[]{:S(2)}) %collective-permute-start.55) | collective-permute-done | bytes 524320 | tf_op jit(solution)/shard_map/ppermute | solution.py:104
  460.6 14.2 %project_first_back.2.rest_0_ = f32[2,128,2048]{2,1,0:T(8,128)} custom-call(bf16[2,48,2048]{2,1,0:T(8,128)(2,1)} %get-tuple-element.274.down_ref, bf16[3,2048,2048]{2,1,0:T(8,128)(2,1)} %w_ref.15, bf16[2,128,2048]{2,1,0:T(8,128)(2,1)} %tok_ref.5, f32[1,2048]{1,0:T(1,128)} %bitcast.225, f32[2,128,2048]{2,1,0:T(8,128)} %get-tuple-element.235.mixed_ref, ...), custom_call_target="tpu_custom_call" | custom-call | flops 32212254 | bytes 251658 | tf_op jit(solution)/shard_map/project_first_back/pallas_call | solution.py:1085
  496.0 14.2 %project_first_back.3 = f32[2,128,2048]{2,1,0:T(8,128)} custom-call(bf16[2,48,2048]{2,1,0:T(8,128)(2,1)} %get-tuple-element.274.down_ref, bf16[3,2048,2048]{2,1,0:T(8,128)(2,1)} %w_ref.15, bf16[2,128,2048]{2,1,0:T(8,128)(2,1)} %tok_ref.5, f32[1,2048]{1,0:T(1,128)} %bitcast.226, ...), custom_call_target="tpu_custom_call", output_to_operand_aliasing={{}: (7, {})} | custom-call | flops 32212254 | bytes 251658 | tf_op jit(solution)/shard_map/project_first_back/pallas_call | solution.py:1085
  518.3 7.0 %collective-permute-done.60 = bf16[256,256]{1,0:T(8,128)(2,1)S(1)} collective-permute-done((bf16[256,256]{1,0:T(8,128)(2,1)S(1)}, bf16[256,256]{1,0:T(8,128)(2,1)S(1)}, u32[]{:S(2)}, u32[]{:S(2)}) %collective-permute-start.60) | collective-permute-done | bytes 131104 | tf_op jit(solution)/shard_map/ppermute | solution.py:109
  531.3 7.7 %collective-permute-done.63 = bf16[256,256]{1,0:T(8,128)(2,1)S(1)} collective-permute-done((bf16[256,256]{1,0:T(8,128)(2,1)S(1)}, bf16[256,256]{1,0:T(8,128)(2,1)S(1)}, u32[]{:S(2)}, u32[]{:S(2)}) %collective-permute-start.63) | collective-permute-done | bytes 131104 | tf_op jit(solution)/shard_map/ppermute | solution.py:109
  (312 shorter events, 192.0 us)
Async XLA Ops:
  18.5 26.8 %collective-permute-start = (bf16[624,256]{1,0:T(8,128)(2,1)S(1)}, bf16[624,256]{1,0:T(8,128)(2,1)S(1)}, u32[]{:S(2)}, u32[]{:S(2)}) collective-permute-start(bf16[624,256]{1,0:T(8,128)(2,1)S(1)} %pad_maximum_fusion.4.rest_0_), channel_id=1, source_target_pairs={{0,1},{1,0},{2,3},{3,2},{4,5},{5,4},{6,7},{7,6},{8,9},{9,8},{10,11... | collective-permute-start | bytes 958472 | tf_op jit(solution)/shard_map/ppermute | solution.py:104
  23.1 45.4 %all-to-all-start = ((bf16[4,3,128,512]{3,2,1,0:T(8,128)(2,1)}), bf16[4,3,128,512]{3,2,1,0:T(8,128)(2,1)S(1)}, u32[]{:S(2)}, u32[]{:S(2)}) async-start(bf16[4,3,128,512]{3,2,1,0:T(8,128)(2,1)} %get-tuple-element.151), calls=%async_computation | async-start | bytes 3145728 | tf_op jit(solution)/shard_map/all_to_all | solution.py:119
  68.5 47.7 %all-to-all-start.1 = ((bf16[4,3,128,512]{3,2,1,0:T(8,128)(2,1)}), bf16[4,3,128,512]{3,2,1,0:T(8,128)(2,1)}, u32[]{:S(2)}, u32[]{:S(2)}) async-start(bf16[4,3,128,512]{3,2,1,0:T(8,128)(2,1)} %get-tuple-element.189), calls=%async_computation.1 | async-start | bytes 3145728 | tf_op jit(solution)/shard_map/all_to_all | solution.py:119
  75.2 21.1 %collective-permute-start.19 = (bf16[128,2048]{1,0:T(8,128)(2,1)}, bf16[128,2048]{1,0:T(8,128)(2,1)}, u32[]{:S(2)}, u32[]{:S(2)}) collective-permute-start(bf16[128,2048]{1,0:T(8,128)(2,1)} %get-tuple-element.196.rest_0_), channel_id=1, source_target_pairs={{0,2},{1,3},{2,0},{3,1},{4,6},{5,7},{6,4},{7,5},{8,10},{9,11},{10,... | collective-permute-start | bytes 1572872 | tf_op jit(solution)/shard_map/ppermute | solution.py:104
  75.7 25.3 %collective-permute-start.20 = (bf16[128,2048]{1,0:T(8,128)(2,1)}, bf16[128,2048]{1,0:T(8,128)(2,1)}, u32[]{:S(2)}, u32[]{:S(2)}) collective-permute-start(bf16[128,2048]{1,0:T(8,128)(2,1)} %get-tuple-element.197.rest_1_), channel_id=1, source_target_pairs={{0,2},{1,3},{2,0},{3,1},{4,6},{5,7},{6,4},{7,5},{8,10},{9,11},{10,... | collective-permute-start | bytes 1572872 | tf_op jit(solution)/shard_map/ppermute | solution.py:104
  77.2 23.9 %collective-permute-start.23 = (bf16[128,2048]{1,0:T(8,128)(2,1)}, bf16[128,2048]{1,0:T(8,128)(2,1)}, u32[]{:S(2)}, u32[]{:S(2)}) collective-permute-start(bf16[128,2048]{1,0:T(8,128)(2,1)} %get-tuple-element.196.rest_0_), channel_id=1, source_target_pairs={{0,4},{1,5},{2,6},{3,7},{4,0},{5,1},{6,2},{7,3},{8,12},{9,13},{10,... | collective-permute-start | bytes 1572872 | tf_op jit(solution)/shard_map/ppermute | solution.py:104
  77.8 24.8 %collective-permute-start.24 = (bf16[128,2048]{1,0:T(8,128)(2,1)}, bf16[128,2048]{1,0:T(8,128)(2,1)}, u32[]{:S(2)}, u32[]{:S(2)}) collective-permute-start(bf16[128,2048]{1,0:T(8,128)(2,1)} %get-tuple-element.197.rest_1_), channel_id=1, source_target_pairs={{0,4},{1,5},{2,6},{3,7},{4,0},{5,1},{6,2},{7,3},{8,12},{9,13},{10,... | collective-permute-start | bytes 1572872 | tf_op jit(solution)/shard_map/ppermute | solution.py:104
  79.9 23.7 %collective-permute-start.17 = (bf16[128,2048]{1,0:T(8,128)(2,1)}, bf16[128,2048]{1,0:T(8,128)(2,1)}, u32[]{:S(2)}, u32[]{:S(2)}) collective-permute-start(bf16[128,2048]{1,0:T(8,128)(2,1)} %get-tuple-element.196.rest_0_), channel_id=1, source_target_pairs={{0,1},{1,0},{2,3},{3,2},{4,5},{5,4},{6,7},{7,6},{8,9},{9,8},{10,11... | collective-permute-start | bytes 1572872 | tf_op jit(solution)/shard_map/ppermute | solution.py:104
  103.6 24.8 %collective-permute-start.22 = (bf16[128,2048]{1,0:T(8,128)(2,1)}, bf16[128,2048]{1,0:T(8,128)(2,1)}, u32[]{:S(2)}, u32[]{:S(2)}) collective-permute-start(bf16[128,2048]{1,0:T(8,128)(2,1)} %collective-permute-done.20.rest_5_), channel_id=1, source_target_pairs={{0,1},{1,0},{2,3},{3,2},{4,5},{5,4},{6,7},{7,6},{8,9},{9,8},{10,11... | collective-permute-start | bytes 1572872 | tf_op jit(solution)/shard_map/ppermute | solution.py:104
  103.6 24.8 %collective-permute-start.25 = (bf16[128,2048]{1,0:T(8,128)(2,1)}, bf16[128,2048]{1,0:T(8,128)(2,1)}, u32[]{:S(2)}, u32[]{:S(2)}) collective-permute-start(bf16[128,2048]{1,0:T(8,128)(2,1)} %collective-permute-done.23.rest_8_), channel_id=1, source_target_pairs={{0,1},{1,0},{2,3},{3,2},{4,5},{5,4},{6,7},{7,6},{8,9},{9,8},{10,11... | collective-permute-start | bytes 1572872 | tf_op jit(solution)/shard_map/ppermute | solution.py:104
  104.1 24.3 %collective-permute-start.26 = (bf16[128,2048]{1,0:T(8,128)(2,1)}, bf16[128,2048]{1,0:T(8,128)(2,1)}, u32[]{:S(2)}, u32[]{:S(2)}) collective-permute-start(bf16[128,2048]{1,0:T(8,128)(2,1)} %collective-permute-done.24.rest_9_), channel_id=1, source_target_pairs={{0,1},{1,0},{2,3},{3,2},{4,5},{5,4},{6,7},{7,6},{8,9},{9,8},{10,11... | collective-permute-start | bytes 1572872 | tf_op jit(solution)/shard_map/ppermute | solution.py:104
  128.5 31.1 %all-to-all-start.2 = ((bf16[4,2,128,512]{3,2,1,0:T(8,128)(2,1)}), bf16[4,2,128,512]{3,2,1,0:T(8,128)(2,1)S(1)}, u32[]{:S(2)}, u32[]{:S(2)}) async-start(bf16[4,2,128,512]{3,2,1,0:T(8,128)(2,1)} %pad_maximum_fusion), calls=%async_computation.2 | async-start | bytes 2097152 | tf_op jit(solution)/shard_map/all_to_all | solution.py:1259
  170.4 24.0 %collective-permute-start.34 = (bf16[128,2048]{1,0:T(8,128)(2,1)}, bf16[128,2048]{1,0:T(8,128)(2,1)S(1)}, u32[]{:S(2)}, u32[]{:S(2)}) collective-permute-start(bf16[128,2048]{1,0:T(8,128)(2,1)} %get-tuple-element.217.rest_1_), channel_id=1, source_target_pairs={{0,2},{1,3},{2,0},{3,1},{4,6},{5,7},{6,4},{7,5},{8,10},{9,11},{10,... | collective-permute-start | bytes 1572872 | tf_op jit(solution)/shard_map/ppermute | solution.py:104
  171.9 23.2 %collective-permute-start.37 = (bf16[128,2048]{1,0:T(8,128)(2,1)}, bf16[128,2048]{1,0:T(8,128)(2,1)S(1)}, u32[]{:S(2)}, u32[]{:S(2)}) collective-permute-start(bf16[128,2048]{1,0:T(8,128)(2,1)} %get-tuple-element.216.rest_0_), channel_id=1, source_target_pairs={{0,4},{1,5},{2,6},{3,7},{4,0},{5,1},{6,2},{7,3},{8,12},{9,13},{10,... | collective-permute-start | bytes 1572872 | tf_op jit(solution)/shard_map/ppermute | solution.py:104
  183.2 22.6 %collective-permute-start.41 = (bf16[128,2048]{1,0:T(8,128)(2,1)S(1)}, bf16[128,2048]{1,0:T(8,128)(2,1)S(1)}, u32[]{:S(2)}, u32[]{:S(2)}) collective-permute-start(bf16[128,2048]{1,0:T(8,128)(2,1)S(1)} %collective-permute-done.33.rest_4_), channel_id=1, source_target_pairs={{0,4},{1,5},{2,6},{3,7},{4,0},{5,1},{6,2},{7,3},{8,12},{9,13},{10,... | collective-permute-start | bytes 1572872 | tf_op jit(solution)/shard_map/ppermute | solution.py:104
  184.8 21.0 %collective-permute-start.42 = (bf16[128,2048]{1,0:T(8,128)(2,1)S(1)}, bf16[128,2048]{1,0:T(8,128)(2,1)S(1)}, u32[]{:S(2)}, u32[]{:S(2)}) collective-permute-start(bf16[128,2048]{1,0:T(8,128)(2,1)S(1)} %collective-permute-done.38.rest_9_), channel_id=1, source_target_pairs={{0,2},{1,3},{2,0},{3,1},{4,6},{5,7},{6,4},{7,5},{8,10},{9,11},{10,... | collective-permute-start | bytes 1572872 | tf_op jit(solution)/shard_map/ppermute | solution.py:104
  315.7 23.2 %collective-permute-start.46 = (bf16[128,2048]{1,0:T(8,128)(2,1)}, bf16[128,2048]{1,0:T(8,128)(2,1)S(1)}, u32[]{:S(2)}, u32[]{:S(2)}) collective-permute-start(bf16[128,2048]{1,0:T(8,128)(2,1)} %get-tuple-element.224), channel_id=1, source_target_pairs={{0,2},{1,3},{2,0},{3,1},{4,6},{5,7},{6,4},{7,5},{8,10},{9,11},{10,... | collective-permute-start | bytes 1572872 | tf_op jit(solution)/shard_map/ppermute | solution.py:104
  316.2 24.2 %collective-permute-start.50 = (bf16[128,2048]{1,0:T(8,128)(2,1)S(1)}, bf16[128,2048]{1,0:T(8,128)(2,1)S(1)}, u32[]{:S(2)}, u32[]{:S(2)}) collective-permute-start(bf16[128,2048]{1,0:T(8,128)(2,1)S(1)} %get-tuple-element.232), channel_id=1, source_target_pairs={{0,4},{1,5},{2,6},{3,7},{4,0},{5,1},{6,2},{7,3},{8,12},{9,13},{10,... | collective-permute-start | bytes 1572872 | tf_op jit(solution)/shard_map/ppermute | solution.py:104
  360.1 28.8 %all-to-all-start.3 = ((bf16[4,2,128,512]{3,2,1,0:T(8,128)(2,1)}), bf16[4,2,128,512]{3,2,1,0:T(8,128)(2,1)S(1)}, u32[]{:S(2)}, u32[]{:S(2)}) async-start(bf16[4,2,128,512]{3,2,1,0:T(8,128)(2,1)} %get-tuple-element.240), calls=%async_computation.3 | async-start | bytes 2097152 | tf_op jit(solution)/shard_map/all_to_all | solution.py:1305
  402.8 41.4 %all-to-all-start.4 = ((bf16[4,3,128,512]{3,2,1,0:T(8,128)(2,1)}), bf16[4,3,128,512]{3,2,1,0:T(8,128)(2,1)S(1)}, u32[]{:S(2)}, u32[]{:S(2)}) async-start(bf16[4,3,128,512]{3,2,1,0:T(8,128)(2,1)} %get-tuple-element.267), calls=%async_computation.4 | async-start | bytes 3145728 | tf_op jit(solution)/shard_map/all_to_all | solution.py:119
  416.5 23.4 %collective-permute-start.55 = (bf16[128,2048]{1,0:T(8,128)(2,1)}, bf16[128,2048]{1,0:T(8,128)(2,1)}, u32[]{:S(2)}, u32[]{:S(2)}) collective-permute-start(bf16[128,2048]{1,0:T(8,128)(2,1)} %get-tuple-element.261), channel_id=1, source_target_pairs={{0,2},{1,3},{2,0},{3,1},{4,6},{5,7},{6,4},{7,5},{8,10},{9,11},{10,... | collective-permute-start | bytes 1572872 | tf_op jit(solution)/shard_map/ppermute | solution.py:104
  417.9 22.2 %collective-permute-start.56 = (bf16[128,2048]{1,0:T(8,128)(2,1)}, bf16[128,2048]{1,0:T(8,128)(2,1)}, u32[]{:S(2)}, u32[]{:S(2)}) collective-permute-start(bf16[128,2048]{1,0:T(8,128)(2,1)} %get-tuple-element.262), channel_id=1, source_target_pairs={{0,4},{1,5},{2,6},{3,7},{4,0},{5,1},{6,2},{7,3},{8,12},{9,13},{10,... | collective-permute-start | bytes 1572872 | tf_op jit(solution)/shard_map/ppermute | solution.py:104
  445.5 40.8 %all-to-all-start.5 = ((bf16[4,3,128,512]{3,2,1,0:T(8,128)(2,1)}), bf16[4,3,128,512]{3,2,1,0:T(8,128)(2,1)S(1)}, u32[]{:S(2)}, u32[]{:S(2)}) async-start(bf16[4,3,128,512]{3,2,1,0:T(8,128)(2,1)} %get-tuple-element.283), calls=%async_computation.5 | async-start | bytes 3145728 | tf_op jit(solution)/shard_map/all_to_all | solution.py:119
  452.7 22.2 %collective-permute-start.57 = (bf16[128,2048]{1,0:T(8,128)(2,1)}, bf16[128,2048]{1,0:T(8,128)(2,1)}, u32[]{:S(2)}, u32[]{:S(2)}) collective-permute-start(bf16[128,2048]{1,0:T(8,128)(2,1)} %get-tuple-element.300), channel_id=1, source_target_pairs={{0,4},{1,5},{2,6},{3,7},{4,0},{5,1},{6,2},{7,3},{8,12},{9,13},{10,... | collective-permute-start | bytes 1572872 | tf_op jit(solution)/shard_map/ppermute | solution.py:104
  (94 other events, 1195.8 us)

commit v2 on v1

--- a/solution.py
+++ b/solution.py
@@ -177,10 +177,12 @@
 
 def near_sums_of(parts, others):
     groups = len(parts[0])
-    beside = swap(others, 1).reshape((4, groups) + parts[0][0].shape)
-    far = [add_low(parts[6][g], beside[3][g]) for g in range(groups)]
+    last = swap(others[1], 1).reshape((groups,) + parts[0][0].shape)
+    beside = swap(others[0], 1).reshape((3, groups) + parts[0][0].shape)
+    far = [add_low(parts[6][g], last[g]) for g in range(groups)]
+    beside = after(beside, far)
     near = [add_low(parts[WAYS[g][0]][g], beside[WAYS[g][0] // 2][g]) for g in range(groups)]
-    return lax.optimization_barrier((far, near)) + (beside,)
+    return far, near, beside
 
 
 def send_near(far, near):
@@ -762,21 +764,27 @@
     if not paired:
         return [shape_of((count, tokens, width), BF16)]
     one = shape_of((tokens // groups, width), BF16)
-    return [one] * (count // 2 * groups) + [shape_of((count // 2, tokens, width), BF16)]
+    return [one] * (count // 2 * groups) + [
+        shape_of((count // 2 - 1, tokens, width), BF16),
+        shape_of((1, tokens, width), BF16),
+    ]
 
 
 def sum_targets(outs, place_ref, m, groups, paired):
     if not paired:
         return [outs[0].at[place_ref[1] ^ m]]
+    if m == 2 * (outs[-2].shape[0] + 1) - 1:
+        return [outs[-1].at[0]]
     if m % 2:
-        return [outs[-1].at[m // 2]]
+        return [outs[-2].at[m // 2]]
     return outs[m // 2 * groups : (m // 2 + 1) * groups]
 
 
 def sums_of(result, count, groups, paired):
     if not paired:
         return result[0], None
-    return {m: result[m // 2 * groups : (m // 2 + 1) * groups] for m in range(0, count, 2)}, result[-1]
+    even = {m: result[m // 2 * groups : (m // 2 + 1) * groups] for m in range(0, count, 2)}
+    return even, result[-2:]
 
 
 def expert_middle(
@@ -1281,7 +1289,7 @@
     if paired:
         far, near, beside = near_sums_of(parts, others)
         produced = expert_produce(
-            place, after(hidden, far), meta, expert_down, capacity, 0, half, groups, paired
+            place, after(hidden, far, near), meta, expert_down, capacity, 0, half, groups, paired
         )
         far, near = send_near(far, near)
         far, produced = lax.optimization_barrier((far, produced))

time: 553 us -> 550 us (level)
  waiting for transfers between devices: 137 us -> 131 us
    ppermute x56 -> x58, waiting for transfers between devices: 93.2 us -> 85.8 us  [swap(): return lax.ppermute(values, 'exp', [(i, i ^ mask) for i in range(count)])]
    convert_element_type x5 -> x7, other arithmetic: 13.1 us -> 14.5 us  [add_low(): functools.reduce(jnp.add, [value.astype(F32) for value in values])]
    ppermute x56 -> x58, starting transfers between devices: 37.2 us -> 38.1 us  [swap(): return lax.ppermute(values, 'exp', [(i, i ^ mask) for i in range(count)])]
    unnamed x100 -> x118, local copies, waits for them, and re-layouts: 14.2 us -> 13.8 us
  transfers between devices with their start and end apart: 72 -> 74, of which waited for: 28 -> 25; matrix products, arithmetic and copies ran while one was open for 7% -> 8% of each run, Pallas kernels for 24% -> 24%
where the time goes in v2:
time: 550 us; the launch traced here: 540 us
  Pallas kernels  269 us (49%)
  waiting for transfers between devices  131 us (24%)
  starting transfers between devices  78.5 us (14%)
  other arithmetic  32.9 us (6%)
  local copies, waits for them, and re-layouts  25.4 us (5%)
    pallas_call x1, Pallas kernels, expert_middle(): kernel_call(body, 'expert_middle', (experts,), [whole_block(meta.shape),...  91.5 us
    ppermute x58, waiting for transfers between devices, swap(): return lax.ppermute(values, 'exp', [(i, i ^ mask) for i in range(count)])  85.8 us
    ppermute x58, starting transfers between devices, swap(): return lax.ppermute(values, 'exp', [(i, i ^ mask) for i in range(count)])  38.1 us
    pallas_call x2, Pallas kernels, expert_produce(): kernel_call(body, 'expert_produce', (last - first,), [whole_block(meta.sh...  30.2 us
    pallas_call x2, Pallas kernels, project_first_back(): kernel_call(body, 'project_first_back', (1,), [group_block(downs.shape, g...  28.4 us
    pallas_call x2, Pallas kernels, attend_back(): kernel_call(body, 'attend_back', (heads // step_heads,), [whole_block((1,...  25.4 us
    pallas_call x1, Pallas kernels, expert_grad_hidden(): kernel_call(body, 'expert_grad_hidden', (experts,), [whole_block(meta.sha...  23.8 us
    ppermute x9, waiting for transfers between devices, shift(): lax.ppermute(values, 'seq', [(i, (i + distance) % count) for i in range(c...  22.1 us
  transfers between devices with their start and end apart: 74, of which 25 were waited for; matrix products, arithmetic and copies ran while one was open for 8% of the time, Pallas kernels for 24%

profile of v2, /device:TPU:0, one launch (start us, length us, event | category | flops | bytes accessed | tf_op | source)
XLA Modules:
  0.0 540.1 jit_solution(11272751132096874393)
XLA Ops:
  1.2 14.1 %project_first.1 = (bf16[4,3,128,512]{3,2,1,0:T(8,128)(2,1)}, bf16[4,3,128,512]{3,2,1,0:T(8,128)(2,1)}, bf16[4,2,128,512]{3,2,1,0:T(8,128)(2,1)}, bf16[256,2048]{1,0:T(8,128)(2,1)}) custom-call(s32[2]{0:T(128)} %pad_add_fusion.place_ref, bf16[256,2048]{1,0:T(8,128)(2,1)} %bitcast.183, f32[1,2048]{1,0:T(1,128)} %bitcast.209, bf16[3,2048,2048]{2,1,0:T(8,128)(2,1)} %w_ref.15), custom_call_target="tpu_custom_call" | custom-call | flops 64424508 | bytes 251658 | tf_op jit(solution)/shard_map/project_first/pallas_call | solution.py:315
  35.4 9.4 %collective-permute-done.5.rest_6_ = bf16[624,256]{1,0:T(8,128)(2,1)S(1)} collective-permute-done((bf16[624,256]{1,0:T(8,128)(2,1)S(1)}, bf16[624,256]{1,0:T(8,128)(2,1)S(1)}, u32[]{:S(2)}, u32[]{:S(2)}) %collective-permute-start.5) | collective-permute-done | bytes 319520 | tf_op jit(solution)/shard_map/ppermute | solution.py:104
  85.6 9.9 %attend.2 = (bf16[4,128,512]{2,1,0:T(8,128)(2,1)}, bf16[4,512,128]{2,1,0:T(8,128)(2,1)}, bf16[4,512,128]{2,1,0:T(8,128)(2,1)}, bf16[4,512,128]{2,1,0:T(8,128)(2,...) custom-call(s32[1]{0:T(128)} %get-tuple-element.323.len_ref, bf16[3,16,512]{2,1,0:T(8,128)(2,1)} %bitcast.200, ...), custom_call_target="tpu_custom_call" | custom-call | flops 5368709 | bytes 104857 | tf_op jit(solution)/shard_map/attend/pallas_call | solution.py:475
  103.5 11.4 %collective-permute-done.27.rest_12_ = bf16[128,2048]{1,0:T(8,128)(2,1)} collective-permute-done((bf16[128,2048]{1,0:T(8,128)(2,1)S(1)}, bf16[128,2048]{1,0:T(8,128)(2,1)}, u32[]{:S(2)}, u32[]{:S(2)}) %collective-permute-start.27) | collective-permute-done | bytes 524320 | tf_op jit(solution)/shard_map/ppermute | solution.py:104
  115.4 10.0 %attend.3 = (bf16[4,128,512]{2,1,0:T(8,128)(2,1)}, bf16[4,512,128]{2,1,0:T(8,128)(2,1)}, bf16[4,512,128]{2,1,0:T(8,128)(2,1)}, bf16[4,512,128]{2,1,0:T(8,128)(2,...) custom-call(s32[1]{0:T(128)} %get-tuple-element.324.len_ref, bf16[3,16,512]{2,1,0:T(8,128)(2,1)} %bitcast.199, ...), custom_call_target="tpu_custom_call" | custom-call | flops 5368709 | bytes 104857 | tf_op jit(solution)/shard_map/attend/pallas_call | solution.py:475
  132.7 23.8 %expert_grad_hidden.1.gh_ref = bf16[4,768,1024]{2,1,0:T(8,128)(2,1)} custom-call(f32[8,2,4,256]{3,2,1,0:T(4,128)} %pad_maximum_fusion.9.meta_ref, bf16[4,1024,2048]{2,1,0:T(8,128)(2,1)} %w_ref.13, bf16[128,2048]{1,0:T(8,128)(2,1)} %get-tuple-element.193.rest_0_, bf16[128,2048]{1,0:T(8,128)(2,1)} %get-tuple-element.194.rest_1_, ...), custom_call_target="tpu_custom_call" | custom-call | flops 161061280 | bytes 251658 | tf_op jit(solution)/shard_map/expert_grad_hidden/pallas_call | solution.py:706
  160.0 7.5 %project_out.1 = (f32[2,128,2048]{2,1,0:T(8,128)}, bf16[2,16,128]{2,1,0:T(8,128)(2,1)}, bf16[128,2048]{1,0:T(8,128)(2,1)}, bf16[128,2048]{1,0:T(8,128)(2,1)}) custom-call(bf16[4,2,128,512]{3,2,1,0:T(8,128)(2,1)} %copy-done.4, bf16[2048,2048]{1,0:T(8,128)(2,1)} %w_ref.12, bf16[2,16,2048]{2,1,0:T(8,128)(2,1)} %get-tuple-element.164.down_ref, ...), custom_call_target="tpu_custom_call" | custom-call | flops 21474836 | bytes 83886 | tf_op jit(solution)/shard_map/project_out/pallas_call | solution.py:607
  171.9 10.7 %collective-permute-done.33.rest_4_ = bf16[128,2048]{1,0:T(8,128)(2,1)S(1)} collective-permute-done((bf16[128,2048]{1,0:T(8,128)(2,1)}, bf16[128,2048]{1,0:T(8,128)(2,1)S(1)}, u32[]{:S(2)}, u32[]{:S(2)}) %collective-permute-start.33) | collective-permute-done | bytes 524320 | tf_op jit(solution)/shard_map/ppermute | solution.py:104
  184.8 9.0 %collective-permute-done.34.rest_5_ = bf16[128,2048]{1,0:T(8,128)(2,1)S(1)} collective-permute-done((bf16[128,2048]{1,0:T(8,128)(2,1)}, bf16[128,2048]{1,0:T(8,128)(2,1)S(1)}, u32[]{:S(2)}, u32[]{:S(2)}) %collective-permute-start.34) | collective-permute-done | bytes 524320 | tf_op jit(solution)/shard_map/ppermute | solution.py:104
  195.1 10.1 %collective-permute-done.41.rest_12_ = bf16[128,2048]{1,0:T(8,128)(2,1)S(1)} collective-permute-done((bf16[128,2048]{1,0:T(8,128)(2,1)S(1)}, bf16[128,2048]{1,0:T(8,128)(2,1)S(1)}, u32[]{:S(2)}, u32[]{:S(2)}) %collective-permute-start.41) | collective-permute-done | bytes 524320 | tf_op jit(solution)/shard_map/ppermute | solution.py:104
  208.0 91.5 %expert_middle.1 = (bf16[4,768,1024]{2,1,0:T(8,128)(2,1)}, bf16[128,2048]{1,0:T(8,128)(2,1)}, bf16[128,2048]{1,0:T(8,128)(2,1)}, bf16[128,2048]{1,0:T(8,128)(2,1...) custom-call(s32[2]{0:T(128)} %pad_add_fusion.place_ref, ...), custom_call_target="tpu_custom_call" | custom-call | flops 547608320 | bytes 587202 | tf_op jit(solution)/shard_map/expert_middle/pallas_call | solution.py:836
  300.1 6.9 %collective-permute-done.46 = bf16[1,256,2048]{2,1,0:T(8,128)(2,1)S(1)} collective-permute-done((bf16[1,256,2048]{2,1,0:T(8,128)(2,1)}, bf16[1,256,2048]{2,1,0:T(8,128)(2,1)S(1)}, u32[]{:S(2)}, u32[]{:S(2)}) %collective-permute-start.46) | collective-permute-done | bytes 1048608 | tf_op jit(solution)/shard_map/ppermute | solution.py:104
  316.5 12.3 %expert_produce.2.rest_0_ = bf16[2,768,2048]{2,1,0:T(8,128)(2,1)} custom-call(s32[2]{0:T(128)} %pad_add_fusion.place_ref, f32[8,2,4,256]{3,2,1,0:T(4,128)} %pad_maximum_fusion.9.meta_ref, bf16[4,768,1024]{2,1,0:T(8,128)(2,1)} %get-tuple-element.225.h_ref, bf16[4,1024,2048]{2,1,0:T(8,128)(2,1)} %w_ref.13), custom_call_target="tpu_custom_call" | custom-call | flops 64424508 | bytes 293601 | tf_op jit(solution)/shard_map/expert_produce/pallas_call | solution.py:913
  336.5 10.5 %collective-permute-done.50.rest_3_ = bf16[128,2048]{1,0:T(8,128)(2,1)S(1)} collective-permute-done((bf16[128,2048]{1,0:T(8,128)(2,1)S(1)}, bf16[128,2048]{1,0:T(8,128)(2,1)S(1)}, u32[]{:S(2)}, u32[]{:S(2)}) %collective-permute-start.50) | collective-permute-done | bytes 524320 | tf_op jit(solution)/shard_map/ppermute | solution.py:104
  348.0 9.4 %project_out_back.1 = (f32[2,128,2048]{2,1,0:T(8,128)}, bf16[2,16,2048]{2,1,0:T(8,128)(2,1)}, bf16[2,16,2048]{2,1,0:T(8,128)(2,1)}, bf16[4,2,128,512]{3,2,1,0:T(8,128)(2,1)}) custom-call(bf16[2,128,2048]{2,1,0:T(8,128)(2,1)} %copy-done.5, f32[1,2048]{1,0:T(1,128)} %bitcast.215, bf16[2048,2048]{1,0:T(8,128)(2,1)} %w_ref.12, ...), custom_call_target="tpu_custom_call" | custom-call | flops 21474836 | bytes 83886 | tf_op jit(solution)/shard_map/project_out_back/pallas_call | solution.py:978
  361.1 17.9 %expert_produce.3 = (bf16[128,2048]{1,0:T(8,128)(2,1)}, bf16[128,2048]{1,0:T(8,128)(2,1)}, bf16[128,2048]{1,0:T(8,128)(2,1)}, bf16[128,2048]{1,0:T(8,128)(2,1)},...) custom-call(s32[2]{0:T(128)} %pad_add_fusion.place_ref, ...), custom_call_target="tpu_custom_call" | custom-call | flops 64424508 | bytes 293601 | tf_op jit(solution)/shard_map/expert_produce/pallas_call | solution.py:913
  379.1 7.3 %all-to-all-done.3.rest_0_.rest_1_.rest_2_.rest_3_ = bf16[4,2,128,512]{3,2,1,0:T(8,128)(2,1)S(1)} async-done(((bf16[4,2,128,512]{3,2,1,0:T(8,128)(2,1)}), bf16[4,2,128,512]{3,2,1,0:T(8,128)(2,1)S(1)}, u32[]{:S(2)}, u32[]{:S(2)}) %all-to-all-start.3) | async-done | bytes 1048608 | tf_op jit(solution)/shard_map/all_to_all | solution.py:1313
  387.4 12.6 %attend_back.2 = (bf16[4,3,128,512]{3,2,1,0:T(8,128)(2,1)}, bf16[48,512]{1,0:T(8,128)(2,1)}) custom-call(s32[1]{0:T(128)} %get-tuple-element.323.len_ref, f32[1,128]{1,0:T(1,128)} %bitcast.222, f32[1,128]{1,0:T(1,128)} %bitcast.226, s32[1,512]{1,0:T(1,128)} %bitcast.207, f32[512,128]{1,0:T(8,128)} %get-tuple-element.177.cos_ref, ...), custom_call_target="tpu_custom_call" | custom-call | flops 13421772 | bytes 146800 | tf_op jit(solution)/shard_map/attend_back/pallas_call | solution.py:542
  416.3 12.8 %attend_back.3 = (bf16[4,3,128,512]{3,2,1,0:T(8,128)(2,1)}, bf16[48,512]{1,0:T(8,128)(2,1)}) custom-call(s32[1]{0:T(128)} %get-tuple-element.324.len_ref, f32[1,128]{1,0:T(1,128)} %bitcast.223, f32[1,128]{1,0:T(1,128)} %bitcast.227, s32[1,512]{1,0:T(1,128)} %bitcast.208, f32[512,128]{1,0:T(8,128)} %get-tuple-element.177.cos_ref, ...), custom_call_target="tpu_custom_call" | custom-call | flops 13421772 | bytes 146800 | tf_op jit(solution)/shard_map/attend_back/pallas_call | solution.py:542
  457.7 14.2 %project_first_back.2.rest_0_ = f32[2,128,2048]{2,1,0:T(8,128)} custom-call(bf16[2,48,2048]{2,1,0:T(8,128)(2,1)} %get-tuple-element.268.down_ref, bf16[3,2048,2048]{2,1,0:T(8,128)(2,1)} %w_ref.15, bf16[2,128,2048]{2,1,0:T(8,128)(2,1)} %tok_ref.5, f32[1,2048]{1,0:T(1,128)} %bitcast.210, f32[2,128,2048]{2,1,0:T(8,128)} %get-tuple-element.230.mixed_ref, ...), custom_call_target="tpu_custom_call" | custom-call | flops 32212254 | bytes 251658 | tf_op jit(solution)/shard_map/project_first_back/pallas_call | solution.py:1093
  476.6 6.6 %all-to-all-done.5.rest_0_.rest_1_.rest_2_.rest_3_.grad_ref = bf16[4,3,128,512]{3,2,1,0:T(8,128)(2,1)S(1)} async-done(((bf16[4,3,128,512]{3,2,1,0:T(8,128)(2,1)}), bf16[4,3,128,512]{3,2,1,0:T(8,128)(2,1)S(1)}, u32[]{:S(2)}, u32[]{:S(2)}) %all-to-all-start.5) | async-done | bytes 1572896 | tf_op jit(solution)/shard_map/all_to_all | solution.py:119
  492.9 14.2 %project_first_back.3 = f32[2,128,2048]{2,1,0:T(8,128)} custom-call(bf16[2,48,2048]{2,1,0:T(8,128)(2,1)} %get-tuple-element.268.down_ref, bf16[3,2048,2048]{2,1,0:T(8,128)(2,1)} %w_ref.15, bf16[2,128,2048]{2,1,0:T(8,128)(2,1)} %tok_ref.5, f32[1,2048]{1,0:T(1,128)} %bitcast.211, ...), custom_call_target="tpu_custom_call", output_to_operand_aliasing={{}: (7, {})} | custom-call | flops 32212254 | bytes 251658 | tf_op jit(solution)/shard_map/project_first_back/pallas_call | solution.py:1093
  515.2 7.0 %collective-permute-done.62 = bf16[256,256]{1,0:T(8,128)(2,1)S(1)} collective-permute-done((bf16[256,256]{1,0:T(8,128)(2,1)S(1)}, bf16[256,256]{1,0:T(8,128)(2,1)S(1)}, u32[]{:S(2)}, u32[]{:S(2)}) %collective-permute-start.62) | collective-permute-done | bytes 131104 | tf_op jit(solution)/shard_map/ppermute | solution.py:109
  528.2 7.7 %collective-permute-done.65 = bf16[256,256]{1,0:T(8,128)(2,1)S(1)} collective-permute-done((bf16[256,256]{1,0:T(8,128)(2,1)S(1)}, bf16[256,256]{1,0:T(8,128)(2,1)S(1)}, u32[]{:S(2)}, u32[]{:S(2)}) %collective-permute-start.65) | collective-permute-done | bytes 131104 | tf_op jit(solution)/shard_map/ppermute | solution.py:109
  (336 shorter events, 191.3 us)
Async XLA Ops:
  18.5 27.0 %collective-permute-start = (bf16[624,256]{1,0:T(8,128)(2,1)S(1)}, bf16[624,256]{1,0:T(8,128)(2,1)S(1)}, u32[]{:S(2)}, u32[]{:S(2)}) collective-permute-start(bf16[624,256]{1,0:T(8,128)(2,1)S(1)} %pad_maximum_fusion.4.rest_0_), channel_id=1, source_target_pairs={{0,1},{1,0},{2,3},{3,2},{4,5},{5,4},{6,7},{7,6},{8,9},{9,8},{10,11... | collective-permute-start | bytes 958472 | tf_op jit(solution)/shard_map/ppermute | solution.py:104
  23.1 45.5 %all-to-all-start = ((bf16[4,3,128,512]{3,2,1,0:T(8,128)(2,1)}), bf16[4,3,128,512]{3,2,1,0:T(8,128)(2,1)S(1)}, u32[]{:S(2)}, u32[]{:S(2)}) async-start(bf16[4,3,128,512]{3,2,1,0:T(8,128)(2,1)} %get-tuple-element.148), calls=%async_computation | async-start | bytes 3145728 | tf_op jit(solution)/shard_map/all_to_all | solution.py:119
  68.7 46.8 %all-to-all-start.1 = ((bf16[4,3,128,512]{3,2,1,0:T(8,128)(2,1)}), bf16[4,3,128,512]{3,2,1,0:T(8,128)(2,1)}, u32[]{:S(2)}, u32[]{:S(2)}) async-start(bf16[4,3,128,512]{3,2,1,0:T(8,128)(2,1)} %get-tuple-element.186), calls=%async_computation.1 | async-start | bytes 3145728 | tf_op jit(solution)/shard_map/all_to_all | solution.py:119
  74.5 21.0 %collective-permute-start.19 = (bf16[128,2048]{1,0:T(8,128)(2,1)}, bf16[128,2048]{1,0:T(8,128)(2,1)S(1)}, u32[]{:S(2)}, u32[]{:S(2)}) collective-permute-start(bf16[128,2048]{1,0:T(8,128)(2,1)} %get-tuple-element.193.rest_0_), channel_id=1, source_target_pairs={{0,2},{1,3},{2,0},{3,1},{4,6},{5,7},{6,4},{7,5},{8,10},{9,11},{10,... | collective-permute-start | bytes 1572872 | tf_op jit(solution)/shard_map/ppermute | solution.py:104
  75.0 25.2 %collective-permute-start.20 = (bf16[128,2048]{1,0:T(8,128)(2,1)}, bf16[128,2048]{1,0:T(8,128)(2,1)S(1)}, u32[]{:S(2)}, u32[]{:S(2)}) collective-permute-start(bf16[128,2048]{1,0:T(8,128)(2,1)} %get-tuple-element.194.rest_1_), channel_id=1, source_target_pairs={{0,2},{1,3},{2,0},{3,1},{4,6},{5,7},{6,4},{7,5},{8,10},{9,11},{10,... | collective-permute-start | bytes 1572872 | tf_op jit(solution)/shard_map/ppermute | solution.py:104
  76.5 23.8 %collective-permute-start.23 = (bf16[128,2048]{1,0:T(8,128)(2,1)}, bf16[128,2048]{1,0:T(8,128)(2,1)S(1)}, u32[]{:S(2)}, u32[]{:S(2)}) collective-permute-start(bf16[128,2048]{1,0:T(8,128)(2,1)} %get-tuple-element.193.rest_0_), channel_id=1, source_target_pairs={{0,4},{1,5},{2,6},{3,7},{4,0},{5,1},{6,2},{7,3},{8,12},{9,13},{10,... | collective-permute-start | bytes 1572872 | tf_op jit(solution)/shard_map/ppermute | solution.py:104
  77.1 24.8 %collective-permute-start.24 = (bf16[128,2048]{1,0:T(8,128)(2,1)}, bf16[128,2048]{1,0:T(8,128)(2,1)}, u32[]{:S(2)}, u32[]{:S(2)}) collective-permute-start(bf16[128,2048]{1,0:T(8,128)(2,1)} %get-tuple-element.194.rest_1_), channel_id=1, source_target_pairs={{0,4},{1,5},{2,6},{3,7},{4,0},{5,1},{6,2},{7,3},{8,12},{9,13},{10,... | collective-permute-start | bytes 1572872 | tf_op jit(solution)/shard_map/ppermute | solution.py:104
  79.2 23.7 %collective-permute-start.17 = (bf16[128,2048]{1,0:T(8,128)(2,1)}, bf16[128,2048]{1,0:T(8,128)(2,1)}, u32[]{:S(2)}, u32[]{:S(2)}) collective-permute-start(bf16[128,2048]{1,0:T(8,128)(2,1)} %get-tuple-element.193.rest_0_), channel_id=1, source_target_pairs={{0,1},{1,0},{2,3},{3,2},{4,5},{5,4},{6,7},{7,6},{8,9},{9,8},{10,11... | collective-permute-start | bytes 1572872 | tf_op jit(solution)/shard_map/ppermute | solution.py:104
  102.9 24.8 %collective-permute-start.22 = (bf16[128,2048]{1,0:T(8,128)(2,1)S(1)}, bf16[128,2048]{1,0:T(8,128)(2,1)}, u32[]{:S(2)}, u32[]{:S(2)}) collective-permute-start(bf16[128,2048]{1,0:T(8,128)(2,1)S(1)} %collective-permute-done.20.rest_5_), channel_id=1, source_target_pairs={{0,1},{1,0},{2,3},{3,2},{4,5},{5,4},{6,7},{7,6},{8,9},{9,8},{10,11... | collective-permute-start | bytes 1572872 | tf_op jit(solution)/shard_map/ppermute | solution.py:104
  102.9 24.8 %collective-permute-start.25 = (bf16[128,2048]{1,0:T(8,128)(2,1)S(1)}, bf16[128,2048]{1,0:T(8,128)(2,1)}, u32[]{:S(2)}, u32[]{:S(2)}) collective-permute-start(bf16[128,2048]{1,0:T(8,128)(2,1)S(1)} %collective-permute-done.23.rest_8_), channel_id=1, source_target_pairs={{0,1},{1,0},{2,3},{3,2},{4,5},{5,4},{6,7},{7,6},{8,9},{9,8},{10,11... | collective-permute-start | bytes 1572872 | tf_op jit(solution)/shard_map/ppermute | solution.py:104
  103.4 24.3 %collective-permute-start.26 = (bf16[128,2048]{1,0:T(8,128)(2,1)}, bf16[128,2048]{1,0:T(8,128)(2,1)}, u32[]{:S(2)}, u32[]{:S(2)}) collective-permute-start(bf16[128,2048]{1,0:T(8,128)(2,1)} %collective-permute-done.24.rest_9_), channel_id=1, source_target_pairs={{0,1},{1,0},{2,3},{3,2},{4,5},{5,4},{6,7},{7,6},{8,9},{9,8},{10,11... | collective-permute-start | bytes 1572872 | tf_op jit(solution)/shard_map/ppermute | solution.py:104
  127.7 31.3 %all-to-all-start.2 = ((bf16[4,2,128,512]{3,2,1,0:T(8,128)(2,1)}), bf16[4,2,128,512]{3,2,1,0:T(8,128)(2,1)S(1)}, u32[]{:S(2)}, u32[]{:S(2)}) async-start(bf16[4,2,128,512]{3,2,1,0:T(8,128)(2,1)} %pad_maximum_fusion), calls=%async_computation.2 | async-start | bytes 2097152 | tf_op jit(solution)/shard_map/all_to_all | solution.py:1267
  169.9 24.0 %collective-permute-start.34 = (bf16[128,2048]{1,0:T(8,128)(2,1)}, bf16[128,2048]{1,0:T(8,128)(2,1)S(1)}, u32[]{:S(2)}, u32[]{:S(2)}) collective-permute-start(bf16[128,2048]{1,0:T(8,128)(2,1)} %get-tuple-element.214.rest_1_), channel_id=1, source_target_pairs={{0,2},{1,3},{2,0},{3,1},{4,6},{5,7},{6,4},{7,5},{8,10},{9,11},{10,... | collective-permute-start | bytes 1572872 | tf_op jit(solution)/shard_map/ppermute | solution.py:104
  171.4 23.2 %collective-permute-start.37 = (bf16[128,2048]{1,0:T(8,128)(2,1)}, bf16[128,2048]{1,0:T(8,128)(2,1)S(1)}, u32[]{:S(2)}, u32[]{:S(2)}) collective-permute-start(bf16[128,2048]{1,0:T(8,128)(2,1)} %get-tuple-element.213.rest_0_), channel_id=1, source_target_pairs={{0,4},{1,5},{2,6},{3,7},{4,0},{5,1},{6,2},{7,3},{8,12},{9,13},{10,... | collective-permute-start | bytes 1572872 | tf_op jit(solution)/shard_map/ppermute | solution.py:104
  182.6 22.6 %collective-permute-start.41 = (bf16[128,2048]{1,0:T(8,128)(2,1)S(1)}, bf16[128,2048]{1,0:T(8,128)(2,1)S(1)}, u32[]{:S(2)}, u32[]{:S(2)}) collective-permute-start(bf16[128,2048]{1,0:T(8,128)(2,1)S(1)} %collective-permute-done.33.rest_4_), channel_id=1, source_target_pairs={{0,4},{1,5},{2,6},{3,7},{4,0},{5,1},{6,2},{7,3},{8,12},{9,13},{10,... | collective-permute-start | bytes 1572872 | tf_op jit(solution)/shard_map/ppermute | solution.py:104
  184.2 21.0 %collective-permute-start.42 = (bf16[128,2048]{1,0:T(8,128)(2,1)S(1)}, bf16[128,2048]{1,0:T(8,128)(2,1)S(1)}, u32[]{:S(2)}, u32[]{:S(2)}) collective-permute-start(bf16[128,2048]{1,0:T(8,128)(2,1)S(1)} %collective-permute-done.38.rest_9_), channel_id=1, source_target_pairs={{0,2},{1,3},{2,0},{3,1},{4,6},{5,7},{6,4},{7,5},{8,10},{9,11},{10,... | collective-permute-start | bytes 1572872 | tf_op jit(solution)/shard_map/ppermute | solution.py:104
  315.4 21.1 %collective-permute-start.47 = (bf16[128,2048]{1,0:T(8,128)(2,1)}, bf16[128,2048]{1,0:T(8,128)(2,1)S(1)}, u32[]{:S(2)}, u32[]{:S(2)}) collective-permute-start(bf16[128,2048]{1,0:T(8,128)(2,1)} %get-tuple-element.302), channel_id=1, source_target_pairs={{0,2},{1,3},{2,0},{3,1},{4,6},{5,7},{6,4},{7,5},{8,10},{9,11},{10,... | collective-permute-start | bytes 1572872 | tf_op jit(solution)/shard_map/ppermute | solution.py:104
  316.0 31.1 %collective-permute-start.51 = (bf16[128,2048]{1,0:T(8,128)(2,1)}, bf16[128,2048]{1,0:T(8,128)(2,1)S(1)}, u32[]{:S(2)}, u32[]{:S(2)}) collective-permute-start(bf16[128,2048]{1,0:T(8,128)(2,1)} %get-tuple-element.301), channel_id=1, source_target_pairs={{0,4},{1,5},{2,6},{3,7},{4,0},{5,1},{6,2},{7,3},{8,12},{9,13},{10,... | collective-permute-start | bytes 1572872 | tf_op jit(solution)/shard_map/ppermute | solution.py:104
  357.4 28.9 %all-to-all-start.3 = ((bf16[4,2,128,512]{3,2,1,0:T(8,128)(2,1)}), bf16[4,2,128,512]{3,2,1,0:T(8,128)(2,1)S(1)}, u32[]{:S(2)}, u32[]{:S(2)}) async-start(bf16[4,2,128,512]{3,2,1,0:T(8,128)(2,1)} %get-tuple-element.236), calls=%async_computation.3 | async-start | bytes 2097152 | tf_op jit(solution)/shard_map/all_to_all | solution.py:1313
  400.6 41.0 %all-to-all-start.4 = ((bf16[4,3,128,512]{3,2,1,0:T(8,128)(2,1)}), bf16[4,3,128,512]{3,2,1,0:T(8,128)(2,1)S(1)}, u32[]{:S(2)}, u32[]{:S(2)}) async-start(bf16[4,3,128,512]{3,2,1,0:T(8,128)(2,1)} %get-tuple-element.261), calls=%async_computation.4 | async-start | bytes 3145728 | tf_op jit(solution)/shard_map/all_to_all | solution.py:119
  414.3 21.1 %collective-permute-start.57 = (bf16[128,2048]{1,0:T(8,128)(2,1)}, bf16[128,2048]{1,0:T(8,128)(2,1)}, u32[]{:S(2)}, u32[]{:S(2)}) collective-permute-start(bf16[128,2048]{1,0:T(8,128)(2,1)} %get-tuple-element.296), channel_id=1, source_target_pairs={{0,2},{1,3},{2,0},{3,1},{4,6},{5,7},{6,4},{7,5},{8,10},{9,11},{10,... | collective-permute-start | bytes 1572872 | tf_op jit(solution)/shard_map/ppermute | solution.py:104
  442.9 40.4 %all-to-all-start.5 = ((bf16[4,3,128,512]{3,2,1,0:T(8,128)(2,1)}), bf16[4,3,128,512]{3,2,1,0:T(8,128)(2,1)S(1)}, u32[]{:S(2)}, u32[]{:S(2)}) async-start(bf16[4,3,128,512]{3,2,1,0:T(8,128)(2,1)} %get-tuple-element.277), calls=%async_computation.5 | async-start | bytes 3145728 | tf_op jit(solution)/shard_map/all_to_all | solution.py:119
  449.8 22.1 %collective-permute-start.59 = (bf16[128,2048]{1,0:T(8,128)(2,1)}, bf16[128,2048]{1,0:T(8,128)(2,1)}, u32[]{:S(2)}, u32[]{:S(2)}) collective-permute-start(bf16[128,2048]{1,0:T(8,128)(2,1)} %get-tuple-element.294), channel_id=1, source_target_pairs={{0,4},{1,5},{2,6},{3,7},{4,0},{5,1},{6,2},{7,3},{8,12},{9,13},{10,... | collective-permute-start | bytes 1572872 | tf_op jit(solution)/shard_map/ppermute | solution.py:104
  451.3 20.6 %collective-permute-start.60 = (bf16[128,2048]{1,0:T(8,128)(2,1)}, bf16[128,2048]{1,0:T(8,128)(2,1)}, u32[]{:S(2)}, u32[]{:S(2)}) collective-permute-start(bf16[128,2048]{1,0:T(8,128)(2,1)} %get-tuple-element.293), channel_id=1, source_target_pairs={{0,2},{1,3},{2,0},{3,1},{4,6},{5,7},{6,4},{7,5},{8,10},{9,11},{10,... | collective-permute-start | bytes 1572872 | tf_op jit(solution)/shard_map/ppermute | solution.py:104
  (105 other events, 1262.9 us)

commit v3 on v2

--- a/solution.py
+++ b/solution.py
@@ -794,7 +794,7 @@
     count = meta.shape[0]
     tokens = meta.shape[-1]
     rows = count * capacity
-    chunk = 256 if rows % 256 == 0 else rows
+    chunk = rows // 2 if rows % 32 == 0 else rows
     numbers = [len(found) for found in gathered]
     arrays = [array for found in gathered for array in found]
 

time: 550 us -> 549 us (level)
  no operation moved by 1% of the time
where the time goes in v3:
time: 549 us; the launch traced here: 539 us
  Pallas kernels  268 us (49%)
  waiting for transfers between devices  131 us (24%)
  starting transfers between devices  78.5 us (14%)
  other arithmetic  32.9 us (6%)
  local copies, waits for them, and re-layouts  25.4 us (5%)
    pallas_call x1, Pallas kernels, expert_middle(): kernel_call(body, 'expert_middle', (experts,), [whole_block(meta.shape),...  90.1 us
    ppermute x58, waiting for transfers between devices, swap(): return lax.ppermute(values, 'exp', [(i, i ^ mask) for i in range(count)])  85.8 us
    ppermute x58, starting transfers between devices, swap(): return lax.ppermute(values, 'exp', [(i, i ^ mask) for i in range(count)])  38.1 us
    pallas_call x2, Pallas kernels, expert_produce(): kernel_call(body, 'expert_produce', (last - first,), [whole_block(meta.sh...  30.2 us
    pallas_call x2, Pallas kernels, project_first_back(): kernel_call(body, 'project_first_back', (1,), [group_block(downs.shape, g...  28.4 us
    pallas_call x2, Pallas kernels, attend_back(): kernel_call(body, 'attend_back', (heads // step_heads,), [whole_block((1,...  25.4 us
    pallas_call x1, Pallas kernels, expert_grad_hidden(): kernel_call(body, 'expert_grad_hidden', (experts,), [whole_block(meta.sha...  23.8 us
    ppermute x9, waiting for transfers between devices, shift(): lax.ppermute(values, 'seq', [(i, (i + distance) % count) for i in range(c...  22.1 us
  transfers between devices with their start and end apart: 74, of which 25 were waited for; matrix products, arithmetic and copies ran while one was open for 8% of the time, Pallas kernels for 24%

profile of v3, /device:TPU:0, one launch (start us, length us, event | category | flops | bytes accessed | tf_op | source)
XLA Modules:
  0.0 538.7 jit_solution(18122780445103715128)
XLA Ops:
  1.2 14.1 %project_first.1 = (bf16[4,3,128,512]{3,2,1,0:T(8,128)(2,1)}, bf16[4,3,128,512]{3,2,1,0:T(8,128)(2,1)}, bf16[4,2,128,512]{3,2,1,0:T(8,128)(2,1)}, bf16[256,2048]{1,0:T(8,128)(2,1)}) custom-call(s32[2]{0:T(128)} %pad_add_fusion.place_ref, bf16[256,2048]{1,0:T(8,128)(2,1)} %bitcast.183, f32[1,2048]{1,0:T(1,128)} %bitcast.209, bf16[3,2048,2048]{2,1,0:T(8,128)(2,1)} %w_ref.15), custom_call_target="tpu_custom_call" | custom-call | flops 64424508 | bytes 251658 | tf_op jit(solution)/shard_map/project_first/pallas_call | solution.py:315
  35.4 9.4 %collective-permute-done.5.rest_6_ = bf16[624,256]{1,0:T(8,128)(2,1)S(1)} collective-permute-done((bf16[624,256]{1,0:T(8,128)(2,1)S(1)}, bf16[624,256]{1,0:T(8,128)(2,1)S(1)}, u32[]{:S(2)}, u32[]{:S(2)}) %collective-permute-start.5) | collective-permute-done | bytes 319520 | tf_op jit(solution)/shard_map/ppermute | solution.py:104
  85.6 9.9 %attend.2 = (bf16[4,128,512]{2,1,0:T(8,128)(2,1)}, bf16[4,512,128]{2,1,0:T(8,128)(2,1)}, bf16[4,512,128]{2,1,0:T(8,128)(2,1)}, bf16[4,512,128]{2,1,0:T(8,128)(2,...) custom-call(s32[1]{0:T(128)} %get-tuple-element.323.len_ref, bf16[3,16,512]{2,1,0:T(8,128)(2,1)} %bitcast.200, ...), custom_call_target="tpu_custom_call" | custom-call | flops 5368709 | bytes 104857 | tf_op jit(solution)/shard_map/attend/pallas_call | solution.py:475
  103.5 11.4 %collective-permute-done.27.rest_12_ = bf16[128,2048]{1,0:T(8,128)(2,1)} collective-permute-done((bf16[128,2048]{1,0:T(8,128)(2,1)S(1)}, bf16[128,2048]{1,0:T(8,128)(2,1)}, u32[]{:S(2)}, u32[]{:S(2)}) %collective-permute-start.27) | collective-permute-done | bytes 524320 | tf_op jit(solution)/shard_map/ppermute | solution.py:104
  115.4 10.0 %attend.3 = (bf16[4,128,512]{2,1,0:T(8,128)(2,1)}, bf16[4,512,128]{2,1,0:T(8,128)(2,1)}, bf16[4,512,128]{2,1,0:T(8,128)(2,1)}, bf16[4,512,128]{2,1,0:T(8,128)(2,...) custom-call(s32[1]{0:T(128)} %get-tuple-element.324.len_ref, bf16[3,16,512]{2,1,0:T(8,128)(2,1)} %bitcast.199, ...), custom_call_target="tpu_custom_call" | custom-call | flops 5368709 | bytes 104857 | tf_op jit(solution)/shard_map/attend/pallas_call | solution.py:475
  132.7 23.8 %expert_grad_hidden.1.gh_ref = bf16[4,768,1024]{2,1,0:T(8,128)(2,1)} custom-call(f32[8,2,4,256]{3,2,1,0:T(4,128)} %pad_maximum_fusion.9.meta_ref, bf16[4,1024,2048]{2,1,0:T(8,128)(2,1)} %w_ref.13, bf16[128,2048]{1,0:T(8,128)(2,1)} %get-tuple-element.193.rest_0_, bf16[128,2048]{1,0:T(8,128)(2,1)} %get-tuple-element.194.rest_1_, ...), custom_call_target="tpu_custom_call" | custom-call | flops 161061280 | bytes 251658 | tf_op jit(solution)/shard_map/expert_grad_hidden/pallas_call | solution.py:706
  160.0 7.5 %project_out.1 = (f32[2,128,2048]{2,1,0:T(8,128)}, bf16[2,16,128]{2,1,0:T(8,128)(2,1)}, bf16[128,2048]{1,0:T(8,128)(2,1)}, bf16[128,2048]{1,0:T(8,128)(2,1)}) custom-call(bf16[4,2,128,512]{3,2,1,0:T(8,128)(2,1)} %copy-done.4, bf16[2048,2048]{1,0:T(8,128)(2,1)} %w_ref.12, bf16[2,16,2048]{2,1,0:T(8,128)(2,1)} %get-tuple-element.164.down_ref, ...), custom_call_target="tpu_custom_call" | custom-call | flops 21474836 | bytes 83886 | tf_op jit(solution)/shard_map/project_out/pallas_call | solution.py:607
  171.9 10.7 %collective-permute-done.33.rest_4_ = bf16[128,2048]{1,0:T(8,128)(2,1)S(1)} collective-permute-done((bf16[128,2048]{1,0:T(8,128)(2,1)}, bf16[128,2048]{1,0:T(8,128)(2,1)S(1)}, u32[]{:S(2)}, u32[]{:S(2)}) %collective-permute-start.33) | collective-permute-done | bytes 524320 | tf_op jit(solution)/shard_map/ppermute | solution.py:104
  184.8 9.0 %collective-permute-done.34.rest_5_ = bf16[128,2048]{1,0:T(8,128)(2,1)S(1)} collective-permute-done((bf16[128,2048]{1,0:T(8,128)(2,1)}, bf16[128,2048]{1,0:T(8,128)(2,1)S(1)}, u32[]{:S(2)}, u32[]{:S(2)}) %collective-permute-start.34) | collective-permute-done | bytes 524320 | tf_op jit(solution)/shard_map/ppermute | solution.py:104
  195.1 10.1 %collective-permute-done.41.rest_12_ = bf16[128,2048]{1,0:T(8,128)(2,1)S(1)} collective-permute-done((bf16[128,2048]{1,0:T(8,128)(2,1)S(1)}, bf16[128,2048]{1,0:T(8,128)(2,1)S(1)}, u32[]{:S(2)}, u32[]{:S(2)}) %collective-permute-start.41) | collective-permute-done | bytes 524320 | tf_op jit(solution)/shard_map/ppermute | solution.py:104
  208.0 90.1 %expert_middle.1 = (bf16[4,768,1024]{2,1,0:T(8,128)(2,1)}, bf16[128,2048]{1,0:T(8,128)(2,1)}, bf16[128,2048]{1,0:T(8,128)(2,1)}, bf16[128,2048]{1,0:T(8,128)(2,1...) custom-call(s32[2]{0:T(128)} %pad_add_fusion.place_ref, ...), custom_call_target="tpu_custom_call" | custom-call | flops 547608320 | bytes 587202 | tf_op jit(solution)/shard_map/expert_middle/pallas_call | solution.py:836
  298.7 6.9 %collective-permute-done.46 = bf16[1,256,2048]{2,1,0:T(8,128)(2,1)S(1)} collective-permute-done((bf16[1,256,2048]{2,1,0:T(8,128)(2,1)}, bf16[1,256,2048]{2,1,0:T(8,128)(2,1)S(1)}, u32[]{:S(2)}, u32[]{:S(2)}) %collective-permute-start.46) | collective-permute-done | bytes 1048608 | tf_op jit(solution)/shard_map/ppermute | solution.py:104
  315.1 12.3 %expert_produce.2.rest_0_ = bf16[2,768,2048]{2,1,0:T(8,128)(2,1)} custom-call(s32[2]{0:T(128)} %pad_add_fusion.place_ref, f32[8,2,4,256]{3,2,1,0:T(4,128)} %pad_maximum_fusion.9.meta_ref, bf16[4,768,1024]{2,1,0:T(8,128)(2,1)} %get-tuple-element.225.h_ref, bf16[4,1024,2048]{2,1,0:T(8,128)(2,1)} %w_ref.13), custom_call_target="tpu_custom_call" | custom-call | flops 64424508 | bytes 293601 | tf_op jit(solution)/shard_map/expert_produce/pallas_call | solution.py:913
  335.1 10.5 %collective-permute-done.50.rest_3_ = bf16[128,2048]{1,0:T(8,128)(2,1)S(1)} collective-permute-done((bf16[128,2048]{1,0:T(8,128)(2,1)S(1)}, bf16[128,2048]{1,0:T(8,128)(2,1)S(1)}, u32[]{:S(2)}, u32[]{:S(2)}) %collective-permute-start.50) | collective-permute-done | bytes 524320 | tf_op jit(solution)/shard_map/ppermute | solution.py:104
  346.6 9.4 %project_out_back.1 = (f32[2,128,2048]{2,1,0:T(8,128)}, bf16[2,16,2048]{2,1,0:T(8,128)(2,1)}, bf16[2,16,2048]{2,1,0:T(8,128)(2,1)}, bf16[4,2,128,512]{3,2,1,0:T(8,128)(2,1)}) custom-call(bf16[2,128,2048]{2,1,0:T(8,128)(2,1)} %copy-done.5, f32[1,2048]{1,0:T(1,128)} %bitcast.215, bf16[2048,2048]{1,0:T(8,128)(2,1)} %w_ref.12, ...), custom_call_target="tpu_custom_call" | custom-call | flops 21474836 | bytes 83886 | tf_op jit(solution)/shard_map/project_out_back/pallas_call | solution.py:978
  359.7 17.9 %expert_produce.3 = (bf16[128,2048]{1,0:T(8,128)(2,1)}, bf16[128,2048]{1,0:T(8,128)(2,1)}, bf16[128,2048]{1,0:T(8,128)(2,1)}, bf16[128,2048]{1,0:T(8,128)(2,1)},...) custom-call(s32[2]{0:T(128)} %pad_add_fusion.place_ref, ...), custom_call_target="tpu_custom_call" | custom-call | flops 64424508 | bytes 293601 | tf_op jit(solution)/shard_map/expert_produce/pallas_call | solution.py:913
  377.6 7.3 %all-to-all-done.3.rest_0_.rest_1_.rest_2_.rest_3_ = bf16[4,2,128,512]{3,2,1,0:T(8,128)(2,1)S(1)} async-done(((bf16[4,2,128,512]{3,2,1,0:T(8,128)(2,1)}), bf16[4,2,128,512]{3,2,1,0:T(8,128)(2,1)S(1)}, u32[]{:S(2)}, u32[]{:S(2)}) %all-to-all-start.3) | async-done | bytes 1048608 | tf_op jit(solution)/shard_map/all_to_all | solution.py:1313
  386.0 12.6 %attend_back.2 = (bf16[4,3,128,512]{3,2,1,0:T(8,128)(2,1)}, bf16[48,512]{1,0:T(8,128)(2,1)}) custom-call(s32[1]{0:T(128)} %get-tuple-element.323.len_ref, f32[1,128]{1,0:T(1,128)} %bitcast.222, f32[1,128]{1,0:T(1,128)} %bitcast.226, s32[1,512]{1,0:T(1,128)} %bitcast.207, f32[512,128]{1,0:T(8,128)} %get-tuple-element.177.cos_ref, ...), custom_call_target="tpu_custom_call" | custom-call | flops 13421772 | bytes 146800 | tf_op jit(solution)/shard_map/attend_back/pallas_call | solution.py:542
  414.9 12.8 %attend_back.3 = (bf16[4,3,128,512]{3,2,1,0:T(8,128)(2,1)}, bf16[48,512]{1,0:T(8,128)(2,1)}) custom-call(s32[1]{0:T(128)} %get-tuple-element.324.len_ref, f32[1,128]{1,0:T(1,128)} %bitcast.223, f32[1,128]{1,0:T(1,128)} %bitcast.227, s32[1,512]{1,0:T(1,128)} %bitcast.208, f32[512,128]{1,0:T(8,128)} %get-tuple-element.177.cos_ref, ...), custom_call_target="tpu_custom_call" | custom-call | flops 13421772 | bytes 146800 | tf_op jit(solution)/shard_map/attend_back/pallas_call | solution.py:542
  456.3 14.2 %project_first_back.2.rest_0_ = f32[2,128,2048]{2,1,0:T(8,128)} custom-call(bf16[2,48,2048]{2,1,0:T(8,128)(2,1)} %get-tuple-element.268.down_ref, bf16[3,2048,2048]{2,1,0:T(8,128)(2,1)} %w_ref.15, bf16[2,128,2048]{2,1,0:T(8,128)(2,1)} %tok_ref.5, f32[1,2048]{1,0:T(1,128)} %bitcast.210, f32[2,128,2048]{2,1,0:T(8,128)} %get-tuple-element.230.mixed_ref, ...), custom_call_target="tpu_custom_call" | custom-call | flops 32212254 | bytes 251658 | tf_op jit(solution)/shard_map/project_first_back/pallas_call | solution.py:1093
  475.2 6.6 %all-to-all-done.5.rest_0_.rest_1_.rest_2_.rest_3_.grad_ref = bf16[4,3,128,512]{3,2,1,0:T(8,128)(2,1)S(1)} async-done(((bf16[4,3,128,512]{3,2,1,0:T(8,128)(2,1)}), bf16[4,3,128,512]{3,2,1,0:T(8,128)(2,1)S(1)}, u32[]{:S(2)}, u32[]{:S(2)}) %all-to-all-start.5) | async-done | bytes 1572896 | tf_op jit(solution)/shard_map/all_to_all | solution.py:119
  491.5 14.2 %project_first_back.3 = f32[2,128,2048]{2,1,0:T(8,128)} custom-call(bf16[2,48,2048]{2,1,0:T(8,128)(2,1)} %get-tuple-element.268.down_ref, bf16[3,2048,2048]{2,1,0:T(8,128)(2,1)} %w_ref.15, bf16[2,128,2048]{2,1,0:T(8,128)(2,1)} %tok_ref.5, f32[1,2048]{1,0:T(1,128)} %bitcast.211, ...), custom_call_target="tpu_custom_call", output_to_operand_aliasing={{}: (7, {})} | custom-call | flops 32212254 | bytes 251658 | tf_op jit(solution)/shard_map/project_first_back/pallas_call | solution.py:1093
  513.8 7.0 %collective-permute-done.62 = bf16[256,256]{1,0:T(8,128)(2,1)S(1)} collective-permute-done((bf16[256,256]{1,0:T(8,128)(2,1)S(1)}, bf16[256,256]{1,0:T(8,128)(2,1)S(1)}, u32[]{:S(2)}, u32[]{:S(2)}) %collective-permute-start.62) | collective-permute-done | bytes 131104 | tf_op jit(solution)/shard_map/ppermute | solution.py:109
  526.7 7.7 %collective-permute-done.65 = bf16[256,256]{1,0:T(8,128)(2,1)S(1)} collective-permute-done((bf16[256,256]{1,0:T(8,128)(2,1)S(1)}, bf16[256,256]{1,0:T(8,128)(2,1)S(1)}, u32[]{:S(2)}, u32[]{:S(2)}) %collective-permute-start.65) | collective-permute-done | bytes 131104 | tf_op jit(solution)/shard_map/ppermute | solution.py:109
  (336 shorter events, 191.3 us)
Async XLA Ops:
  18.5 27.0 %collective-permute-start = (bf16[624,256]{1,0:T(8,128)(2,1)S(1)}, bf16[624,256]{1,0:T(8,128)(2,1)S(1)}, u32[]{:S(2)}, u32[]{:S(2)}) collective-permute-start(bf16[624,256]{1,0:T(8,128)(2,1)S(1)} %pad_maximum_fusion.4.rest_0_), channel_id=1, source_target_pairs={{0,1},{1,0},{2,3},{3,2},{4,5},{5,4},{6,7},{7,6},{8,9},{9,8},{10,11... | collective-permute-start | bytes 958472 | tf_op jit(solution)/shard_map/ppermute | solution.py:104
  23.1 45.5 %all-to-all-start = ((bf16[4,3,128,512]{3,2,1,0:T(8,128)(2,1)}), bf16[4,3,128,512]{3,2,1,0:T(8,128)(2,1)S(1)}, u32[]{:S(2)}, u32[]{:S(2)}) async-start(bf16[4,3,128,512]{3,2,1,0:T(8,128)(2,1)} %get-tuple-element.148), calls=%async_computation | async-start | bytes 3145728 | tf_op jit(solution)/shard_map/all_to_all | solution.py:119
  68.7 46.8 %all-to-all-start.1 = ((bf16[4,3,128,512]{3,2,1,0:T(8,128)(2,1)}), bf16[4,3,128,512]{3,2,1,0:T(8,128)(2,1)}, u32[]{:S(2)}, u32[]{:S(2)}) async-start(bf16[4,3,128,512]{3,2,1,0:T(8,128)(2,1)} %get-tuple-element.186), calls=%async_computation.1 | async-start | bytes 3145728 | tf_op jit(solution)/shard_map/all_to_all | solution.py:119
  74.5 21.0 %collective-permute-start.19 = (bf16[128,2048]{1,0:T(8,128)(2,1)}, bf16[128,2048]{1,0:T(8,128)(2,1)S(1)}, u32[]{:S(2)}, u32[]{:S(2)}) collective-permute-start(bf16[128,2048]{1,0:T(8,128)(2,1)} %get-tuple-element.193.rest_0_), channel_id=1, source_target_pairs={{0,2},{1,3},{2,0},{3,1},{4,6},{5,7},{6,4},{7,5},{8,10},{9,11},{10,... | collective-permute-start | bytes 1572872 | tf_op jit(solution)/shard_map/ppermute | solution.py:104
  75.0 25.2 %collective-permute-start.20 = (bf16[128,2048]{1,0:T(8,128)(2,1)}, bf16[128,2048]{1,0:T(8,128)(2,1)S(1)}, u32[]{:S(2)}, u32[]{:S(2)}) collective-permute-start(bf16[128,2048]{1,0:T(8,128)(2,1)} %get-tuple-element.194.rest_1_), channel_id=1, source_target_pairs={{0,2},{1,3},{2,0},{3,1},{4,6},{5,7},{6,4},{7,5},{8,10},{9,11},{10,... | collective-permute-start | bytes 1572872 | tf_op jit(solution)/shard_map/ppermute | solution.py:104
  76.5 23.8 %collective-permute-start.23 = (bf16[128,2048]{1,0:T(8,128)(2,1)}, bf16[128,2048]{1,0:T(8,128)(2,1)S(1)}, u32[]{:S(2)}, u32[]{:S(2)}) collective-permute-start(bf16[128,2048]{1,0:T(8,128)(2,1)} %get-tuple-element.193.rest_0_), channel_id=1, source_target_pairs={{0,4},{1,5},{2,6},{3,7},{4,0},{5,1},{6,2},{7,3},{8,12},{9,13},{10,... | collective-permute-start | bytes 1572872 | tf_op jit(solution)/shard_map/ppermute | solution.py:104
  77.1 24.8 %collective-permute-start.24 = (bf16[128,2048]{1,0:T(8,128)(2,1)}, bf16[128,2048]{1,0:T(8,128)(2,1)}, u32[]{:S(2)}, u32[]{:S(2)}) collective-permute-start(bf16[128,2048]{1,0:T(8,128)(2,1)} %get-tuple-element.194.rest_1_), channel_id=1, source_target_pairs={{0,4},{1,5},{2,6},{3,7},{4,0},{5,1},{6,2},{7,3},{8,12},{9,13},{10,... | collective-permute-start | bytes 1572872 | tf_op jit(solution)/shard_map/ppermute | solution.py:104
  79.2 23.7 %collective-permute-start.17 = (bf16[128,2048]{1,0:T(8,128)(2,1)}, bf16[128,2048]{1,0:T(8,128)(2,1)}, u32[]{:S(2)}, u32[]{:S(2)}) collective-permute-start(bf16[128,2048]{1,0:T(8,128)(2,1)} %get-tuple-element.193.rest_0_), channel_id=1, source_target_pairs={{0,1},{1,0},{2,3},{3,2},{4,5},{5,4},{6,7},{7,6},{8,9},{9,8},{10,11... | collective-permute-start | bytes 1572872 | tf_op jit(solution)/shard_map/ppermute | solution.py:104
  102.9 24.8 %collective-permute-start.22 = (bf16[128,2048]{1,0:T(8,128)(2,1)S(1)}, bf16[128,2048]{1,0:T(8,128)(2,1)}, u32[]{:S(2)}, u32[]{:S(2)}) collective-permute-start(bf16[128,2048]{1,0:T(8,128)(2,1)S(1)} %collective-permute-done.20.rest_5_), channel_id=1, source_target_pairs={{0,1},{1,0},{2,3},{3,2},{4,5},{5,4},{6,7},{7,6},{8,9},{9,8},{10,11... | collective-permute-start | bytes 1572872 | tf_op jit(solution)/shard_map/ppermute | solution.py:104
  102.9 24.8 %collective-permute-start.25 = (bf16[128,2048]{1,0:T(8,128)(2,1)S(1)}, bf16[128,2048]{1,0:T(8,128)(2,1)}, u32[]{:S(2)}, u32[]{:S(2)}) collective-permute-start(bf16[128,2048]{1,0:T(8,128)(2,1)S(1)} %collective-permute-done.23.rest_8_), channel_id=1, source_target_pairs={{0,1},{1,0},{2,3},{3,2},{4,5},{5,4},{6,7},{7,6},{8,9},{9,8},{10,11... | collective-permute-start | bytes 1572872 | tf_op jit(solution)/shard_map/ppermute | solution.py:104
  103.4 24.3 %collective-permute-start.26 = (bf16[128,2048]{1,0:T(8,128)(2,1)}, bf16[128,2048]{1,0:T(8,128)(2,1)}, u32[]{:S(2)}, u32[]{:S(2)}) collective-permute-start(bf16[128,2048]{1,0:T(8,128)(2,1)} %collective-permute-done.24.rest_9_), channel_id=1, source_target_pairs={{0,1},{1,0},{2,3},{3,2},{4,5},{5,4},{6,7},{7,6},{8,9},{9,8},{10,11... | collective-permute-start | bytes 1572872 | tf_op jit(solution)/shard_map/ppermute | solution.py:104
  127.7 31.3 %all-to-all-start.2 = ((bf16[4,2,128,512]{3,2,1,0:T(8,128)(2,1)}), bf16[4,2,128,512]{3,2,1,0:T(8,128)(2,1)S(1)}, u32[]{:S(2)}, u32[]{:S(2)}) async-start(bf16[4,2,128,512]{3,2,1,0:T(8,128)(2,1)} %pad_maximum_fusion), calls=%async_computation.2 | async-start | bytes 2097152 | tf_op jit(solution)/shard_map/all_to_all | solution.py:1267
  169.9 24.0 %collective-permute-start.34 = (bf16[128,2048]{1,0:T(8,128)(2,1)}, bf16[128,2048]{1,0:T(8,128)(2,1)S(1)}, u32[]{:S(2)}, u32[]{:S(2)}) collective-permute-start(bf16[128,2048]{1,0:T(8,128)(2,1)} %get-tuple-element.214.rest_1_), channel_id=1, source_target_pairs={{0,2},{1,3},{2,0},{3,1},{4,6},{5,7},{6,4},{7,5},{8,10},{9,11},{10,... | collective-permute-start | bytes 1572872 | tf_op jit(solution)/shard_map/ppermute | solution.py:104
  171.4 23.2 %collective-permute-start.37 = (bf16[128,2048]{1,0:T(8,128)(2,1)}, bf16[128,2048]{1,0:T(8,128)(2,1)S(1)}, u32[]{:S(2)}, u32[]{:S(2)}) collective-permute-start(bf16[128,2048]{1,0:T(8,128)(2,1)} %get-tuple-element.213.rest_0_), channel_id=1, source_target_pairs={{0,4},{1,5},{2,6},{3,7},{4,0},{5,1},{6,2},{7,3},{8,12},{9,13},{10,... | collective-permute-start | bytes 1572872 | tf_op jit(solution)/shard_map/ppermute | solution.py:104
  182.6 22.6 %collective-permute-start.41 = (bf16[128,2048]{1,0:T(8,128)(2,1)S(1)}, bf16[128,2048]{1,0:T(8,128)(2,1)S(1)}, u32[]{:S(2)}, u32[]{:S(2)}) collective-permute-start(bf16[128,2048]{1,0:T(8,128)(2,1)S(1)} %collective-permute-done.33.rest_4_), channel_id=1, source_target_pairs={{0,4},{1,5},{2,6},{3,7},{4,0},{5,1},{6,2},{7,3},{8,12},{9,13},{10,... | collective-permute-start | bytes 1572872 | tf_op jit(solution)/shard_map/ppermute | solution.py:104
  184.2 21.0 %collective-permute-start.42 = (bf16[128,2048]{1,0:T(8,128)(2,1)S(1)}, bf16[128,2048]{1,0:T(8,128)(2,1)S(1)}, u32[]{:S(2)}, u32[]{:S(2)}) collective-permute-start(bf16[128,2048]{1,0:T(8,128)(2,1)S(1)} %collective-permute-done.38.rest_9_), channel_id=1, source_target_pairs={{0,2},{1,3},{2,0},{3,1},{4,6},{5,7},{6,4},{7,5},{8,10},{9,11},{10,... | collective-permute-start | bytes 1572872 | tf_op jit(solution)/shard_map/ppermute | solution.py:104
  314.0 21.1 %collective-permute-start.47 = (bf16[128,2048]{1,0:T(8,128)(2,1)}, bf16[128,2048]{1,0:T(8,128)(2,1)S(1)}, u32[]{:S(2)}, u32[]{:S(2)}) collective-permute-start(bf16[128,2048]{1,0:T(8,128)(2,1)} %get-tuple-element.302), channel_id=1, source_target_pairs={{0,2},{1,3},{2,0},{3,1},{4,6},{5,7},{6,4},{7,5},{8,10},{9,11},{10,... | collective-permute-start | bytes 1572872 | tf_op jit(solution)/shard_map/ppermute | solution.py:104
  314.6 31.1 %collective-permute-start.51 = (bf16[128,2048]{1,0:T(8,128)(2,1)}, bf16[128,2048]{1,0:T(8,128)(2,1)S(1)}, u32[]{:S(2)}, u32[]{:S(2)}) collective-permute-start(bf16[128,2048]{1,0:T(8,128)(2,1)} %get-tuple-element.301), channel_id=1, source_target_pairs={{0,4},{1,5},{2,6},{3,7},{4,0},{5,1},{6,2},{7,3},{8,12},{9,13},{10,... | collective-permute-start | bytes 1572872 | tf_op jit(solution)/shard_map/ppermute | solution.py:104
  356.0 28.9 %all-to-all-start.3 = ((bf16[4,2,128,512]{3,2,1,0:T(8,128)(2,1)}), bf16[4,2,128,512]{3,2,1,0:T(8,128)(2,1)S(1)}, u32[]{:S(2)}, u32[]{:S(2)}) async-start(bf16[4,2,128,512]{3,2,1,0:T(8,128)(2,1)} %get-tuple-element.236), calls=%async_computation.3 | async-start | bytes 2097152 | tf_op jit(solution)/shard_map/all_to_all | solution.py:1313
  399.2 41.0 %all-to-all-start.4 = ((bf16[4,3,128,512]{3,2,1,0:T(8,128)(2,1)}), bf16[4,3,128,512]{3,2,1,0:T(8,128)(2,1)S(1)}, u32[]{:S(2)}, u32[]{:S(2)}) async-start(bf16[4,3,128,512]{3,2,1,0:T(8,128)(2,1)} %get-tuple-element.261), calls=%async_computation.4 | async-start | bytes 3145728 | tf_op jit(solution)/shard_map/all_to_all | solution.py:119
  412.9 21.1 %collective-permute-start.57 = (bf16[128,2048]{1,0:T(8,128)(2,1)}, bf16[128,2048]{1,0:T(8,128)(2,1)}, u32[]{:S(2)}, u32[]{:S(2)}) collective-permute-start(bf16[128,2048]{1,0:T(8,128)(2,1)} %get-tuple-element.296), channel_id=1, source_target_pairs={{0,2},{1,3},{2,0},{3,1},{4,6},{5,7},{6,4},{7,5},{8,10},{9,11},{10,... | collective-permute-start | bytes 1572872 | tf_op jit(solution)/shard_map/ppermute | solution.py:104
  441.4 40.4 %all-to-all-start.5 = ((bf16[4,3,128,512]{3,2,1,0:T(8,128)(2,1)}), bf16[4,3,128,512]{3,2,1,0:T(8,128)(2,1)S(1)}, u32[]{:S(2)}, u32[]{:S(2)}) async-start(bf16[4,3,128,512]{3,2,1,0:T(8,128)(2,1)} %get-tuple-element.277), calls=%async_computation.5 | async-start | bytes 3145728 | tf_op jit(solution)/shard_map/all_to_all | solution.py:119
  448.4 22.1 %collective-permute-start.59 = (bf16[128,2048]{1,0:T(8,128)(2,1)}, bf16[128,2048]{1,0:T(8,128)(2,1)}, u32[]{:S(2)}, u32[]{:S(2)}) collective-permute-start(bf16[128,2048]{1,0:T(8,128)(2,1)} %get-tuple-element.294), channel_id=1, source_target_pairs={{0,4},{1,5},{2,6},{3,7},{4,0},{5,1},{6,2},{7,3},{8,12},{9,13},{10,... | collective-permute-start | bytes 1572872 | tf_op jit(solution)/shard_map/ppermute | solution.py:104
  449.9 20.6 %collective-permute-start.60 = (bf16[128,2048]{1,0:T(8,128)(2,1)}, bf16[128,2048]{1,0:T(8,128)(2,1)}, u32[]{:S(2)}, u32[]{:S(2)}) collective-permute-start(bf16[128,2048]{1,0:T(8,128)(2,1)} %get-tuple-element.293), channel_id=1, source_target_pairs={{0,2},{1,3},{2,0},{3,1},{4,6},{5,7},{6,4},{7,5},{8,10},{9,11},{10,... | collective-permute-start | bytes 1572872 | tf_op jit(solution)/shard_map/ppermute | solution.py:104
  (105 other events, 1262.9 us)
